TPU v7x, 128 devices: a whole 4x4x4 slice. The times are simulated.
128 devices in a mesh: gx: 2 (over core), gy: 16 (over y, x), gz: 4 (over z).
Axes of the slice: x: 4, y: 4, z: 4, core: 2. Of those that a mesh axis runs over, the one named last changes fastest.
Arguments:
- species_field: float32 [48, 2048, 2048], P('gz', 'gx', 'gy')
- x_mode_basis: float32 [2048, 256], P('gx'), may hold values from -0.125 to 0.125
- y_mode_basis: float32 [2048, 256], P('gy'), may hold values from -0.125 to 0.125
Outputs:
- gram_x: float32 [2048, 2048], P(('gx', 'gy'))
- gram_y: float32 [2048, 2048], P('gy', 'gx')
- reduced_core_tensor: float32 [256, 48, 256], P('gx', 'gz', 'gy')
All inputs are finite; a program needn't handle non-finite values.
Results may differ from a plain program's by a relative error of at most 0.000092.
Values sent between devices are 32-bit elements; how exact they have to be, the bound alone decides.
No kernel may reach another device: no remote copies, remote signals or barrier semaphores. Data moves between devices by JAX's collectives and lax.ppermute only.
A program may use at most 128 MiB of HBM per device.

v0:
```python
import jax
import jax.numpy as jnp
from jax import lax
from jax.sharding import PartitionSpec as P


def per_device(species_field, x_mode_basis, y_mode_basis):
    exact_precision = lax.Precision.HIGHEST
    total_y = species_field.shape[2] * lax.axis_size("gy")
    total_slices = species_field.shape[0] * lax.axis_size("gz")
    fibers = lax.all_to_all(species_field, "gx", split_axis=0, concat_axis=1, tiled=True)
    partial_value = jnp.einsum("sxy,szy->xz", fibers, fibers, precision=exact_precision)
    rows_x = lax.psum_scatter(partial_value, ("gx", "gy"), scatter_dimension=0, tiled=True)
    rows_x = rows_x / (total_y * total_slices)
    gram_x = lax.psum(rows_x, "gz")
    reduced_result = lax.psum_scatter(
        jnp.einsum("xr,sxy->rsy", x_mode_basis, species_field, precision=exact_precision),
        "gx",
        scatter_dimension=0,
        tiled=True,
    )
    columns = jnp.einsum(
        "rsy,rsz->yz",
        reduced_result,
        lax.all_gather(reduced_result, "gy", axis=2, tiled=True),
        precision=exact_precision,
    )
    rank_total = x_mode_basis.shape[1]
    part_y = lax.psum_scatter(columns, "gx", scatter_dimension=1, tiled=True) / (
        rank_total * total_slices
    )
    core_term_list = jnp.einsum(
        "mtl,lw->mtw", reduced_result, y_mode_basis, precision=exact_precision
    )
    reduced_core_tensor = lax.psum_scatter(core_term_list, "gy", scatter_dimension=2, tiled=True)
    gram_y = lax.psum(part_y, "gz")
    return (gram_x, gram_y, reduced_core_tensor)


def solution(mesh):
    in_specs = (P("gz", "gx", "gy"), P("gx", None), P("gy", None))
    out_specs = (P(("gx", "gy"), None), P("gy", "gx"), P("gx", "gz", "gy"))
    return jax.shard_map(
        per_device, mesh=mesh, in_specs=in_specs, out_specs=out_specs, check_vma=False
    )
```

profile of v0, /device:TPU:0, one launch (start us, length us, event | category | flops | bytes accessed | tf_op | source)
XLA Modules:
  0.0 305.5 jit_solution(4467132945716309359)
XLA Ops:
  8.0 0.0 copy-start
  8.0 0.0 reduce-scatter.7.cloned.1.call-start
  8.1 1.2 copy-done
  9.2 8.7 %fusion = f32[256,12,128]{2,0,1:T(8,128)} fusion(f32[12,1024,128]{2,1,0:T(8,128)} %param.3, f32[1024,256]{1,0:T(8,128)S(1)} %copy-done), kind=kOutput, calls=%fused_computation.2 | convolution fusion | flops 4831838208 | bytes 8912896 | tf_op jit(solution)/shard_map/xr,sxy->rsy/dot_general | solution.py:17
  17.9 0.0 reduce-scatter.7.cloned.1.call-update
  17.9 0.0 all-gather.2.cloned.1.call-start
  18.0 14.2 %reduce-scatter.7.cloned.1.call-done = f32[128,12,128]{2,0,1:T(8,128)} async-done(((f32[256,12,128]{2,0,1:T(8,128)}), f32[128,12,128]{2,0,1:T(8,128)}) %reduce-scatter.7.cloned.1.call-update) | async-done | bytes 786448 | tf_op jit(solution)/shard_map/reduce_scatter | solution.py:16
  32.1 0.0 all-gather.2.cloned.1.call-update
  32.2 0.0 reduce-scatter.5.cloned.1.call-start
  32.2 10.3 %all_to_all.18 = f32[12,1024,128]{2,1,0:T(8,128)S(1)} all-to-all(f32[12,1024,128]{2,1,0:T(8,128)} %param.3), channel_id=1, replica_groups=mesh['gx'=2,'gy'=16,'gz'=4] {'gx'}, dimensions={0} | all-to-all | bytes 12582912 | tf_op jit(solution)/shard_map/all_to_all | solution.py:11
  42.6 0.4 copy.6
  43.0 42.8 %convolution_bitcast_fusion = f32[2048,2048]{1,0:T(8,128)} fusion(f32[6,2048,128]{2,1,0:T(8,128)S(1)} %bitcast.21), kind=kOutput, calls=%fused_computation | convolution fusion | flops 38654705664 | bytes 23068672 | tf_op jit(solution)/shard_map/sxy,szy->xz/dot_general | solution.py:12
  85.8 0.0 reduce-scatter.5.cloned.1.call-update
  85.9 0.0 copy-start.2
  85.9 0.3 reduce-scatter.9.cloned.1.call-start
  86.1 49.4 %all-gather.2.cloned.1.call-done = f32[128,12,2048]{2,0,1:T(8,128)} async-done(((f32[128,12,128]{2,0,1:T(8,128)}), f32[128,12,2048]{2,0,1:T(8,128)}) %all-gather.2.cloned.1.call-update) | async-done | bytes 12582928 | tf_op jit(solution)/shard_map/all_gather | solution.py:25
  135.5 0.0 copy-done.1
  135.6 10.7 %convolution_bitcast_fusion.1 = f32[128,2048]{1,0:T(8,128)} fusion(f32[128,12,128]{2,0,1:T(8,128)S(1)} %copy-done.1, f32[128,12,2048]{2,0,1:T(8,128)} %all-gather.2.cloned.1.call-done), kind=kOutput, calls=%fused_computation.1 | convolution fusion | flops 4831838208 | bytes 14417920 | tf_op jit(solution)/shard_map/rsy,rsz->yz/dot_general | solution.py:22
  146.2 0.0 reduce-scatter.9.cloned.1.call-update
  146.2 0.0 reduce-scatter.11.cloned.1.call-start
  146.3 0.0 copy-done.2
  146.3 2.6 fusion.2
  148.9 0.0 reduce-scatter.11.cloned.1.call-update
  148.9 0.0 all-reduce.3.cloned.1.call-start
  149.0 53.6 %reduce-scatter.5.cloned.1.call-done = f32[64,2048]{1,0:T(8,128)} async-done(((f32[2048,2048]{1,0:T(8,128)}), f32[64,2048]{1,0:T(8,128)}) %reduce-scatter.5.cloned.1.call-update) | async-done | bytes 524304 | tf_op jit(solution)/shard_map/reduce_scatter | solution.py:13
  202.6 1.9 broadcast_multiply_fusion.1
  204.5 10.9 %reduce-scatter.9.cloned.1.call-done = f32[128,1024]{1,0:T(8,128)} async-done(((f32[128,2048]{1,0:T(8,128)}), f32[128,1024]{1,0:T(8,128)}) %reduce-scatter.9.cloned.1.call-update) | async-done | bytes 524304 | tf_op jit(solution)/shard_map/reduce_scatter | solution.py:29
  215.4 1.9 broadcast_multiply_fusion
  217.3 0.0 all-reduce.3.cloned.1.call-update
  217.3 77.1 %reduce-scatter.11.cloned.1.call-done = f32[128,12,16]{0,2,1:T(8,128)} async-done(((f32[128,12,256]{0,2,1:T(8,128)}), f32[128,12,16]{0,2,1:T(8,128)}) %reduce-scatter.11.cloned.1.call-update) | async-done | bytes 98320 | tf_op jit(solution)/shard_map/reduce_scatter | solution.py:35
  294.4 1.9 copy.17
  296.3 1.9 copy.18
  (2 shorter events, 0.0 us)
Async XLA Ops:
  8.0 1.2 copy-start
  8.0 24.1 %reduce-scatter.7.cloned.1.call-start = ((), (), s32[]{:S(2)}) async-start(), calls=%async_computation.6 | async-start | bytes 2359296 | tf_op jit(solution)/shard_map/reduce_scatter | solution.py:16
  17.9 117.6 %all-gather.2.cloned.1.call-start = ((), (), s32[]{:S(2)}) async-start(), calls=%async_computation.7 | async-start | bytes 13369344 | tf_op jit(solution)/shard_map/all_gather | solution.py:25
  32.2 170.4 %reduce-scatter.5.cloned.1.call-start = ((), (), s32[]{:S(2)}) async-start(), calls=%async_computation.5 | async-start | bytes 17301504 | tf_op jit(solution)/shard_map/reduce_scatter | solution.py:13
  85.8 49.7 %copy-start.1 = (f32[128,12,128]{2,0,1:T(8,128)S(1)}, f32[128,12,128]{2,0,1:T(8,128)}, u32[]{:S(2)}) copy-start(f32[128,12,128]{2,0,1:T(8,128)} %reduce-scatter.7.cloned.1.call-done) | copy-start | bytes 2359300
  85.9 60.4 %copy-start.2 = (f32[128,256]{1,0:T(8,128)S(1)}, f32[128,256]{1,0:T(8,128)}, u32[]{:S(2)}) copy-start(f32[128,256]{1,0:T(8,128)} %param.5) | copy-start | bytes 393220
  85.9 129.6 %reduce-scatter.9.cloned.1.call-start = ((), (), s32[]{:S(2)}) async-start(), calls=%async_computation.8 | async-start | bytes 1572864 | tf_op jit(solution)/shard_map/reduce_scatter | solution.py:29
  146.2 148.2 %reduce-scatter.11.cloned.1.call-start = ((), (), s32[]{:S(2)}) async-start(), calls=%async_computation.9 | async-start | bytes 1671168 | tf_op jit(solution)/shard_map/reduce_scatter | solution.py:35
  148.9 145.5 %all-reduce.3.cloned.1.call-start = ((), (), s32[]{:S(2)}) async-start(), calls=%async_computation.10 | async-start | bytes 2097152 | tf_op jit(solution)/shard_map/psum | solution.py:15
Sparse Core Ops, SparseCore 0:
  18.0 14.0 reduce-scatter.6
  34.5 101.0 all-gather.1
  217.5 47.6 all-reduce.2
Sparse Core Ops, SparseCore 1:
  85.9 116.6 reduce-scatter.4
  204.9 10.4 reduce-scatter.8
  219.4 74.9 reduce-scatter.10
where the time goes:
time: 306 us
  waiting for transfers between devices  205 us (67%)
  matrix products  64.7 us (21%)
  between operations  15.5 us (5%)
  blocking collectives  10.3 us (3%)
  local copies, waits for them, and re-layouts  5.38 us (2%)
  other arithmetic  3.77 us (1%)
    reduce_scatter x1, waiting for transfers between devices, per_device(): lax.psum_scatter(core_term_list, 'gy', scatter_dimension=2, tiled=True)  77.1 us
    reduce_scatter x1, waiting for transfers between devices, per_device(): lax.psum_scatter(partial_value, ('gx', 'gy'), scatter_dimension=0, tiled=...  53.6 us
    all_gather x1, waiting for transfers between devices, per_device(): lax.all_gather(reduced_result, 'gy', axis=2, tiled=True)  49.4 us
    dot_general x1, matrix products, per_device(): jnp.einsum('sxy,szy->xz', fibers, fibers, precision=exact_precision)  42.8 us
    reduce_scatter x1, waiting for transfers between devices, per_device(): lax.psum_scatter(jnp.einsum('xr,sxy->rsy', x_mode_basis, species_field, p...  14.2 us
    reduce_scatter x1, waiting for transfers between devices, per_device(): lax.psum_scatter(columns, 'gx', scatter_dimension=1, tiled=True)  10.9 us
    dot_general x1, matrix products, per_device(): jnp.einsum('rsy,rsz->yz', reduced_result, lax.all_gather(reduced_result,...  10.7 us
    all_to_all x1, blocking collectives, per_device(): lax.all_to_all(species_field, 'gx', split_axis=0, concat_axis=1, tiled=True)  10.3 us
  transfers between devices with their start and end apart: 6, of which 5 were waited for; matrix products, arithmetic and copies ran while one was open for 20% of the time, Pallas kernels for 0%

commit v1 on v0

v1 whole, which is shorter than its diff:
```python
import functools

import jax
import jax.numpy as jnp
from jax import lax
from jax.experimental import pallas as pl
from jax.experimental.pallas import tpu as pltpu
from jax.sharding import PartitionSpec as P

F32 = jnp.float32
BF16 = jnp.bfloat16
VMEM_LIMIT = 58 * 1024 * 1024

PERM_X = {d: [(y * 4 + x, y * 4 + (x + d) % 4) for y in range(4) for x in range(4)] for d in (1, 2, 3)}
PERM_Y = {d: [(y * 4 + x, (y + d) % 4 * 4 + x) for y in range(4) for x in range(4)] for d in (1, 2, 3)}
PERM_Z = {d: [(z, (z + d) % 4) for z in range(4)] for d in (1, 2, 3)}
SWAP = [(0, 1), (1, 0)]


def shift_x(v, d):
    return lax.ppermute(v, "gy", PERM_X[d])


def shift_y(v, d):
    return lax.ppermute(v, "gy", PERM_Y[d])


def shift_z(v, d):
    return lax.ppermute(v, "gz", PERM_Z[d])


def split(v):
    high = v.astype(BF16)
    return high, (v - high.astype(F32)).astype(BF16)


def dot3(a_high, a_low, b_high, b_low, dims):
    dot = functools.partial(lax.dot_general, dimension_numbers=(dims, ((), ())), preferred_element_type=F32)
    return dot(a_high, b_high) + (dot(a_high, b_low) + dot(a_low, b_high))


def project_kernel(field, basis, own, other):
    f_high, f_low = split(jnp.concatenate([field[0], field[1]], axis=1))
    x_high, x_low = split(basis[...])
    out = dot3(x_high, x_low, f_high, f_low, ((1,), (0,)))
    own[...] = out[:128]
    other[...] = out[128:]


def project(field, basis_t):
    out = jax.ShapeDtypeStruct((128, 1536), F32)
    return pl.pallas_call(
        project_kernel,
        grid=(6,),
        in_specs=[
            pl.BlockSpec((2, 1024, 128), lambda i: (i, 0, 0)),
            pl.BlockSpec((256, 1024), lambda i: (0, 0)),
        ],
        out_specs=[pl.BlockSpec((128, 256), lambda i: (0, i))] * 2,
        out_shape=[out, out],
        compiler_params=pltpu.CompilerParams(vmem_limit_bytes=VMEM_LIMIT),
        cost_estimate=pl.CostEstimate(flops=2400000000, bytes_accessed=9000000, transcendentals=0),
        name="project",
    )(field, basis_t)


def emit_pieces(place, buf, dy, lane_of, a_refs, b_refs, c_refs):
    x0, z0 = place[1], place[3]
    for dx in range(4):
        x = lax.rem(x0 + dx, 4)
        lane = pl.multiple_of(lane_of(x), 128)
        for dz in range(4):
            z = lax.rem(z0 + dz, 4)
            row = pl.multiple_of(x * 64 + z * 16, 16)
            a_refs[dx][dy, dz] = buf[pl.ds(row, 16), pl.ds(lane, 384)]
            b_refs[dy][dz, dx] = buf[pl.ds(row, 16), pl.ds(lane + 384, 384)]
            c_refs[dz][dx, dy] = buf[pl.ds(row, 16), pl.ds(lane + 768, 384)]


def gram_x_kernel(place, own, other, *refs):
    a_refs, b_refs, c_refs = refs[0:4], refs[4:8], refs[8:12]
    high, low, buf = refs[12:]
    for half, src in enumerate((own, other)):
        for s in range(12):
            v_high, v_low = split(src[s])
            high[half * 1024 : half * 1024 + 1024, s * 128 : s * 128 + 128] = v_high
            low[half * 1024 : half * 1024 + 1024, s * 128 : s * 128 + 128] = v_low
    y0 = place[2]
    for dy in range(4):
        b = lax.rem(y0 + dy, 4)
        rows = pl.ds(pl.multiple_of(b * 256, 256), 256)

        @pl.loop(0, 5)
        def _(n):
            cols = pl.ds(pl.multiple_of((b + n) * 256, 256), 256)
            buf[:, pl.ds(pl.multiple_of(n * 256, 256), 256)] = dot3(
                high[rows, :], low[rows, :], high[cols, :], low[cols, :], ((1,), (1,))
            )

        emit_pieces(place, buf, dy, lambda x: (x // 2) * 128, a_refs, b_refs, c_refs)


def gram_y_kernel(place, own, other, *refs):
    a_refs, b_refs, c_refs = refs[0:4], refs[4:8], refs[8:12]
    high, low, buf = refs[12:]
    for j in range(16):
        tiles = [src[j, :, s * 128 : s * 128 + 128] for src in (own, other) for s in range(12)]
        v = jnp.concatenate(tiles + [jnp.zeros((64, 128), F32)], axis=0).T
        v_high, v_low = split(v)
        for start in (j * 128, 2048 + j * 128):
            if start < 3072:
                high[start : start + 128, :] = v_high
                low[start : start + 128, :] = v_low
    h, y0 = place[0], place[2]
    for dy in range(4):
        b = lax.rem(y0 + dy, 4)
        starts = [pl.multiple_of((b * 4 + x) * 128 + h * 64, 64) for x in range(4)]
        l_high = jnp.concatenate([high[pl.ds(r, 64), :] for r in starts], axis=0)
        l_low = jnp.concatenate([low[pl.ds(r, 64), :] for r in starts], axis=0)
        for n in range(6):
            cols = pl.ds(pl.multiple_of(b * 512 + n * 256, 256), 256)
            buf[:, n * 256 : n * 256 + 256] = dot3(l_high, l_low, high[cols, :], low[cols, :], ((1,), (1,)))
        emit_pieces(place, buf, dy, lambda x: x * 128, a_refs, b_refs, c_refs)


def gram_pieces(kernel, name, place, own, other, scratch, flops):
    out = jax.ShapeDtypeStruct((4, 4, 16, 384), F32)
    whole = pl.BlockSpec(memory_space=pltpu.VMEM)
    outs = pl.pallas_call(
        kernel,
        in_specs=[pl.BlockSpec(memory_space=pltpu.SMEM), whole, whole],
        out_specs=[whole] * 12,
        out_shape=[out] * 12,
        scratch_shapes=scratch,
        compiler_params=pltpu.CompilerParams(vmem_limit_bytes=VMEM_LIMIT),
        cost_estimate=pl.CostEstimate(flops=flops, bytes_accessed=20000000, transcendentals=0),
        name=name,
    )(place, own, other)
    return outs[0:4], outs[4:8], outs[8:12]


def exchange(pieces, shift):
    return [pieces[0]] + [shift(pieces[d], d) for d in (1, 2, 3)]


def total(terms):
    return (terms[0] + terms[1]) + (terms[2] + terms[3])


def rolled(v, start):
    return lax.dynamic_slice_in_dim(jnp.concatenate([v, v], axis=0), start, v.shape[0], axis=0)


def per_device(species_field, x_mode_basis, y_mode_basis):
    h, j, z0 = lax.axis_index("gx"), lax.axis_index("gy"), lax.axis_index("gz")
    x0, y0 = j % 4, j // 4
    place = jnp.stack([h, x0, y0, z0]).astype(jnp.int32)
    nx = 2 * species_field.shape[1]
    ny = 16 * species_field.shape[2]
    slices = 4 * species_field.shape[0]
    ranks = x_mode_basis.shape[1]

    other_field = lax.ppermute(species_field, "gx", SWAP)
    basis_t = x_mode_basis.T
    basis_t = jnp.where(h == 0, basis_t, jnp.concatenate([basis_t[128:], basis_t[:128]], axis=0))
    mine, theirs = project(species_field, basis_t)
    reduced = mine + lax.ppermute(theirs, "gx", SWAP)
    fibers = lax.all_to_all(reduced.reshape(16, 8, 1536), "gy", 0, 0, tiled=True)
    other_fibers = lax.ppermute(fibers, "gx", SWAP)

    gx_a, gx_b, gx_c = gram_pieces(
        gram_x_kernel, "gram_x", place, species_field, other_field,
        [pltpu.VMEM((2048, 1536), BF16), pltpu.VMEM((2048, 1536), BF16), pltpu.VMEM((256, 1280), F32)], 12000000000,
    )
    gy_a, gy_b, gy_c = gram_pieces(
        gram_y_kernel, "gram_y", place, fibers, other_fibers,
        [pltpu.VMEM((3072, 256), BF16), pltpu.VMEM((3072, 256), BF16), pltpu.VMEM((256, 1536), F32)], 2400000000,
    )

    y_all = lax.all_to_all(
        jnp.broadcast_to(lax.dynamic_slice_in_dim(y_mode_basis, h * 64, 64, axis=0), (16, 64, 256)), "gy", 0, 0, tiled=True
    )
    y_other = lax.ppermute(y_all, "gx", SWAP)
    y_pair = jnp.where(h == 0, jnp.stack([y_all, y_other], axis=1), jnp.stack([y_other, y_all], axis=1))
    core = lax.dot_general(
        fibers.reshape(16, 8, 12, 128).transpose(2, 1, 0, 3).reshape(96, ny),
        y_pair.reshape(ny, 256),
        (((1,), (0,)), ((), ())),
        precision=lax.Precision.HIGH,
        preferred_element_type=F32,
    )
    core = lax.all_to_all(core.reshape(96, 16, 16).transpose(1, 0, 2).reshape(16, 12, 128), "gy", 0, 0, tiled=True)
    core = core.reshape(16, 12, 8, 16).transpose(0, 2, 1, 3).reshape(128, 12, 16)

    def first(pieces, shift):
        return exchange(pieces, shift)

    ax, bx, cx = first(gx_a, shift_x), first(gx_b, shift_y), first(gx_c, shift_z)
    ay, by, cy = first(gy_a, shift_x), first(gy_b, shift_y), first(gy_c, shift_z)

    def second(tx, ty, shift):
        parts = [jnp.stack([total([t[d] for t in tx]), total([t[d] for t in ty])], axis=1) for d in range(4)]
        return exchange(parts, shift)

    a2, b2, c2 = second(ax, ay, shift_y), second(bx, by, shift_z), second(cx, cy, shift_x)

    def third(t, shift):
        return total(exchange([total([v[d] for v in t]) for d in range(4)], shift))

    window = jnp.concatenate([third(a2, shift_z), third(b2, shift_x), third(c2, shift_y)], axis=2)

    wide = jnp.pad(window.reshape(2, 16, 9, 128).transpose(0, 2, 1, 3), ((0, 0), (0, 7), (0, 0), (0, 0)))
    block_x = h * 8 + j // 2
    direct_x = rolled(wide[0], (16 - block_x) % 16)
    direct_y = rolled(wide[1], (16 - j) % 16)
    to_x = jnp.broadcast_to(direct_x[:, None], (16, 2, 16, 128)).reshape(32, 16, 128)
    to_y = jnp.broadcast_to(direct_y[None], (2, 16, 16, 128)).reshape(32, 16, 128)
    got = lax.all_to_all(jnp.stack([to_x, to_y], axis=1), ("gx", "gy"), 0, 0, tiled=True)
    got_x = got[:, 0].reshape(16, 2, 16, 2, 64)
    got_x = jnp.where(j % 2 == 0, got_x[:, :, :, 0], got_x[:, :, :, 1]).transpose(0, 2, 1, 3).reshape(16, 16, 128)
    is_direct_x = (jnp.arange(16) - block_x) % 16 <= 8
    part_x = jnp.where(is_direct_x[:, None, None], direct_x, got_x)

    def half_of(v, k):
        return jnp.where(k == 0, v[:8], v[8:])

    keep = half_of(direct_y, h)
    come = lax.ppermute(half_of(direct_y, 1 - h), "gx", SWAP)
    direct_y = jnp.where(h == 0, jnp.stack([keep, come], axis=1), jnp.stack([come, keep], axis=1))
    got_y = jnp.stack([half_of(got[:16, 1], h), half_of(got[16:, 1], h)], axis=1)
    is_direct_y = (h * 8 + jnp.arange(8) - j) % 16 <= 8
    part_y = jnp.where(is_direct_y[:, None, None, None], direct_y, got_y)

    part = jnp.concatenate([part_x, part_y.reshape(16, 16, 128)], axis=0)
    quarters = exchange([part] * 4, shift_z)
    quarters = jnp.stack([quarters[3], quarters[2], quarters[1], quarters[0]])
    quarters = rolled(quarters, 3 - z0)

    all_x = quarters[:, :16].transpose(1, 0, 2, 3).reshape(16, 64, 128)
    turned_x = all_x.reshape(16, 64, 2, 64).transpose(0, 3, 2, 1).reshape(16, 64, 128)
    gram_x = jnp.where(is_direct_x[:, None, None], all_x, turned_x).transpose(1, 0, 2).reshape(64, nx) / (ny * slices)
    all_y = quarters[:, 16:].reshape(4, 8, 2, 16, 128).transpose(1, 2, 0, 3, 4).reshape(8, 128, 128)
    turned_y = all_y.transpose(0, 2, 1)
    gram_y = jnp.where(is_direct_y[:, None, None], all_y, turned_y).transpose(1, 0, 2).reshape(128, ny // 2) / (ranks * slices)
    return (gram_x, gram_y, core)


def solution(mesh):
    in_specs = (P("gz", "gx", "gy"), P("gx", None), P("gy", None))
    out_specs = (P(("gx", "gy"), None), P("gy", "gx"), P("gx", "gz", "gy"))
    return jax.shard_map(
        per_device, mesh=mesh, in_specs=in_specs, out_specs=out_specs, check_vma=False
    )
```

time: 306 us -> 244 us (0.80)
  waiting for transfers between devices: 205 us -> 67.1 us
  starting transfers between devices: 0.47 us -> 72.6 us
  matrix products: 64.7 us -> 0.98 us
  Pallas kernels: 0 us -> 40.2 us
  other arithmetic: 3.77 us -> 19.9 us
  between operations: 15.5 us -> 1.42 us
  local copies, waits for them, and re-layouts: 5.38 us -> 19.3 us
  blocking collectives: 10.3 us -> 21.8 us
    reduce_scatter x4 -> x0, waiting for transfers between devices: 156 us -> none  [the longest x1 77.1 us: per_device(): lax.psum_scatter(core_term_list, 'gy', scatter_dimension=2, tiled=True)]
    dot_general x4 -> x1, matrix products: 64.7 us -> 0.98 us  [per_device(): lax.dot_general(fibers.reshape(16, 8, 12, 128).transpose(2, 1, 0, 3).resh...]
    ppermute x0 -> x44, starting transfers between devices: none -> 58.4 us  [the longest x15 25.7 us: shift_z(): return lax.ppermute(v, 'gz', PERM_Z[d])]
    ppermute x0 -> x44, waiting for transfers between devices: none -> 52.7 us  [the longest x15 24.6 us: shift_z(): return lax.ppermute(v, 'gz', PERM_Z[d])]
    all_gather x1 -> x0, waiting for transfers between devices: 49.4 us -> none  [per_device(): lax.all_gather(reduced_result, 'gy', axis=2, tiled=True)]
    pallas_call x0 -> x3, Pallas kernels: none -> 40.2 us  [the longest x2 32.8 us: gram_pieces(): pl.pallas_call(kernel, in_specs=[pl.BlockSpec(memory_space=pltpu.SMEM), w...]
    all_to_all x0 -> x3, waiting for transfers between devices: none -> 14.5 us  [the longest x1 7.45 us: per_device(): lax.all_to_all(jnp.stack([to_x, to_y], axis=1), ('gx', 'gy'), 0, 0, tiled...]
    all_to_all x0 -> x3, starting transfers between devices: none -> 14.3 us  [the longest x1 6.95 us: per_device(): lax.all_to_all(jnp.stack([to_x, to_y], axis=1), ('gx', 'gy'), 0, 0, tiled...]
  transfers between devices with their start and end apart: 6 -> 47, of which waited for: 5 -> 20; matrix products, arithmetic and copies ran while one was open for 20% -> 10% of each run, Pallas kernels for 0% -> 17%
where the time goes in v1:
time: 244 us; the launch traced here: 243 us
  starting transfers between devices  72.6 us (30%)
  waiting for transfers between devices  67.1 us (27%)
  Pallas kernels  40.2 us (16%)
  blocking collectives  21.8 us (9%)
  other arithmetic  19.9 us (8%)
  local copies, waits for them, and re-layouts  19.3 us (8%)
    pallas_call x2, Pallas kernels, gram_pieces(): pl.pallas_call(kernel, in_specs=[pl.BlockSpec(memory_space=pltpu.SMEM), w...  32.8 us
    ppermute x15, starting transfers between devices, shift_z(): return lax.ppermute(v, 'gz', PERM_Z[d])  25.7 us
    ppermute x15, waiting for transfers between devices, shift_z(): return lax.ppermute(v, 'gz', PERM_Z[d])  24.6 us
    all_to_all x1, blocking collectives, per_device(): lax.all_to_all(reduced.reshape(16, 8, 1536), 'gy', 0, 0, tiled=True)  21.8 us
    ppermute x12, starting transfers between devices, shift_y(): return lax.ppermute(v, 'gy', PERM_Y[d])  18 us
    ppermute x12, waiting for transfers between devices, shift_x(): return lax.ppermute(v, 'gy', PERM_X[d])  15.7 us
    ppermute x12, starting transfers between devices, shift_x(): return lax.ppermute(v, 'gy', PERM_X[d])  13.7 us
    ppermute x12, waiting for transfers between devices, shift_y(): return lax.ppermute(v, 'gy', PERM_Y[d])  8.79 us
  transfers between devices with their start and end apart: 47, of which 20 were waited for; matrix products, arithmetic and copies ran while one was open for 10% of the time, Pallas kernels for 17%

profile of v1, /device:TPU:0, one launch (start us, length us, event | category | flops | bytes accessed | tf_op | source)
XLA Modules:
  0.0 243.4 jit_solution(18396960593357604262)
XLA Ops:
  3.6 7.4 %project.1 = (f32[128,1536]{1,0:T(8,128)}, f32[128,1536]{1,0:T(8,128)}) custom-call(f32[12,1024,128]{2,1,0:T(8,128)} %field.1, f32[256,1024]{1,0:T(8,128)} %maximum_select_fusion.1.basis), custom_call_target="tpu_custom_call" | custom-call | flops 2400000000 | bytes 9000000 | tf_op jit(solution)/shard_map/project/pallas_call | solution.py:52
  11.5 2.1 collective-permute-done.4
  14.9 21.8 %all_to_all.20.own = f32[16,8,1536]{2,1,0:T(8,128)S(1)} all-to-all(f32[16,8,1536]{2,1,0:T(8,128)S(1)} %add_bitcast_fusion), channel_id=1, replica_groups=mesh['gx'=2,'gy'=16,'gz'=4] {'gy'}, dimensions={0} | all-to-all | bytes 1572864 | tf_op jit(solution)/shard_map/all_to_all | solution.py:168
  39.9 6.8 %gram_y.1 = (f32[4,4,16,384]{3,2,1,0:T(8,128)}, f32[4,4,16,384]{3,2,1,0:T(8,128)}, f32[4,4,16,384]{3,2,1,0:T(8,128)}, f32[4,4,16,384]{3,2,1,0:T(8,128)}, f32[4,4...) custom-call(s32[4]{0:T(128)} %pad_add_fusion.place, ...), custom_call_target="tpu_custom_call" | custom-call | flops 2400000000 | bytes 20000000 | tf_op jit(solution)/shard_map/gram_y/pallas_call | solution.py:129
  49.9 3.8 %all-to-all-start.2 = ((f32[16,64,256]{2,1,0:T(8,128)}), f32[16,64,256]{2,1,0:T(8,128)S(1)}, u32[]{:S(2)}, u32[]{:S(2)}) async-start(f32[16,64,256]{2,1,0:T(8,128)} %broadcast_in_dim.63), calls=%async_computation.2 | async-start | bytes 2097152 | tf_op jit(solution)/shard_map/all_to_all | solution.py:180
  54.0 3.1 %collective-permute-start.8 = (f32[4,4,16,384]{3,2,1,0:T(8,128)}, f32[4,4,16,384]{3,2,1,0:T(8,128)S(1)}, u32[]{:S(2)}, u32[]{:S(2)}) collective-permute-start(f32[4,4,16,384]{3,2,1,0:T(8,128)} %get-tuple-element.38), channel_id=1, source_target_pairs={{0,12},{4,0},{8,4},{12,8},{16,28},{20,16},{24,20},{28,24},{32,44},... | collective-permute-start | bytes 1179656 | tf_op jit(solution)/shard_map/ppermute | solution.py:21
  58.6 14.2 %collective-permute-done.6 = f32[4,4,16,384]{3,2,1,0:T(8,128)S(1)} collective-permute-done((f32[4,4,16,384]{3,2,1,0:T(8,128)}, f32[4,4,16,384]{3,2,1,0:T(8,128)S(1)}, u32[]{:S(2)}, u32[]{:S(2)}) %collective-permute-start.6) | collective-permute-done | bytes 393248 | tf_op jit(solution)/shard_map/ppermute | solution.py:21
  77.3 26.0 %gram_x.1 = (f32[4,4,16,384]{3,2,1,0:T(8,128)}, f32[4,4,16,384]{3,2,1,0:T(8,128)}, f32[4,4,16,384]{3,2,1,0:T(8,128)}, f32[4,4,16,384]{3,2,1,0:T(8,128)}, f32[4,4...) custom-call(s32[4]{0:T(128)} %pad_add_fusion.place, ...), custom_call_target="tpu_custom_call" | custom-call | flops 12000000000 | bytes 20000000 | tf_op jit(solution)/shard_map/gram_x/pallas_call | solution.py:129
  103.4 3.7 %collective-permute-start.31 = (f32[4,4,16,384]{3,2,1,0:T(8,128)}, f32[4,4,16,384]{3,2,1,0:T(8,128)S(1)}, u32[]{:S(2)}, u32[]{:S(2)}) collective-permute-start(f32[4,4,16,384]{3,2,1,0:T(8,128)} %get-tuple-element.53), channel_id=1, source_target_pairs={{0,2},{1,3},{2,0},{3,1},{4,6},{5,7},{6,4},{7,5},{8,10},{9,11},{10,... | collective-permute-start | bytes 1179656 | tf_op jit(solution)/shard_map/ppermute | solution.py:29
  110.9 2.4 collective-permute-start.3
  115.3 4.6 %collective-permute-done.32 = f32[4,4,16,384]{3,2,1,0:T(8,128)S(1)} collective-permute-done((f32[4,4,16,384]{3,2,1,0:T(8,128)}, f32[4,4,16,384]{3,2,1,0:T(8,128)S(1)}, u32[]{:S(2)}, u32[]{:S(2)}) %collective-permute-start.32) | collective-permute-done | bytes 393248 | tf_op jit(solution)/shard_map/ppermute | solution.py:29
  119.9 3.2 %collective-permute-start.16 = (f32[4,4,16,384]{3,2,1,0:T(8,128)}, f32[4,4,16,384]{3,2,1,0:T(8,128)}, u32[]{:S(2)}, u32[]{:S(2)}) collective-permute-start(f32[4,4,16,384]{3,2,1,0:T(8,128)} %get-tuple-element.41), channel_id=1, source_target_pairs={{0,32},{4,36},{8,40},{12,44},{16,48},{20,52},{24,56},{28,60},{32,0... | collective-permute-start | bytes 1179656 | tf_op jit(solution)/shard_map/ppermute | solution.py:25
  123.8 3.2 %collective-permute-start.17 = (f32[4,4,16,384]{3,2,1,0:T(8,128)}, f32[4,4,16,384]{3,2,1,0:T(8,128)}, u32[]{:S(2)}, u32[]{:S(2)}) collective-permute-start(f32[4,4,16,384]{3,2,1,0:T(8,128)} %get-tuple-element.42), channel_id=1, source_target_pairs={{0,48},{4,52},{8,56},{12,60},{16,0},{20,4},{24,8},{28,12},{32,16},... | collective-permute-start | bytes 1179656 | tf_op jit(solution)/shard_map/ppermute | solution.py:25
  132.8 4.0 %collective-permute-start.29 = (f32[4,4,16,384]{3,2,1,0:T(8,128)}, f32[4,4,16,384]{3,2,1,0:T(8,128)S(1)}, u32[]{:S(2)}, u32[]{:S(2)}) collective-permute-start(f32[4,4,16,384]{3,2,1,0:T(8,128)} %get-tuple-element.50), channel_id=1, source_target_pairs={{0,3},{1,0},{2,1},{3,2},{4,7},{5,4},{6,5},{7,6},{8,11},{9,8},{10,9... | collective-permute-start | bytes 1179656 | tf_op jit(solution)/shard_map/ppermute | solution.py:29
  136.8 3.8 %collective-permute-done.17 = f32[4,4,16,384]{3,2,1,0:T(8,128)} collective-permute-done((f32[4,4,16,384]{3,2,1,0:T(8,128)}, f32[4,4,16,384]{3,2,1,0:T(8,128)}, u32[]{:S(2)}, u32[]{:S(2)}) %collective-permute-start.17) | collective-permute-done | bytes 393248 | tf_op jit(solution)/shard_map/ppermute | solution.py:25
  142.6 6.6 %collective-permute-done.27 = f32[4,4,16,384]{3,2,1,0:T(8,128)S(1)} collective-permute-done((f32[4,4,16,384]{3,2,1,0:T(8,128)}, f32[4,4,16,384]{3,2,1,0:T(8,128)S(1)}, u32[]{:S(2)}, u32[]{:S(2)}) %collective-permute-start.27) | collective-permute-done | bytes 393248 | tf_op jit(solution)/shard_map/ppermute | solution.py:29
  153.4 3.4 %collective-permute-start.22 = (f32[4,2,16,384]{3,2,1,0:T(8,128)S(1)}, f32[4,2,16,384]{3,2,1,0:T(8,128)S(1)}, u32[]{:S(2)}, u32[]{:S(2)}) collective-permute-start(f32[4,2,16,384]{3,2,1,0:T(8,128)S(1)} %pad_maximum_fusion.6), channel_id=1, source_target_pairs={{0,2},{1,3},{2,0},{3,1},{4,6},{5,7},{6,4},{7,5},{8,10},{9,11},{10,... | collective-permute-start | bytes 589832 | tf_op jit(solution)/shard_map/ppermute | solution.py:29
  157.8 2.3 collective-permute-done.21
  161.9 3.6 %collective-permute-done.22 = f32[4,2,16,384]{3,2,1,0:T(8,128)S(1)} collective-permute-done((f32[4,2,16,384]{3,2,1,0:T(8,128)S(1)}, f32[4,2,16,384]{3,2,1,0:T(8,128)S(1)}, u32[]{:S(2)}, u32[]{:S(2)}) %collective-permute-start.22) | collective-permute-done | bytes 196640 | tf_op jit(solution)/shard_map/ppermute | solution.py:29
  166.6 3.4 %collective-permute-start.13 = (f32[2,16,384]{2,1,0:T(8,128)S(1)}, f32[2,16,384]{2,1,0:T(8,128)S(1)}, u32[]{:S(2)}, u32[]{:S(2)}) collective-permute-start(f32[2,16,384]{2,1,0:T(8,128)S(1)} %get-tuple-element.96), channel_id=1, source_target_pairs={{0,2},{1,3},{2,0},{3,1},{4,6},{5,7},{6,4},{7,5},{8,10},{9,11},{10,... | collective-permute-start | bytes 147464 | tf_op jit(solution)/shard_map/ppermute | solution.py:29
  170.0 2.9 %collective-permute-start.14 = (f32[2,16,384]{2,1,0:T(8,128)S(1)}, f32[2,16,384]{2,1,0:T(8,128)S(1)}, u32[]{:S(2)}, u32[]{:S(2)}) collective-permute-start(f32[2,16,384]{2,1,0:T(8,128)S(1)} %get-tuple-element.95), channel_id=1, source_target_pairs={{0,3},{1,0},{2,1},{3,2},{4,7},{5,4},{6,5},{7,6},{8,11},{9,8},{10,9... | collective-permute-start | bytes 147464 | tf_op jit(solution)/shard_map/ppermute | solution.py:29
  176.4 2.2 collective-permute-start.38
  178.8 3.1 %collective-permute-start.37 = (f32[2,16,384]{2,1,0:T(8,128)S(1)}, f32[2,16,384]{2,1,0:T(8,128)S(1)}, u32[]{:S(2)}, u32[]{:S(2)}) collective-permute-start(f32[2,16,384]{2,1,0:T(8,128)S(1)} %get-tuple-element.101), channel_id=1, source_target_pairs={{0,32},{4,36},{8,40},{12,44},{16,48},{20,52},{24,56},{28,60},{32,0... | collective-permute-start | bytes 147464 | tf_op jit(solution)/shard_map/ppermute | solution.py:25
  181.9 2.1 collective-permute-done.36
  186.1 6.9 %all-to-all-start.1 = ((f32[32,2,16,128]{3,1,2,0:T(2,128)}), f32[32,2,16,128]{3,1,2,0:T(2,128)S(1)}, u32[]{:S(2)}, u32[]{:S(2)}) async-start(f32[32,2,16,128]{3,1,2,0:T(2,128)} %pad_maximum_fusion), calls=%async_computation.1 | async-start | bytes 1048576 | tf_op jit(solution)/shard_map/all_to_all | solution.py:218
  195.0 1.9 copy.164
  197.6 7.5 %all-to-all-done.1 = f32[32,2,16,128]{3,1,2,0:T(2,128)S(1)} async-done(((f32[32,2,16,128]{3,1,2,0:T(2,128)}), f32[32,2,16,128]{3,1,2,0:T(2,128)S(1)}, u32[]{:S(2)}, u32[]{:S(2)}) %all-to-all-start.1) | async-done | bytes 524320 | tf_op jit(solution)/shard_map/all_to_all | solution.py:218
  206.8 1.9 fusion.116
  216.9 3.5 %all-to-all-start.3 = ((f32[16,12,128]{2,1,0:T(8,128)}), f32[16,12,128]{2,1,0:T(8,128)S(1)}, u32[]{:S(2)}, u32[]{:S(2)}) async-start(f32[16,12,128]{2,1,0:T(8,128)} %reshape.1125), calls=%async_computation.3 | async-start | bytes 262144 | tf_op jit(solution)/shard_map/all_to_all | solution.py:192
  221.4 7.0 %all-to-all-done.3 = f32[16,12,128]{2,1,0:T(8,128)S(1)} async-done(((f32[16,12,128]{2,1,0:T(8,128)}), f32[16,12,128]{2,1,0:T(8,128)S(1)}, u32[]{:S(2)}, u32[]{:S(2)}) %all-to-all-start.3) | async-done | bytes 98336 | tf_op jit(solution)/shard_map/all_to_all | solution.py:192
  229.6 2.0 collective-permute-start.42
  231.6 6.0 %collective-permute-done.42 = f32[32,16,128]{2,0,1:T(8,128)S(1)} collective-permute-done((f32[32,16,128]{2,0,1:T(8,128)}, f32[32,16,128]{2,0,1:T(8,128)S(1)}, u32[]{:S(2)}, u32[]{:S(2)}) %collective-permute-start.42) | collective-permute-done | bytes 262176 | tf_op jit(solution)/shard_map/ppermute | solution.py:29
  (194 shorter events, 65.6 us)
Async XLA Ops:
  0.6 74.8 %collective-permute-start = (f32[12,1024,128]{2,1,0:T(8,128)}, f32[12,1024,128]{2,1,0:T(8,128)}, u32[]{:S(2)}, u32[]{:S(2)}) collective-permute-start(f32[12,1024,128]{2,1,0:T(8,128)} %field.1), channel_id=1, source_target_pairs={{0,64},{64,0},{1,65},{65,1},{2,66},{66,2},{3,67},{67,3},{4,68},{68... | collective-permute-start | bytes 18874376 | tf_op jit(solution)/shard_map/ppermute | solution.py:163
  46.7 26.0 %collective-permute-start.6 = (f32[4,4,16,384]{3,2,1,0:T(8,128)}, f32[4,4,16,384]{3,2,1,0:T(8,128)S(1)}, u32[]{:S(2)}, u32[]{:S(2)}) collective-permute-start(f32[4,4,16,384]{3,2,1,0:T(8,128)} %get-tuple-element.36), channel_id=1, source_target_pairs={{0,4},{4,8},{8,12},{12,0},{16,20},{20,24},{24,28},{28,16},{32,36},... | collective-permute-start | bytes 1179656 | tf_op jit(solution)/shard_map/ppermute | solution.py:21
  47.3 26.3 %collective-permute-start.7 = (f32[4,4,16,384]{3,2,1,0:T(8,128)}, f32[4,4,16,384]{3,2,1,0:T(8,128)S(1)}, u32[]{:S(2)}, u32[]{:S(2)}) collective-permute-start(f32[4,4,16,384]{3,2,1,0:T(8,128)} %get-tuple-element.37), channel_id=1, source_target_pairs={{0,8},{4,12},{8,0},{12,4},{16,24},{20,28},{24,16},{28,20},{32,40},... | collective-permute-start | bytes 1179656 | tf_op jit(solution)/shard_map/ppermute | solution.py:21
  49.9 77.9 %all-to-all-start.2 = ((f32[16,64,256]{2,1,0:T(8,128)}), f32[16,64,256]{2,1,0:T(8,128)S(1)}, u32[]{:S(2)}, u32[]{:S(2)}) async-start(f32[16,64,256]{2,1,0:T(8,128)} %broadcast_in_dim.63), calls=%async_computation.2 | async-start | bytes 2097152 | tf_op jit(solution)/shard_map/all_to_all | solution.py:180
  54.0 49.4 %collective-permute-start.8 = (f32[4,4,16,384]{3,2,1,0:T(8,128)}, f32[4,4,16,384]{3,2,1,0:T(8,128)S(1)}, u32[]{:S(2)}, u32[]{:S(2)}) collective-permute-start(f32[4,4,16,384]{3,2,1,0:T(8,128)} %get-tuple-element.38), channel_id=1, source_target_pairs={{0,12},{4,0},{8,4},{12,8},{16,28},{20,16},{24,20},{28,24},{32,44},... | collective-permute-start | bytes 1179656 | tf_op jit(solution)/shard_map/ppermute | solution.py:21
  57.1 49.9 %collective-permute-start.18 = (f32[4,4,16,384]{3,2,1,0:T(8,128)}, f32[4,4,16,384]{3,2,1,0:T(8,128)S(1)}, u32[]{:S(2)}, u32[]{:S(2)}) collective-permute-start(f32[4,4,16,384]{3,2,1,0:T(8,128)} %get-tuple-element.44), channel_id=1, source_target_pairs={{0,16},{4,20},{8,24},{12,28},{16,32},{20,36},{24,40},{28,44},{32,4... | collective-permute-start | bytes 1179656 | tf_op jit(solution)/shard_map/ppermute | solution.py:25
  72.7 35.3 %collective-permute-start.19 = (f32[4,4,16,384]{3,2,1,0:T(8,128)S(1)}, f32[4,4,16,384]{3,2,1,0:T(8,128)S(1)}, u32[]{:S(2)}, u32[]{:S(2)}) collective-permute-start(f32[4,4,16,384]{3,2,1,0:T(8,128)S(1)} %copy-done.19), channel_id=1, source_target_pairs={{0,32},{4,36},{8,40},{12,44},{16,48},{20,52},{24,56},{28,60},{32,0... | collective-permute-start | bytes 1179656 | tf_op jit(solution)/shard_map/ppermute | solution.py:25
  73.6 36.3 %collective-permute-start.20 = (f32[4,4,16,384]{3,2,1,0:T(8,128)}, f32[4,4,16,384]{3,2,1,0:T(8,128)}, u32[]{:S(2)}, u32[]{:S(2)}) collective-permute-start(f32[4,4,16,384]{3,2,1,0:T(8,128)} %get-tuple-element.46), channel_id=1, source_target_pairs={{0,48},{4,52},{8,56},{12,60},{16,0},{20,4},{24,8},{28,12},{32,16},... | collective-permute-start | bytes 1179656 | tf_op jit(solution)/shard_map/ppermute | solution.py:25
  75.4 35.5 %collective-permute-start.30 = (f32[4,4,16,384]{3,2,1,0:T(8,128)}, f32[4,4,16,384]{3,2,1,0:T(8,128)S(1)}, u32[]{:S(2)}, u32[]{:S(2)}) collective-permute-start(f32[4,4,16,384]{3,2,1,0:T(8,128)} %get-tuple-element.52), channel_id=1, source_target_pairs={{0,1},{1,2},{2,3},{3,0},{4,5},{5,6},{6,7},{7,4},{8,9},{9,10},{10,1... | collective-permute-start | bytes 1179656 | tf_op jit(solution)/shard_map/ppermute | solution.py:29
  103.4 11.7 %collective-permute-start.31 = (f32[4,4,16,384]{3,2,1,0:T(8,128)}, f32[4,4,16,384]{3,2,1,0:T(8,128)S(1)}, u32[]{:S(2)}, u32[]{:S(2)}) collective-permute-start(f32[4,4,16,384]{3,2,1,0:T(8,128)} %get-tuple-element.53), channel_id=1, source_target_pairs={{0,2},{1,3},{2,0},{3,1},{4,6},{5,7},{6,4},{7,5},{8,10},{9,11},{10,... | collective-permute-start | bytes 1179656 | tf_op jit(solution)/shard_map/ppermute | solution.py:29
  107.0 12.8 %collective-permute-start.32 = (f32[4,4,16,384]{3,2,1,0:T(8,128)}, f32[4,4,16,384]{3,2,1,0:T(8,128)S(1)}, u32[]{:S(2)}, u32[]{:S(2)}) collective-permute-start(f32[4,4,16,384]{3,2,1,0:T(8,128)} %get-tuple-element.54), channel_id=1, source_target_pairs={{0,3},{1,0},{2,1},{3,2},{4,7},{5,4},{6,5},{7,6},{8,11},{9,8},{10,9... | collective-permute-start | bytes 1179656 | tf_op jit(solution)/shard_map/ppermute | solution.py:29
  108.0 15.8 %collective-permute-start.1 = (f32[4,4,16,384]{3,2,1,0:T(8,128)}, f32[4,4,16,384]{3,2,1,0:T(8,128)S(1)}, u32[]{:S(2)}, u32[]{:S(2)}) collective-permute-start(f32[4,4,16,384]{3,2,1,0:T(8,128)} %get-tuple-element.30), channel_id=1, source_target_pairs={{0,4},{4,8},{8,12},{12,0},{16,20},{20,24},{24,28},{28,16},{32,36},... | collective-permute-start | bytes 1179656 | tf_op jit(solution)/shard_map/ppermute | solution.py:21
  109.9 17.9 %collective-permute-start.2 = (f32[4,4,16,384]{3,2,1,0:T(8,128)}, f32[4,4,16,384]{3,2,1,0:T(8,128)}, u32[]{:S(2)}, u32[]{:S(2)}) collective-permute-start(f32[4,4,16,384]{3,2,1,0:T(8,128)} %get-tuple-element.31), channel_id=1, source_target_pairs={{0,8},{4,12},{8,0},{12,4},{16,24},{20,28},{24,16},{28,20},{32,40},... | collective-permute-start | bytes 1179656 | tf_op jit(solution)/shard_map/ppermute | solution.py:21
  110.9 16.9 %collective-permute-start.3 = (f32[4,4,16,384]{3,2,1,0:T(8,128)}, f32[4,4,16,384]{3,2,1,0:T(8,128)}, u32[]{:S(2)}, u32[]{:S(2)}) collective-permute-start(f32[4,4,16,384]{3,2,1,0:T(8,128)} %get-tuple-element.32), channel_id=1, source_target_pairs={{0,12},{4,0},{8,4},{12,8},{16,28},{20,16},{24,20},{28,24},{32,44},... | collective-permute-start | bytes 1179656 | tf_op jit(solution)/shard_map/ppermute | solution.py:21
  115.0 17.7 %collective-permute-start.15 = (f32[4,4,16,384]{3,2,1,0:T(8,128)}, f32[4,4,16,384]{3,2,1,0:T(8,128)}, u32[]{:S(2)}, u32[]{:S(2)}) collective-permute-start(f32[4,4,16,384]{3,2,1,0:T(8,128)} %get-tuple-element.40), channel_id=1, source_target_pairs={{0,16},{4,20},{8,24},{12,28},{16,32},{20,36},{24,40},{28,44},{32,4... | collective-permute-start | bytes 1179656 | tf_op jit(solution)/shard_map/ppermute | solution.py:25
  119.9 12.9 %collective-permute-start.16 = (f32[4,4,16,384]{3,2,1,0:T(8,128)}, f32[4,4,16,384]{3,2,1,0:T(8,128)}, u32[]{:S(2)}, u32[]{:S(2)}) collective-permute-start(f32[4,4,16,384]{3,2,1,0:T(8,128)} %get-tuple-element.41), channel_id=1, source_target_pairs={{0,32},{4,36},{8,40},{12,44},{16,48},{20,52},{24,56},{28,60},{32,0... | collective-permute-start | bytes 1179656 | tf_op jit(solution)/shard_map/ppermute | solution.py:25
  123.8 16.8 %collective-permute-start.17 = (f32[4,4,16,384]{3,2,1,0:T(8,128)}, f32[4,4,16,384]{3,2,1,0:T(8,128)}, u32[]{:S(2)}, u32[]{:S(2)}) collective-permute-start(f32[4,4,16,384]{3,2,1,0:T(8,128)} %get-tuple-element.42), channel_id=1, source_target_pairs={{0,48},{4,52},{8,56},{12,60},{16,0},{20,4},{24,8},{28,12},{32,16},... | collective-permute-start | bytes 1179656 | tf_op jit(solution)/shard_map/ppermute | solution.py:25
  127.7 65.7 %collective-permute-start.43 = (f32[16,64,256]{2,1,0:T(8,128)S(1)}, f32[16,64,256]{2,1,0:T(8,128)S(1)}, u32[]{:S(2)}, u32[]{:S(2)}) collective-permute-start(f32[16,64,256]{2,1,0:T(8,128)S(1)} %all-to-all-done.2), channel_id=1, source_target_pairs={{0,64},{64,0},{1,65},{65,1},{2,66},{66,2},{3,67},{67,3},{4,68},{68... | collective-permute-start | bytes 3145736 | tf_op jit(solution)/shard_map/ppermute | solution.py:183
  127.8 21.4 %collective-permute-start.27 = (f32[4,4,16,384]{3,2,1,0:T(8,128)}, f32[4,4,16,384]{3,2,1,0:T(8,128)S(1)}, u32[]{:S(2)}, u32[]{:S(2)}) collective-permute-start(f32[4,4,16,384]{3,2,1,0:T(8,128)} %get-tuple-element.48), channel_id=1, source_target_pairs={{0,1},{1,2},{2,3},{3,0},{4,5},{5,6},{6,7},{7,4},{8,9},{9,10},{10,1... | collective-permute-start | bytes 1179656 | tf_op jit(solution)/shard_map/ppermute | solution.py:29
  132.8 17.1 %collective-permute-start.28 = (f32[4,4,16,384]{3,2,1,0:T(8,128)}, f32[4,4,16,384]{3,2,1,0:T(8,128)S(1)}, u32[]{:S(2)}, u32[]{:S(2)}) collective-permute-start(f32[4,4,16,384]{3,2,1,0:T(8,128)} %get-tuple-element.49), channel_id=1, source_target_pairs={{0,2},{1,3},{2,0},{3,1},{4,6},{5,7},{6,4},{7,5},{8,10},{9,11},{10,... | collective-permute-start | bytes 1179656 | tf_op jit(solution)/shard_map/ppermute | solution.py:29
  132.8 19.6 %collective-permute-start.29 = (f32[4,4,16,384]{3,2,1,0:T(8,128)}, f32[4,4,16,384]{3,2,1,0:T(8,128)S(1)}, u32[]{:S(2)}, u32[]{:S(2)}) collective-permute-start(f32[4,4,16,384]{3,2,1,0:T(8,128)} %get-tuple-element.50), channel_id=1, source_target_pairs={{0,3},{1,0},{2,1},{3,2},{4,7},{5,4},{6,5},{7,6},{8,11},{9,8},{10,9... | collective-permute-start | bytes 1179656 | tf_op jit(solution)/shard_map/ppermute | solution.py:29
  140.6 12.8 %collective-permute-start.9 = (f32[4,2,16,384]{3,2,1,0:T(8,128)S(1)}, f32[4,2,16,384]{3,2,1,0:T(8,128)S(1)}, u32[]{:S(2)}, u32[]{:S(2)}) collective-permute-start(f32[4,2,16,384]{3,2,1,0:T(8,128)S(1)} %copy.134), channel_id=1, source_target_pairs={{0,16},{4,20},{8,24},{12,28},{16,32},{20,36},{24,40},{28,44},{32,4... | collective-permute-start | bytes 589832 | tf_op jit(solution)/shard_map/ppermute | solution.py:25
  149.2 8.0 %collective-permute-start.10 = (f32[4,2,16,384]{3,2,1,0:T(8,128)S(1)}, f32[4,2,16,384]{3,2,1,0:T(8,128)S(1)}, u32[]{:S(2)}, u32[]{:S(2)}) collective-permute-start(f32[4,2,16,384]{3,2,1,0:T(8,128)S(1)} %pad_maximum_fusion.3), channel_id=1, source_target_pairs={{0,32},{4,36},{8,40},{12,44},{16,48},{20,52},{24,56},{28,60},{32,0... | collective-permute-start | bytes 589832 | tf_op jit(solution)/shard_map/ppermute | solution.py:25
  153.4 12.1 %collective-permute-start.22 = (f32[4,2,16,384]{3,2,1,0:T(8,128)S(1)}, f32[4,2,16,384]{3,2,1,0:T(8,128)S(1)}, u32[]{:S(2)}, u32[]{:S(2)}) collective-permute-start(f32[4,2,16,384]{3,2,1,0:T(8,128)S(1)} %pad_maximum_fusion.6), channel_id=1, source_target_pairs={{0,2},{1,3},{2,0},{3,1},{4,6},{5,7},{6,4},{7,5},{8,10},{9,11},{10,... | collective-permute-start | bytes 589832 | tf_op jit(solution)/shard_map/ppermute | solution.py:29
  157.2 8.3 %collective-permute-start.23 = (f32[4,2,16,384]{3,2,1,0:T(8,128)S(1)}, f32[4,2,16,384]{3,2,1,0:T(8,128)S(1)}, u32[]{:S(2)}, u32[]{:S(2)}) collective-permute-start(f32[4,2,16,384]{3,2,1,0:T(8,128)S(1)} %copy.141), channel_id=1, source_target_pairs={{0,3},{1,0},{2,1},{3,2},{4,7},{5,4},{6,5},{7,6},{8,11},{9,8},{10,9... | collective-permute-start | bytes 589832 | tf_op jit(solution)/shard_map/ppermute | solution.py:29
  157.8 8.8 %collective-permute-start.33 = (f32[4,2,16,384]{3,2,1,0:T(8,128)S(1)}, f32[4,2,16,384]{3,2,1,0:T(8,128)S(1)}, u32[]{:S(2)}, u32[]{:S(2)}) collective-permute-start(f32[4,2,16,384]{3,2,1,0:T(8,128)S(1)} %copy.143), channel_id=1, source_target_pairs={{0,4},{4,8},{8,12},{12,0},{16,20},{20,24},{24,28},{28,16},{32,36},... | collective-permute-start | bytes 589832 | tf_op jit(solution)/shard_map/ppermute | solution.py:21
  160.1 9.9 %collective-permute-start.34 = (f32[4,2,16,384]{3,2,1,0:T(8,128)S(1)}, f32[4,2,16,384]{3,2,1,0:T(8,128)S(1)}, u32[]{:S(2)}, u32[]{:S(2)}) collective-permute-start(f32[4,2,16,384]{3,2,1,0:T(8,128)S(1)} %copy.144), channel_id=1, source_target_pairs={{0,8},{4,12},{8,0},{12,4},{16,24},{20,28},{24,16},{28,20},{32,40},... | collective-permute-start | bytes 589832 | tf_op jit(solution)/shard_map/ppermute | solution.py:21
  186.1 18.9 %all-to-all-start.1 = ((f32[32,2,16,128]{3,1,2,0:T(2,128)}), f32[32,2,16,128]{3,1,2,0:T(2,128)S(1)}, u32[]{:S(2)}, u32[]{:S(2)}) async-start(f32[32,2,16,128]{3,1,2,0:T(2,128)} %pad_maximum_fusion), calls=%async_computation.1 | async-start | bytes 1048576 | tf_op jit(solution)/shard_map/all_to_all | solution.py:218
  214.7 16.8 %collective-permute-start.40 = (f32[32,16,128]{2,0,1:T(8,128)}, f32[32,16,128]{2,0,1:T(8,128)S(1)}, u32[]{:S(2)}, u32[]{:S(2)}) collective-permute-start(f32[32,16,128]{2,0,1:T(8,128)} %pad_maximum_fusion.1), channel_id=1, source_target_pairs={{0,3},{1,0},{2,1},{3,2},{4,7},{5,4},{6,5},{7,6},{8,11},{9,8},{10,9... | collective-permute-start | bytes 786440 | tf_op jit(solution)/shard_map/ppermute | solution.py:29
  216.9 11.5 %all-to-all-start.3 = ((f32[16,12,128]{2,1,0:T(8,128)}), f32[16,12,128]{2,1,0:T(8,128)S(1)}, u32[]{:S(2)}, u32[]{:S(2)}) async-start(f32[16,12,128]{2,1,0:T(8,128)} %reshape.1125), calls=%async_computation.3 | async-start | bytes 262144 | tf_op jit(solution)/shard_map/all_to_all | solution.py:192
  220.5 11.1 %collective-permute-start.41 = (f32[32,16,128]{2,0,1:T(8,128)}, f32[32,16,128]{2,0,1:T(8,128)S(1)}, u32[]{:S(2)}, u32[]{:S(2)}) collective-permute-start(f32[32,16,128]{2,0,1:T(8,128)} %pad_maximum_fusion.1), channel_id=1, source_target_pairs={{0,2},{1,3},{2,0},{3,1},{4,6},{5,7},{6,4},{7,5},{8,10},{9,11},{10,... | collective-permute-start | bytes 786440 | tf_op jit(solution)/shard_map/ppermute | solution.py:29
  229.6 8.0 %collective-permute-start.42 = (f32[32,16,128]{2,0,1:T(8,128)}, f32[32,16,128]{2,0,1:T(8,128)S(1)}, u32[]{:S(2)}, u32[]{:S(2)}) collective-permute-start(f32[32,16,128]{2,0,1:T(8,128)} %pad_maximum_fusion.1), channel_id=1, source_target_pairs={{0,1},{1,2},{2,3},{3,0},{4,5},{5,6},{6,7},{7,4},{8,9},{9,10},{10,1... | collective-permute-start | bytes 786440 | tf_op jit(solution)/shard_map/ppermute | solution.py:29
  (35 other events, 368.7 us)

commit v2 on v0

v2 whole, which is shorter than its diff:
```python
import functools

import jax
import jax.numpy as jnp
from jax import lax
from jax.experimental import pallas as pl
from jax.experimental.pallas import tpu as pltpu
from jax.sharding import PartitionSpec as P

F32 = jnp.float32
BF16 = jnp.bfloat16
VMEM_LIMIT = 58 * 1024 * 1024

SWAP = [(0, 1), (1, 0)]


def device(h, y, x, z):
    return (h * 16 + y % 4 * 4 + x % 4) * 4 + z % 4


def stepper(axis):
    def step(v, d):
        pairs = []
        for h in range(2):
            by = d if h == 0 else -d
            move = [by if name == axis else 0 for name in "yxz"]
            for y in range(4):
                for x in range(4):
                    for z in range(4):
                        pairs.append((device(h, y, x, z), device(h, y + move[0], x + move[1], z + move[2])))
        return lax.ppermute(v, ("gx", "gy", "gz"), pairs)

    return step


shift_x, shift_y, shift_z = stepper("x"), stepper("y"), stepper("z")


def ahead(place, axis, d):
    return lax.rem(place[axis] + d * place[4], 4)


def split(v):
    high = v.astype(BF16)
    return high, (v - high.astype(F32)).astype(BF16)


def dot3(a_high, a_low, b_high, b_low, dims):
    dot = functools.partial(lax.dot_general, dimension_numbers=(dims, ((), ())), preferred_element_type=F32)
    return dot(a_high, b_high) + (dot(a_high, b_low) + dot(a_low, b_high))


def project_kernel(place, field, basis, own, other, land, x_land, x_high, x_low, sems):
    def load(k):
        part = pl.ds(k * 2, 2)
        return pltpu.make_async_copy(field.at[part], land.at[part], sems.at[k])

    x_load = pltpu.make_async_copy(basis, x_land, sems.at[6])
    x_load.start()
    for k in range(6):
        load(k).start()
    x_load.wait()
    turned = x_land[...].T
    for half in range(2):
        rows = pl.ds(pl.multiple_of((place[0] ^ half) * 128, 128), 128)
        x_high[rows, :], x_low[rows, :] = split(turned[half * 128 : half * 128 + 128])
    for k in range(6):
        load(k).wait()
        f_high, f_low = split(jnp.concatenate([land[2 * k], land[2 * k + 1]], axis=1))
        out = dot3(x_high[...], x_low[...], f_high, f_low, ((1,), (0,)))
        own[:, k * 256 : k * 256 + 256] = out[:128]
        other[:, k * 256 : k * 256 + 256] = out[128:]


def project(place, field, basis):
    out = jax.ShapeDtypeStruct((128, 1536), F32)
    return pl.pallas_call(
        project_kernel,
        in_specs=[pl.BlockSpec(memory_space=pltpu.SMEM)] + [pl.BlockSpec(memory_space=pl.ANY)] * 2,
        out_specs=[pl.BlockSpec(memory_space=pltpu.VMEM)] * 2,
        out_shape=[out, out],
        scratch_shapes=[
            pltpu.VMEM((12, 1024, 128), F32),
            pltpu.VMEM((1024, 256), F32),
            pltpu.VMEM((256, 1024), BF16),
            pltpu.VMEM((256, 1024), BF16),
            pltpu.SemaphoreType.DMA((7,)),
        ],
        compiler_params=pltpu.CompilerParams(vmem_limit_bytes=VMEM_LIMIT),
        cost_estimate=pl.CostEstimate(flops=2400000000, bytes_accessed=9000000, transcendentals=0),
        name="project",
    )(place, field, basis)


def send_out(place, buf, b, lane_of, g, refs, sems):
    a_refs, b_refs, c_refs = refs[0:4], refs[4:8], refs[8:12]
    dy = lax.rem((b - place[2] + 4) * place[4], 4)

    def piece(x, row, rows, third):
        row = pl.multiple_of(x * 64 + row, 16)
        return buf.at[pl.ds(row, rows), pl.ds(pl.multiple_of(lane_of(x) + third * 384, 128), 384)]

    wide, thin = pl.ds(g * 64, 64), pl.ds(g * 16, 16)
    for dx in range(4):
        x = ahead(place, 1, dx)
        pltpu.make_async_copy(piece(x, 0, 64, 0), a_refs[dx].at[b, wide], sems.at[dx]).start()
    for d in range(4):

        @pl.when(dy == d)
        def _():
            for x in range(4):
                pltpu.make_async_copy(piece(x, 0, 64, 1), b_refs[d].at[x, wide], sems.at[4 + d]).start()

        z = ahead(place, 3, d)
        for x in range(4):
            pltpu.make_async_copy(piece(x, z * 16, 16, 2), c_refs[d].at[b * 4 + x, thin], sems.at[8 + d]).start()


def wait_out(g, refs, sems):
    for i, ref in enumerate(refs):
        part = ref.at[:, pl.ds(g * 64, 64)] if i < 8 else ref.at[:, pl.ds(g * 16, 16)]
        pltpu.make_async_copy(part, part, sems.at[i]).wait()


def core_copies(place, buf, refs, sems):
    copies = []
    for d in range(4):
        for other in range(4):
            for half in range(2):
                rows = pl.ds(128 + half * 16, 16)
                q = pl.multiple_of((other * 4 + ahead(place, 1, d)) * 16, 16)
                src = buf.at[pl.ds(q, 16), pl.ds(half * 384, 384)]
                copies.append(pltpu.make_async_copy(src, refs[d].at[other, rows], sems.at[d]))
                q = pl.multiple_of((ahead(place, 2, d) * 4 + other) * 16, 16)
                src = buf.at[pl.ds(q, 16), pl.ds(768 + half * 384, 384)]
                copies.append(pltpu.make_async_copy(src, refs[4 + d].at[other, rows], sems.at[4 + d]))
    return copies


def gram_x_kernel(place, own, other, reduced, y_basis, *refs):
    high, low, buf, land, core, out_sems, sems, core_sems = refs[12:]

    def load(k):
        src = own if k < 6 else other
        part = pl.ds(k % 6 * 2, 2)
        return pltpu.make_async_copy(src.at[part], land.at[pl.ds(k * 2, 2)], sems.at[k])

    def prepare(half):
        for k in range(half * 6, half * 6 + 6):
            load(k).wait()
            for s in range(2):
                v_high, v_low = split(land[k * 2 + s])
                lane = (k % 6 * 2 + s) * 128
                high[half * 1024 : half * 1024 + 1024, lane : lane + 128] = v_high
                low[half * 1024 : half * 1024 + 1024, lane : lane + 128] = v_low

    def multiply(b, start, stop):
        rows, cols = slice(b * 256, b * 256 + 256), slice(start, stop)
        buf[b, :, start - b * 256 : stop - b * 256] = dot3(
            high[rows, :], low[rows, :], high[cols, :], low[cols, :], ((1,), (1,))
        )

    for k in range(12):
        load(k).start()
    y_high, y_low = split(y_basis[...].T)
    for s in range(12):
        r_high, r_low = split(reduced[:, s * 128 : s * 128 + 128])
        core[:, s * 128 : s * 128 + 128] = dot3(y_high, y_low, r_high, r_low, ((1,), (1,)))
    for copy in core_copies(place, core, refs, core_sems):
        copy.start()
    prepare(0)
    for b in range(4):
        multiply(b, b * 256, 1024)
    prepare(1)
    for b in range(4):
        multiply(b, 1024, b * 256 + 1280)
        send_out(place, buf.at[b], b, lambda x: (x // 2) * 128, 0, refs, out_sems)
    wait_out(0, refs[:12], out_sems)
    for i in range(8):
        part = refs[i].at[:, pl.ds(128, 32)]
        pltpu.make_async_copy(part, part, core_sems.at[i]).wait()


def gram_y_kernel(place, own, other, *refs):
    refs = refs[12:]
    high, low, buf, out_sems = refs[12:]
    for j in range(16):
        tiles = [src[j, :, s * 128 : s * 128 + 128] for src in (own, other) for s in range(12)]
        v = jnp.concatenate(tiles + [jnp.zeros((64, 128), F32)], axis=0).T
        v_high, v_low = split(v)
        for start in (j * 128, 2048 + j * 128):
            if start < 3072:
                high[start : start + 128, :] = v_high
                low[start : start + 128, :] = v_low
    h = place[0]
    for b in range(4):
        starts = [pl.multiple_of((b * 4 + x) * 128 + h * 64, 64) for x in range(4)]
        l_high = jnp.concatenate([high[pl.ds(r, 64), :] for r in starts], axis=0)
        l_low = jnp.concatenate([low[pl.ds(r, 64), :] for r in starts], axis=0)
        cols = slice(b * 512, b * 512 + 1536)
        buf[b] = dot3(l_high, l_low, high[cols, :], low[cols, :], ((1,), (1,)))
        send_out(place, buf.at[b], b, lambda x: x * 128, 1, refs, out_sems)
    wait_out(1, refs[:12], out_sems)


def gram_pieces(kernel, name, place, pieces, args, spaces, scratch, flops):
    ab = jax.ShapeDtypeStruct((4, 160, 384), F32)
    c = jax.ShapeDtypeStruct((16, 32, 384), F32)
    anywhere = pl.BlockSpec(memory_space=pl.ANY)
    return pl.pallas_call(
        kernel,
        in_specs=[pl.BlockSpec(memory_space=pltpu.SMEM)]
        + [pl.BlockSpec(memory_space=space) for space in spaces]
        + [anywhere] * len(pieces),
        out_specs=[anywhere] * 12,
        out_shape=[ab] * 8 + [c] * 4,
        scratch_shapes=scratch,
        input_output_aliases={1 + len(args) + i: i for i in range(len(pieces))},
        compiler_params=pltpu.CompilerParams(vmem_limit_bytes=VMEM_LIMIT),
        cost_estimate=pl.CostEstimate(flops=flops, bytes_accessed=20000000, transcendentals=0),
        name=name,
    )(place, *args, *pieces)


GRAM_X_SCRATCH = [
    pltpu.VMEM((2048, 1536), BF16),
    pltpu.VMEM((2048, 1536), BF16),
    pltpu.VMEM((4, 256, 1280), F32),
    pltpu.VMEM((24, 1024, 128), F32),
    pltpu.VMEM((256, 1536), F32),
    pltpu.SemaphoreType.DMA((12,)),
    pltpu.SemaphoreType.DMA((12,)),
    pltpu.SemaphoreType.DMA((8,)),
]
GRAM_Y_SCRATCH = [
    pltpu.VMEM((3072, 256), BF16),
    pltpu.VMEM((3072, 256), BF16),
    pltpu.VMEM((4, 256, 1536), F32),
    pltpu.SemaphoreType.DMA((12,)),
]


def sum4(terms, index):
    return (terms[0][index] + terms[1][index]) + (terms[2][index] + terms[3][index])


def sum_first_kernel(place, *refs):
    step = pl.program_id(0)
    a, b, c, outs = refs[0:4], refs[4:8], refs[8:12], refs[12:]
    total = sum4(a, 0)
    for d in range(4):

        @pl.when(step == d)
        def _():
            outs[d][...] = total

        z = ahead(place, 3, d)
        for g in range(2):
            rows = pl.ds(pl.multiple_of(g * 64 + z * 16, 16), 16)
            outs[4 + d][step, g * 16 : g * 16 + 16, :] = sum4(b, (0, rows, slice(None)))
        outs[8 + d][step] = sum4(c, ahead(place, 1, d))
    outs[12][step] = sum4(b, (0, slice(128, 160), slice(None)))


def sum_first(place, a, b, c):
    def whole(shape):
        return pl.BlockSpec(shape, lambda i, place: (0,) * len(shape))

    shapes = [(160, 384)] * 4 + [(4, 32, 384)] * 9
    return pl.pallas_call(
        sum_first_kernel,
        grid_spec=pltpu.PrefetchScalarGridSpec(
            num_scalar_prefetch=1,
            grid=(4,),
            in_specs=[pl.BlockSpec((1, 160, 384), lambda i, place: (ahead(place, 2, i), 0, 0))] * 4
            + [pl.BlockSpec((1, 160, 384), lambda i, place: (i, 0, 0))] * 4
            + [pl.BlockSpec((4, 32, 384), lambda i, place: (i, 0, 0))] * 4,
            out_specs=[whole(shape) for shape in shapes],
        ),
        out_shape=[jax.ShapeDtypeStruct(shape, F32) for shape in shapes],
        compiler_params=pltpu.CompilerParams(vmem_limit_bytes=VMEM_LIMIT),
        cost_estimate=pl.CostEstimate(flops=3000000, bytes_accessed=14000000, transcendentals=0),
        name="sum_first",
    )(place, *a, *b, *c)


def sum_second_kernel(place, *refs):
    a, b, c, b_core, outs = refs[0:4], refs[4:8], refs[8:12], refs[12], refs[13:]
    for d in range(4):
        for g in range(2):
            rows = pl.ds(pl.multiple_of(g * 64 + ahead(place, 3, d) * 16, 16), 16)
            outs[d][g * 16 : g * 16 + 16, :] = sum4(a, (rows, slice(None)))
        x = ahead(place, 1, d)
        outs[4 + d][:32, :] = sum4(b, x)
        outs[4 + d][32:, :] = b_core[x]
        outs[8 + d][...] = sum4(c, ahead(place, 2, d))
    outs[12][...] = sum4(a, (slice(128, 160), slice(None)))


def sum_last_kernel(place, *refs):
    a, b, c, a_core = refs[0:4], refs[4:8], refs[8:12], refs[12]
    slots, direct_x, keep, give, core, wide = refs[13:]
    h = place[0]
    j = place[2] * 4 + place[1]
    block_x = h * 8 + j // 2
    core[:32, :] = a_core[...]
    core[32:, :] = sum4(b, (slice(32, 64), slice(None)))
    parts = [sum4(t, (slice(0, 32), slice(None))) for t in (a, b, c)]
    zero = jnp.zeros((16, 128), F32)
    for k in range(16):
        lane = k % 3 * 128
        tile_x = parts[k // 3][:16, lane : lane + 128] if k < 9 else zero
        tile_y = parts[k // 3][16:, lane : lane + 128] if k < 9 else zero
        to_x, to_y = lax.rem(block_x + k, 16), lax.rem(j + k, 16)
        direct_x[to_x] = tile_x
        wide[lax.rem(to_y + 8 * h, 16)] = tile_y
        slots[2 * to_x, 0] = tile_x
        slots[2 * to_x + 1, 0] = tile_x
        slots[to_y, 1] = tile_y
        slots[16 + to_y, 1] = tile_y
    keep[...] = wide[:8]
    give[...] = wide[8:]


def select_kernel(place, got, direct_x, keep, come, out):
    h = place[0]
    j = place[2] * 4 + place[1]
    block_x = h * 8 + j // 2
    for block in range(16):
        first, second = got[2 * block, 0], got[2 * block + 1, 0]
        even = jnp.concatenate([first[:, :64], second[:, :64]], axis=1)
        odd = jnp.concatenate([first[:, 64:], second[:, 64:]], axis=1)
        turned = jnp.where(lax.rem(j, 2) == 0, even, odd)
        out[block] = jnp.where(lax.rem(block - block_x + 16, 16) <= 8, direct_x[block], turned)
    for block in range(8):
        is_direct = lax.rem(h * 8 + block - j + 16, 16) <= 8
        for half in range(2):
            direct = jnp.where(h == half, keep[block], come[block])
            out[16 + 2 * block + half] = jnp.where(is_direct, direct, got[half * 16 + h * 8 + block, 1])


def assemble_kernel(scale_x, scale_y, place, q0, q1, q2, q3, gram_x, gram_y, rows):
    h = place[0]
    j = place[2] * 4 + place[1]
    block_x = h * 8 + j // 2
    for d, quarter in enumerate((q0, q1, q2, q3)):
        z = ahead(place, 3, 4 - d)
        rows[:, pl.ds(pl.multiple_of(z * 16, 16), 16), :] = quarter[...]
    for block in range(16):
        direct = rows[block]
        turned = direct.T
        turned = jnp.concatenate([turned[:64], turned[64:]], axis=1)
        is_direct = lax.rem(block - block_x + 16, 16) <= 8
        gram_x[:, block * 128 : block * 128 + 128] = jnp.where(is_direct, direct, turned) * scale_x
    for block in range(8):
        direct = jnp.concatenate([rows[16 + 2 * block], rows[17 + 2 * block]], axis=0)
        is_direct = lax.rem(h * 8 + block - j + 16, 16) <= 8
        gram_y[:, block * 128 : block * 128 + 128] = jnp.where(is_direct, direct, direct.T) * scale_y


def small_kernel(kernel, name, out_shape, scratch, *args):
    return pl.pallas_call(
        kernel,
        in_specs=[pl.BlockSpec(memory_space=pltpu.SMEM)] + [pl.BlockSpec(memory_space=pltpu.VMEM)] * (len(args) - 1),
        out_shape=out_shape,
        scratch_shapes=scratch,
        compiler_params=pltpu.CompilerParams(vmem_limit_bytes=VMEM_LIMIT),
        name=name,
    )(*args)


def per_device(species_field, x_mode_basis, y_mode_basis):
    h, j, z0 = lax.axis_index("gx"), lax.axis_index("gy"), lax.axis_index("gz")
    x0, y0 = j % 4, j // 4
    place = jnp.stack([h, x0, y0, z0, 1 + 2 * h]).astype(jnp.int32)
    nx = 2 * species_field.shape[1]
    ny = 16 * species_field.shape[2]
    slices = 4 * species_field.shape[0]
    ranks = x_mode_basis.shape[1]

    other_field = lax.ppermute(species_field, "gx", SWAP)
    mine, theirs = project(place, species_field, x_mode_basis)
    reduced = mine + lax.ppermute(theirs, "gx", SWAP)
    fibers = lax.all_to_all(reduced.reshape(16, 8, 1536), "gy", 0, 0, tiled=True)

    pieces = gram_pieces(
        gram_x_kernel, "gram_x", place, [], (species_field, other_field, reduced, y_mode_basis),
        (pl.ANY, pl.ANY, pltpu.VMEM, pltpu.VMEM), GRAM_X_SCRATCH, 12000000000,
    )
    pieces, fibers = lax.optimization_barrier((pieces, fibers))
    other_fibers = lax.ppermute(fibers, "gx", SWAP)
    pieces = gram_pieces(
        gram_y_kernel, "gram_y", place, pieces, (fibers, other_fibers), (pltpu.VMEM, pltpu.VMEM), GRAM_Y_SCRATCH, 2400000000
    )

    def stage(a, b, c, shifts):
        def send(terms, d):
            return [shift(t, d) for shift, t in zip(shifts, terms)]

        near = [send([a[d], b[d], c[d]], d) for d in (1, 3)]
        far, near[0] = lax.optimization_barrier(([a[2], b[2], c[2]], near[0]))
        came = lax.optimization_barrier(near + [send(far, 2)])
        return [[own[0]] + [t[i] for t in came] for i, own in enumerate((a, b, c))]

    a, b, c = stage(pieces[0:4], pieces[4:8], pieces[8:12], (shift_x, shift_y, shift_z))
    *sums, b_core = sum_first(place, a, b, c)
    a, b, c = stage(sums[0:4], sums[4:8], sums[8:12], (shift_y, shift_z, shift_x))
    small, wide = jax.ShapeDtypeStruct((32, 384), F32), jax.ShapeDtypeStruct((64, 384), F32)
    *sums, a_core = small_kernel(
        sum_second_kernel, "sum_second", [small] * 4 + [wide] * 4 + [small] * 5, [], place, *a, *b, *c, b_core
    )
    a, b, c = stage(sums[0:4], sums[4:8], sums[8:12], (shift_z, shift_x, shift_y))
    blocks = jax.ShapeDtypeStruct((8, 16, 128), F32)
    slots, direct_x, keep, give, core = small_kernel(
        sum_last_kernel, "sum_last",
        [jax.ShapeDtypeStruct((32, 2, 16, 128), F32), jax.ShapeDtypeStruct((16, 16, 128), F32), blocks, blocks, wide],
        [pltpu.VMEM((16, 16, 128), F32)],
        place, *a, *b, *c, a_core,
    )
    core = core.reshape(2, 2, 16, 3, 128).transpose(4, 0, 1, 3, 2).reshape(128, 12, 16)

    got = lax.all_to_all(slots, ("gx", "gy"), 0, 0, tiled=True)
    come = lax.ppermute(give, "gx", SWAP)
    part = small_kernel(
        select_kernel, "select", jax.ShapeDtypeStruct((32, 16, 128), F32), [], place, got, direct_x, keep, come
    )
    quarters = [part] + [shift_z(part, d) for d in (1, 2, 3)]
    gram_x, gram_y = small_kernel(
        functools.partial(assemble_kernel, 1.0 / (ny * slices), 1.0 / (ranks * slices)),
        "assemble",
        [jax.ShapeDtypeStruct((64, nx), F32), jax.ShapeDtypeStruct((128, ny // 2), F32)],
        [pltpu.VMEM((32, 64, 128), F32)],
        place, *quarters,
    )
    return (gram_x, gram_y, core)


def solution(mesh):
    in_specs = (P("gz", "gx", "gy"), P("gx", None), P("gy", None))
    out_specs = (P(("gx", "gy"), None), P("gy", "gx"), P("gx", "gz", "gy"))
    return jax.shard_map(
        per_device, mesh=mesh, in_specs=in_specs, out_specs=out_specs, check_vma=False
    )
```

time: 306 us -> 211 us (0.69)
  waiting for transfers between devices: 205 us -> 72 us
  starting transfers between devices: 0.47 us -> 72.7 us
  matrix products: 64.7 us -> 0 us
  Pallas kernels: 0 us -> 55.1 us
  between operations: 15.5 us -> 0.96 us
  blocking collectives: 10.3 us -> 0 us
    reduce_scatter x4 -> x0, waiting for transfers between devices: 156 us -> none  [the longest x1 77.1 us: per_device(): lax.psum_scatter(core_term_list, 'gy', scatter_dimension=2, tiled=True)]
    dot_general x4 -> x0, matrix products: 64.7 us -> none  [the longest x1 42.8 us: per_device(): jnp.einsum('sxy,szy->xz', fibers, fibers, precision=exact_precision)]
    ppermute x0 -> x34, waiting for transfers between devices: none -> 61.6 us  [the longest x30 56.1 us: step(): return lax.ppermute(v, ('gx', 'gy', 'gz'), pairs)]
    ppermute x0 -> x34, starting transfers between devices: none -> 59.8 us  [the longest x30 58.6 us: step(): return lax.ppermute(v, ('gx', 'gy', 'gz'), pairs)]
    pallas_call x0 -> x8, Pallas kernels: none -> 55.1 us  [the longest x2 28.8 us: gram_pieces(): pl.pallas_call(kernel, in_specs=[pl.BlockSpec(memory_space=pltpu.SMEM)] +...]
    all_gather x1 -> x0, waiting for transfers between devices: 49.4 us -> none  [per_device(): lax.all_gather(reduced_result, 'gy', axis=2, tiled=True)]
    all_to_all x0 -> x2, starting transfers between devices: none -> 12.9 us  [the longest x1 7.32 us: per_device(): lax.all_to_all(reduced.reshape(16, 8, 1536), 'gy', 0, 0, tiled=True)]
    all_to_all x0 -> x2, waiting for transfers between devices: none -> 10.4 us  [the longest x1 10.4 us: per_device(): got = lax.all_to_all(slots, ('gx', 'gy'), 0, 0, tiled=True)]
  transfers between devices with their start and end apart: 6 -> 36, of which waited for: 5 -> 20; matrix products, arithmetic and copies ran while one was open for 20% -> 2% of each run, Pallas kernels for 0% -> 15%
where the time goes in v2:
time: 211 us; the launch traced here: 210 us
  starting transfers between devices  72.7 us (34%)
  waiting for transfers between devices  72 us (34%)
  Pallas kernels  55.1 us (26%)
  local copies, waits for them, and re-layouts  6.85 us (3%)
    ppermute x30, starting transfers between devices, step(): return lax.ppermute(v, ('gx', 'gy', 'gz'), pairs)  58.6 us
    ppermute x30, waiting for transfers between devices, step(): return lax.ppermute(v, ('gx', 'gy', 'gz'), pairs)  56.1 us
    pallas_call x2, Pallas kernels, gram_pieces(): pl.pallas_call(kernel, in_specs=[pl.BlockSpec(memory_space=pltpu.SMEM)] +...  28.8 us
    all_to_all x1, waiting for transfers between devices, per_device(): got = lax.all_to_all(slots, ('gx', 'gy'), 0, 0, tiled=True)  10.4 us
    pallas_call x4, Pallas kernels, small_kernel(): pl.pallas_call(kernel, in_specs=[pl.BlockSpec(memory_space=pltpu.SMEM)] +...  9.83 us
    pallas_call x1, Pallas kernels, project(): pl.pallas_call(project_kernel, in_specs=[pl.BlockSpec(memory_space=pltpu....  9.29 us
    all_to_all x1, starting transfers between devices, per_device(): lax.all_to_all(reduced.reshape(16, 8, 1536), 'gy', 0, 0, tiled=True)  7.32 us
    pallas_call x1, Pallas kernels, sum_first(): pl.pallas_call(sum_first_kernel, grid_spec=pltpu.PrefetchScalarGridSpec(n...  7.2 us
  transfers between devices with their start and end apart: 36, of which 20 were waited for; matrix products, arithmetic and copies ran while one was open for 2% of the time, Pallas kernels for 15%

profile of v2, /device:TPU:0, one launch (start us, length us, event | category | flops | bytes accessed | tf_op | source)
XLA Modules:
  0.0 209.8 jit_solution(14196023618275596078)
XLA Ops:
  1.4 9.3 %project.1 = (f32[128,1536]{1,0:T(8,128)}, f32[128,1536]{1,0:T(8,128)}) custom-call(s32[5]{0:T(128)} %stack.23.place, f32[12,1024,128]{2,1,0:T(8,128)} %own.1, f32[1024,256]{1,0:T(8,128)} %basis.1), custom_call_target="tpu_custom_call" | custom-call | flops 2400000000 | bytes 9000000 | tf_op jit(solution)/shard_map/project/pallas_call | solution.py:77
  11.2 2.1 %collective-permute-done.1 = f32[128,1536]{1,0:T(8,128)S(1)} collective-permute-done((f32[128,1536]{1,0:T(8,128)}, f32[128,1536]{1,0:T(8,128)S(1)}, u32[]{:S(2)}, u32[]{:S(2)}) %collective-permute-start.1) | collective-permute-done | bytes 786464 | tf_op jit(solution)/shard_map/ppermute | solution.py:383
  13.3 2.1 %add.9.reduced = f32[128,1536]{1,0:T(8,128)} add(f32[128,1536]{1,0:T(8,128)} %get-tuple-element.120, f32[128,1536]{1,0:T(8,128)S(1)} %collective-permute-done.1) | non-fusion elementwise | flops 196608 | bytes 2359296 | tf_op jit(solution)/shard_map/add | solution.py:383
  15.4 7.3 %all-to-all-start = ((f32[16,8,1536]{2,1,0:T(8,128)}), f32[16,8,1536]{2,1,0:T(8,128)S(1)}, u32[]{:S(2)}, u32[]{:S(2)}) async-start(f32[16,8,1536]{2,1,0:T(8,128)} %bitcast.5), calls=%async_computation | async-start | bytes 1572864 | tf_op jit(solution)/shard_map/all_to_all | solution.py:384
  22.8 23.0 %gram_x.1 = (f32[4,160,384]{2,1,0:T(8,128)}, f32[4,160,384]{2,1,0:T(8,128)}, f32[4,160,384]{2,1,0:T(8,128)}, f32[4,160,384]{2,1,0:T(8,128)}, f32[4,160,384]{2,1,...) custom-call(s32[5]{0:T(128)} %stack.23.place, ...), custom_call_target="tpu_custom_call" | custom-call | flops 12000000000 | bytes 20000000 | tf_op jit(solution)/shard_map/gram_x/pallas_call | solution.py:210
  46.0 2.2 %collective-permute-done.2.other = f32[16,8,1536]{2,1,0:T(8,128)S(1)} collective-permute-done((f32[16,8,1536]{2,1,0:T(8,128)S(1)}, f32[16,8,1536]{2,1,0:T(8,128)S(1)}, u32[]{:S(2)}, u32[]{:S(2)}) %collective-permute-start.2) | collective-permute-done | bytes 786464 | tf_op jit(solution)/shard_map/ppermute | solution.py:391
  49.1 5.8 %gram_y.1 = (f32[4,160,384]{2,1,0:T(8,128)}, f32[4,160,384]{2,1,0:T(8,128)}, f32[4,160,384]{2,1,0:T(8,128)}, f32[4,160,384]{2,1,0:T(8,128)}, f32[4,160,384]{2,1,...) custom-call(s32[5]{0:T(128)} %stack.23.place, ...), custom_call_target="tpu_custom_call", output_to_operand_aliasing={{0}: (3, {}), {1}: (4, {}), {2}: (5, {}), {3}: (6, {}), {4}... | custom-call | flops 2400000000 | bytes 20000000 | tf_op jit(solution)/shard_map/gram_y/pallas_call | solution.py:210
  60.1 2.1 %collective-permute-start.8 = (f32[16,32,384]{2,1,0:T(8,128)}, f32[16,32,384]{2,1,0:T(8,128)S(1)}, u32[]{:S(2)}, u32[]{:S(2)}) collective-permute-start(f32[16,32,384]{2,1,0:T(8,128)} %get-tuple-element.159), channel_id=1, source_target_pairs={{0,3},{1,0},{2,1},{3,2},{4,7},{5,4},{6,5},{7,6},{8,11},{9,8},{10,9... | collective-permute-start | bytes 2359304 | tf_op jit(solution)/shard_map/ppermute | solution.py:31
  64.0 12.8 %collective-permute-done.5.refs_9_ = f32[16,32,384]{2,1,0:T(8,128)S(1)} collective-permute-done((f32[16,32,384]{2,1,0:T(8,128)}, f32[16,32,384]{2,1,0:T(8,128)S(1)}, u32[]{:S(2)}, u32[]{:S(2)}) %collective-permute-start.5) | collective-permute-done | bytes 786464 | tf_op jit(solution)/shard_map/ppermute | solution.py:31
  76.8 2.6 %collective-permute-start.7 = (f32[4,160,384]{2,1,0:T(8,128)}, f32[4,160,384]{2,1,0:T(8,128)S(1)}, u32[]{:S(2)}, u32[]{:S(2)}) collective-permute-start(f32[4,160,384]{2,1,0:T(8,128)} %get-tuple-element.158), channel_id=1, source_target_pairs={{0,48},{1,49},{2,50},{3,51},{4,52},{5,53},{6,54},{7,55},{8,56},{9,... | collective-permute-start | bytes 2949128 | tf_op jit(solution)/shard_map/ppermute | solution.py:31
  79.4 4.6 %collective-permute-start.9 = (f32[4,160,384]{2,1,0:T(8,128)}, f32[4,160,384]{2,1,0:T(8,128)S(1)}, u32[]{:S(2)}, u32[]{:S(2)}) collective-permute-start(f32[4,160,384]{2,1,0:T(8,128)} %get-tuple-element.160), channel_id=1, source_target_pairs={{0,8},{1,9},{2,10},{3,11},{4,12},{5,13},{6,14},{7,15},{8,0},{9,1},... | collective-permute-start | bytes 2949128 | tf_op jit(solution)/shard_map/ppermute | solution.py:31
  84.0 3.1 %collective-permute-start.10 = (f32[4,160,384]{2,1,0:T(8,128)}, f32[4,160,384]{2,1,0:T(8,128)S(1)}, u32[]{:S(2)}, u32[]{:S(2)}) collective-permute-start(f32[4,160,384]{2,1,0:T(8,128)} %get-tuple-element.161), channel_id=1, source_target_pairs={{0,32},{1,33},{2,34},{3,35},{4,36},{5,37},{6,38},{7,39},{8,40},{9,... | collective-permute-start | bytes 2949128 | tf_op jit(solution)/shard_map/ppermute | solution.py:31
  88.8 10.4 %collective-permute-done.7.refs_6_ = f32[4,160,384]{2,1,0:T(8,128)S(1)} collective-permute-done((f32[4,160,384]{2,1,0:T(8,128)}, f32[4,160,384]{2,1,0:T(8,128)S(1)}, u32[]{:S(2)}, u32[]{:S(2)}) %collective-permute-start.7) | collective-permute-done | bytes 983072 | tf_op jit(solution)/shard_map/ppermute | solution.py:31
  99.3 5.3 %collective-permute-done.11.refs_11_ = f32[16,32,384]{2,1,0:T(8,128)S(1)} collective-permute-done((f32[16,32,384]{2,1,0:T(8,128)}, f32[16,32,384]{2,1,0:T(8,128)S(1)}, u32[]{:S(2)}, u32[]{:S(2)}) %collective-permute-start.11) | collective-permute-done | bytes 786464 | tf_op jit(solution)/shard_map/ppermute | solution.py:31
  106.1 4.4 %collective-permute-done.10.refs_7_ = f32[4,160,384]{2,1,0:T(8,128)S(1)} collective-permute-done((f32[4,160,384]{2,1,0:T(8,128)}, f32[4,160,384]{2,1,0:T(8,128)S(1)}, u32[]{:S(2)}, u32[]{:S(2)}) %collective-permute-start.10) | collective-permute-done | bytes 983072 | tf_op jit(solution)/shard_map/ppermute | solution.py:31
  111.4 7.2 %sum_first.1 = (f32[160,384]{1,0:T(8,128)}, f32[160,384]{1,0:T(8,128)}, f32[160,384]{1,0:T(8,128)}, f32[160,384]{1,0:T(8,128)}, f32[4,32,384]{2,1,0:T(8,128)}, /...) custom-call(s32[5]{0:T(128)} %stack.23.place, ...), custom_call_target="tpu_custom_call" | custom-call | flops 3000000 | bytes 14000000 | tf_op jit(solution)/shard_map/sum_first/pallas_call | solution.py:270
  118.7 5.6 %collective-permute-start.12 = (f32[160,384]{1,0:T(8,128)}, f32[160,384]{1,0:T(8,128)S(1)}, u32[]{:S(2)}, u32[]{:S(2)}) collective-permute-start(f32[160,384]{1,0:T(8,128)} %get-tuple-element.178), channel_id=1, source_target_pairs={{0,16},{1,17},{2,18},{3,19},{4,20},{5,21},{6,22},{7,23},{8,24},{9,... | collective-permute-start | bytes 737288 | tf_op jit(solution)/shard_map/ppermute | solution.py:31
  125.2 2.6 %collective-permute-start.14 = (f32[4,32,384]{2,1,0:T(8,128)}, f32[4,32,384]{2,1,0:T(8,128)S(1)}, u32[]{:S(2)}, u32[]{:S(2)}) collective-permute-start(f32[4,32,384]{2,1,0:T(8,128)} %get-tuple-element.180), channel_id=1, source_target_pairs={{0,4},{1,5},{2,6},{3,7},{4,8},{5,9},{6,10},{7,11},{8,12},{9,13},{1... | collective-permute-start | bytes 589832 | tf_op jit(solution)/shard_map/ppermute | solution.py:31
  127.8 3.2 %collective-permute-start.16 = (f32[4,32,384]{2,1,0:T(8,128)}, f32[4,32,384]{2,1,0:T(8,128)S(1)}, u32[]{:S(2)}, u32[]{:S(2)}) collective-permute-start(f32[4,32,384]{2,1,0:T(8,128)} %get-tuple-element.185), channel_id=1, source_target_pairs={{0,3},{1,0},{2,1},{3,2},{4,7},{5,4},{6,5},{7,6},{8,11},{9,8},{10,9... | collective-permute-start | bytes 589832 | tf_op jit(solution)/shard_map/ppermute | solution.py:31
  132.3 5.0 %collective-permute-start.18 = (f32[160,384]{1,0:T(8,128)}, f32[160,384]{1,0:T(8,128)S(1)}, u32[]{:S(2)}, u32[]{:S(2)}) collective-permute-start(f32[160,384]{1,0:T(8,128)} %get-tuple-element.187), channel_id=1, source_target_pairs={{0,32},{1,33},{2,34},{3,35},{4,36},{5,37},{6,38},{7,39},{8,40},{9,... | collective-permute-start | bytes 737288 | tf_op jit(solution)/shard_map/ppermute | solution.py:31
  141.1 2.1 collective-permute-done.17.refs_10_
  143.2 2.3 %collective-permute-done.19.refs_7_ = f32[4,32,384]{2,1,0:T(8,128)S(1)} collective-permute-done((f32[4,32,384]{2,1,0:T(8,128)}, f32[4,32,384]{2,1,0:T(8,128)S(1)}, u32[]{:S(2)}, u32[]{:S(2)}) %collective-permute-start.19) | collective-permute-done | bytes 196640 | tf_op jit(solution)/shard_map/ppermute | solution.py:31
  148.3 2.9 %sum_second.1 = (f32[32,384]{1,0:T(8,128)}, f32[32,384]{1,0:T(8,128)}, f32[32,384]{1,0:T(8,128)}, f32[32,384]{1,0:T(8,128)}, f32[64,384]{1,0:T(8,128)}, /*index=...) custom-call(s32[5]{0:T(128)} %stack.23.place, ...), custom_call_target="tpu_custom_call" | custom-call | tf_op jit(solution)/shard_map/sum_second/pallas_call | solution.py:362
  153.5 3.0 %collective-permute-start.24 = (f32[32,384]{1,0:T(8,128)}, f32[32,384]{1,0:T(8,128)S(1)}, u32[]{:S(2)}, u32[]{:S(2)}) collective-permute-start(f32[32,384]{1,0:T(8,128)} %get-tuple-element.212), channel_id=1, source_target_pairs={{0,3},{1,0},{2,1},{3,2},{4,7},{5,4},{6,5},{7,6},{8,11},{9,8},{10,9... | collective-permute-start | bytes 147464 | tf_op jit(solution)/shard_map/ppermute | solution.py:31
  164.8 3.0 %collective-permute-done.27.refs_3_ = f32[32,384]{1,0:T(8,128)S(1)} collective-permute-done((f32[32,384]{1,0:T(8,128)}, f32[32,384]{1,0:T(8,128)S(1)}, u32[]{:S(2)}, u32[]{:S(2)}) %collective-permute-start.27) | collective-permute-done | bytes 49184 | tf_op jit(solution)/shard_map/ppermute | solution.py:31
  169.1 2.2 %sum_last.1 = (f32[32,2,16,128]{3,2,1,0:T(8,128)}, f32[16,16,128]{2,1,0:T(8,128)}, f32[8,16,128]{2,1,0:T(8,128)}, f32[8,16,128]{2,1,0:T(8,128)}, f32[64,384]{1,0:T(8,128)}) custom-call(s32[5]{0:T(128)} %stack.23.place, f32[32,384]{1,0:T(8,128)} %get-tuple-element.202.refs_0_, f32[32,384]{1,0:T(8,128)} %copy-done.28, f32[32,384]{1,0:T(8,128)} %copy-done.30, ...), custom_call_target="tpu_custom_call" | custom-call | tf_op jit(solution)/shard_map/sum_last/pallas_call | solution.py:362
  171.2 5.6 %all-to-all-start.1 = ((f32[32,2,16,128]{3,2,1,0:T(8,128)}), f32[32,2,16,128]{3,2,1,0:T(8,128)S(1)}, u32[]{:S(2)}, u32[]{:S(2)}) async-start(f32[32,2,16,128]{3,2,1,0:T(8,128)} %get-tuple-element.230), calls=%async_computation.1 | async-start | bytes 1048576 | tf_op jit(solution)/shard_map/all_to_all | solution.py:422
  178.4 10.4 %all-to-all-done.1.got = f32[32,2,16,128]{3,2,1,0:T(8,128)S(1)} async-done(((f32[32,2,16,128]{3,2,1,0:T(8,128)}), f32[32,2,16,128]{3,2,1,0:T(8,128)S(1)}, u32[]{:S(2)}, u32[]{:S(2)}) %all-to-all-start.1) | async-done | bytes 524320 | tf_op jit(solution)/shard_map/all_to_all | solution.py:422
  192.3 2.8 %collective-permute-start.32 = (f32[32,16,128]{2,1,0:T(8,128)}, f32[32,16,128]{2,1,0:T(8,128)S(1)}, u32[]{:S(2)}, u32[]{:S(2)}) collective-permute-start(f32[32,16,128]{2,1,0:T(8,128)} %select.7.q0), channel_id=1, source_target_pairs={{0,2},{1,3},{2,0},{3,1},{4,6},{5,7},{6,4},{7,5},{8,10},{9,11},{10,... | collective-permute-start | bytes 786440 | tf_op jit(solution)/shard_map/ppermute | solution.py:31
  196.7 4.4 %collective-permute-done.33.q3 = f32[32,16,128]{2,1,0:T(8,128)S(1)} collective-permute-done((f32[32,16,128]{2,1,0:T(8,128)}, f32[32,16,128]{2,1,0:T(8,128)S(1)}, u32[]{:S(2)}, u32[]{:S(2)}) %collective-permute-start.33) | collective-permute-done | bytes 262176 | tf_op jit(solution)/shard_map/ppermute | solution.py:31
  202.5 3.8 %collective-permute-done.31.q1 = f32[32,16,128]{2,1,0:T(8,128)S(1)} collective-permute-done((f32[32,16,128]{2,1,0:T(8,128)}, f32[32,16,128]{2,1,0:T(8,128)S(1)}, u32[]{:S(2)}, u32[]{:S(2)}) %collective-permute-start.31) | collective-permute-done | bytes 262176 | tf_op jit(solution)/shard_map/ppermute | solution.py:31
  207.0 2.8 %assemble.1 = (f32[64,2048]{1,0:T(8,128)}, f32[128,1024]{1,0:T(8,128)}) custom-call(s32[5]{0:T(128)} %stack.23.place, f32[32,16,128]{2,1,0:T(8,128)} %select.7.q0, f32[32,16,128]{2,1,0:T(8,128)} %copy-done.14, f32[32,16,128]{2,1,0:T(8,128)} %copy-done.13, f32[32,16,128]{2,1,0:T(8,128)} %copy-done.12), custom_call_target="tpu_custom_call" | custom-call | tf_op jit(solution)/shard_map/assemble/pallas_call | solution.py:362
  (120 shorter events, 42.5 us)
Async XLA Ops:
  0.6 22.1 %collective-permute-start = (f32[12,1024,128]{2,1,0:T(8,128)}, f32[12,1024,128]{2,1,0:T(8,128)}, u32[]{:S(2)}, u32[]{:S(2)}) collective-permute-start(f32[12,1024,128]{2,1,0:T(8,128)} %own.1), channel_id=1, source_target_pairs={{0,64},{64,0},{1,65},{65,1},{2,66},{66,2},{3,67},{67,3},{4,68},{68... | collective-permute-start | bytes 18874376 | tf_op jit(solution)/shard_map/ppermute | solution.py:381
  15.4 30.4 %all-to-all-start = ((f32[16,8,1536]{2,1,0:T(8,128)}), f32[16,8,1536]{2,1,0:T(8,128)S(1)}, u32[]{:S(2)}, u32[]{:S(2)}) async-start(f32[16,8,1536]{2,1,0:T(8,128)} %bitcast.5), calls=%async_computation | async-start | bytes 1572864 | tf_op jit(solution)/shard_map/all_to_all | solution.py:384
  54.9 24.5 %collective-permute-start.3 = (f32[4,160,384]{2,1,0:T(8,128)}, f32[4,160,384]{2,1,0:T(8,128)S(1)}, u32[]{:S(2)}, u32[]{:S(2)}) collective-permute-start(f32[4,160,384]{2,1,0:T(8,128)} %get-tuple-element.151), channel_id=1, source_target_pairs={{0,4},{1,5},{2,6},{3,7},{4,8},{5,9},{6,10},{7,11},{8,12},{9,13},{1... | collective-permute-start | bytes 2949128 | tf_op jit(solution)/shard_map/ppermute | solution.py:31
  56.7 22.7 %collective-permute-start.4 = (f32[4,160,384]{2,1,0:T(8,128)}, f32[4,160,384]{2,1,0:T(8,128)S(1)}, u32[]{:S(2)}, u32[]{:S(2)}) collective-permute-start(f32[4,160,384]{2,1,0:T(8,128)} %get-tuple-element.152), channel_id=1, source_target_pairs={{0,16},{1,17},{2,18},{3,19},{4,20},{5,21},{6,22},{7,23},{8,24},{9,... | collective-permute-start | bytes 2949128 | tf_op jit(solution)/shard_map/ppermute | solution.py:31
  58.2 18.6 %collective-permute-start.5 = (f32[16,32,384]{2,1,0:T(8,128)}, f32[16,32,384]{2,1,0:T(8,128)S(1)}, u32[]{:S(2)}, u32[]{:S(2)}) collective-permute-start(f32[16,32,384]{2,1,0:T(8,128)} %get-tuple-element.153), channel_id=1, source_target_pairs={{0,1},{1,2},{2,3},{3,0},{4,5},{5,6},{6,7},{7,4},{8,9},{9,10},{10,1... | collective-permute-start | bytes 2359304 | tf_op jit(solution)/shard_map/ppermute | solution.py:31
  60.1 27.0 %collective-permute-start.8 = (f32[16,32,384]{2,1,0:T(8,128)}, f32[16,32,384]{2,1,0:T(8,128)S(1)}, u32[]{:S(2)}, u32[]{:S(2)}) collective-permute-start(f32[16,32,384]{2,1,0:T(8,128)} %get-tuple-element.159), channel_id=1, source_target_pairs={{0,3},{1,0},{2,1},{3,2},{4,7},{5,4},{6,5},{7,6},{8,11},{9,8},{10,9... | collective-permute-start | bytes 2359304 | tf_op jit(solution)/shard_map/ppermute | solution.py:31
  62.2 26.6 %collective-permute-start.6 = (f32[4,160,384]{2,1,0:T(8,128)}, f32[4,160,384]{2,1,0:T(8,128)S(1)}, u32[]{:S(2)}, u32[]{:S(2)}) collective-permute-start(f32[4,160,384]{2,1,0:T(8,128)} %get-tuple-element.157), channel_id=1, source_target_pairs={{0,12},{1,13},{2,14},{3,15},{4,0},{5,1},{6,2},{7,3},{8,4},{9,5},{1... | collective-permute-start | bytes 2949128 | tf_op jit(solution)/shard_map/ppermute | solution.py:31
  76.8 22.4 %collective-permute-start.7 = (f32[4,160,384]{2,1,0:T(8,128)}, f32[4,160,384]{2,1,0:T(8,128)S(1)}, u32[]{:S(2)}, u32[]{:S(2)}) collective-permute-start(f32[4,160,384]{2,1,0:T(8,128)} %get-tuple-element.158), channel_id=1, source_target_pairs={{0,48},{1,49},{2,50},{3,51},{4,52},{5,53},{6,54},{7,55},{8,56},{9,... | collective-permute-start | bytes 2949128 | tf_op jit(solution)/shard_map/ppermute | solution.py:31
  79.4 26.7 %collective-permute-start.9 = (f32[4,160,384]{2,1,0:T(8,128)}, f32[4,160,384]{2,1,0:T(8,128)S(1)}, u32[]{:S(2)}, u32[]{:S(2)}) collective-permute-start(f32[4,160,384]{2,1,0:T(8,128)} %get-tuple-element.160), channel_id=1, source_target_pairs={{0,8},{1,9},{2,10},{3,11},{4,12},{5,13},{6,14},{7,15},{8,0},{9,1},... | collective-permute-start | bytes 2949128 | tf_op jit(solution)/shard_map/ppermute | solution.py:31
  84.0 26.4 %collective-permute-start.10 = (f32[4,160,384]{2,1,0:T(8,128)}, f32[4,160,384]{2,1,0:T(8,128)S(1)}, u32[]{:S(2)}, u32[]{:S(2)}) collective-permute-start(f32[4,160,384]{2,1,0:T(8,128)} %get-tuple-element.161), channel_id=1, source_target_pairs={{0,32},{1,33},{2,34},{3,35},{4,36},{5,37},{6,38},{7,39},{8,40},{9,... | collective-permute-start | bytes 2949128 | tf_op jit(solution)/shard_map/ppermute | solution.py:31
  87.2 17.4 %collective-permute-start.11 = (f32[16,32,384]{2,1,0:T(8,128)}, f32[16,32,384]{2,1,0:T(8,128)S(1)}, u32[]{:S(2)}, u32[]{:S(2)}) collective-permute-start(f32[16,32,384]{2,1,0:T(8,128)} %get-tuple-element.162), channel_id=1, source_target_pairs={{0,2},{1,3},{2,0},{3,1},{4,6},{5,7},{6,4},{7,5},{8,10},{9,11},{10,... | collective-permute-start | bytes 2359304 | tf_op jit(solution)/shard_map/ppermute | solution.py:31
  118.7 13.6 %collective-permute-start.12 = (f32[160,384]{1,0:T(8,128)}, f32[160,384]{1,0:T(8,128)S(1)}, u32[]{:S(2)}, u32[]{:S(2)}) collective-permute-start(f32[160,384]{1,0:T(8,128)} %get-tuple-element.178), channel_id=1, source_target_pairs={{0,16},{1,17},{2,18},{3,19},{4,20},{5,21},{6,22},{7,23},{8,24},{9,... | collective-permute-start | bytes 737288 | tf_op jit(solution)/shard_map/ppermute | solution.py:31
  124.3 7.9 %collective-permute-start.13 = (f32[4,32,384]{2,1,0:T(8,128)}, f32[4,32,384]{2,1,0:T(8,128)S(1)}, u32[]{:S(2)}, u32[]{:S(2)}) collective-permute-start(f32[4,32,384]{2,1,0:T(8,128)} %get-tuple-element.179), channel_id=1, source_target_pairs={{0,1},{1,2},{2,3},{3,0},{4,5},{5,6},{6,7},{7,4},{8,9},{9,10},{10,1... | collective-permute-start | bytes 589832 | tf_op jit(solution)/shard_map/ppermute | solution.py:31
  125.2 7.1 %collective-permute-start.14 = (f32[4,32,384]{2,1,0:T(8,128)}, f32[4,32,384]{2,1,0:T(8,128)S(1)}, u32[]{:S(2)}, u32[]{:S(2)}) collective-permute-start(f32[4,32,384]{2,1,0:T(8,128)} %get-tuple-element.180), channel_id=1, source_target_pairs={{0,4},{1,5},{2,6},{3,7},{4,8},{5,9},{6,10},{7,11},{8,12},{9,13},{1... | collective-permute-start | bytes 589832 | tf_op jit(solution)/shard_map/ppermute | solution.py:31
  127.8 12.4 %collective-permute-start.16 = (f32[4,32,384]{2,1,0:T(8,128)}, f32[4,32,384]{2,1,0:T(8,128)S(1)}, u32[]{:S(2)}, u32[]{:S(2)}) collective-permute-start(f32[4,32,384]{2,1,0:T(8,128)} %get-tuple-element.185), channel_id=1, source_target_pairs={{0,3},{1,0},{2,1},{3,2},{4,7},{5,4},{6,5},{7,6},{8,11},{9,8},{10,9... | collective-permute-start | bytes 589832 | tf_op jit(solution)/shard_map/ppermute | solution.py:31
  131.0 12.1 %collective-permute-start.15 = (f32[160,384]{1,0:T(8,128)}, f32[160,384]{1,0:T(8,128)S(1)}, u32[]{:S(2)}, u32[]{:S(2)}) collective-permute-start(f32[160,384]{1,0:T(8,128)} %get-tuple-element.184), channel_id=1, source_target_pairs={{0,48},{1,49},{2,50},{3,51},{4,52},{5,53},{6,54},{7,55},{8,56},{9,... | collective-permute-start | bytes 737288 | tf_op jit(solution)/shard_map/ppermute | solution.py:31
  132.3 15.3 %collective-permute-start.18 = (f32[160,384]{1,0:T(8,128)}, f32[160,384]{1,0:T(8,128)S(1)}, u32[]{:S(2)}, u32[]{:S(2)}) collective-permute-start(f32[160,384]{1,0:T(8,128)} %get-tuple-element.187), channel_id=1, source_target_pairs={{0,32},{1,33},{2,34},{3,35},{4,36},{5,37},{6,38},{7,39},{8,40},{9,... | collective-permute-start | bytes 737288 | tf_op jit(solution)/shard_map/ppermute | solution.py:31
  137.3 5.9 %collective-permute-start.17 = (f32[4,32,384]{2,1,0:T(8,128)}, f32[4,32,384]{2,1,0:T(8,128)S(1)}, u32[]{:S(2)}, u32[]{:S(2)}) collective-permute-start(f32[4,32,384]{2,1,0:T(8,128)} %get-tuple-element.186), channel_id=1, source_target_pairs={{0,12},{1,13},{2,14},{3,15},{4,0},{5,1},{6,2},{7,3},{8,4},{9,5},{1... | collective-permute-start | bytes 589832 | tf_op jit(solution)/shard_map/ppermute | solution.py:31
  138.1 7.4 %collective-permute-start.19 = (f32[4,32,384]{2,1,0:T(8,128)}, f32[4,32,384]{2,1,0:T(8,128)S(1)}, u32[]{:S(2)}, u32[]{:S(2)}) collective-permute-start(f32[4,32,384]{2,1,0:T(8,128)} %get-tuple-element.188), channel_id=1, source_target_pairs={{0,2},{1,3},{2,0},{3,1},{4,6},{5,7},{6,4},{7,5},{8,10},{9,11},{10,... | collective-permute-start | bytes 589832 | tf_op jit(solution)/shard_map/ppermute | solution.py:31
  140.2 7.4 %collective-permute-start.20 = (f32[4,32,384]{2,1,0:T(8,128)}, f32[4,32,384]{2,1,0:T(8,128)S(1)}, u32[]{:S(2)}, u32[]{:S(2)}) collective-permute-start(f32[4,32,384]{2,1,0:T(8,128)} %get-tuple-element.189), channel_id=1, source_target_pairs={{0,8},{1,9},{2,10},{3,11},{4,12},{5,13},{6,14},{7,15},{8,0},{9,1},... | collective-permute-start | bytes 589832 | tf_op jit(solution)/shard_map/ppermute | solution.py:31
  151.2 7.8 %collective-permute-start.22 = (f32[64,384]{1,0:T(8,128)}, f32[64,384]{1,0:T(8,128)S(1)}, u32[]{:S(2)}, u32[]{:S(2)}) collective-permute-start(f32[64,384]{1,0:T(8,128)} %get-tuple-element.207), channel_id=1, source_target_pairs={{0,4},{1,5},{2,6},{3,7},{4,8},{5,9},{6,10},{7,11},{8,12},{9,13},{1... | collective-permute-start | bytes 294920 | tf_op jit(solution)/shard_map/ppermute | solution.py:31
  153.3 5.7 %collective-permute-start.21 = (f32[32,384]{1,0:T(8,128)}, f32[32,384]{1,0:T(8,128)S(1)}, u32[]{:S(2)}, u32[]{:S(2)}) collective-permute-start(f32[32,384]{1,0:T(8,128)} %get-tuple-element.206), channel_id=1, source_target_pairs={{0,1},{1,2},{2,3},{3,0},{4,5},{5,6},{6,7},{7,4},{8,9},{9,10},{10,1... | collective-permute-start | bytes 147464 | tf_op jit(solution)/shard_map/ppermute | solution.py:31
  153.3 5.7 %collective-permute-start.23 = (f32[32,384]{1,0:T(8,128)}, f32[32,384]{1,0:T(8,128)S(1)}, u32[]{:S(2)}, u32[]{:S(2)}) collective-permute-start(f32[32,384]{1,0:T(8,128)} %get-tuple-element.208), channel_id=1, source_target_pairs={{0,16},{1,17},{2,18},{3,19},{4,20},{5,21},{6,22},{7,23},{8,24},{9,... | collective-permute-start | bytes 147464 | tf_op jit(solution)/shard_map/ppermute | solution.py:31
  153.5 9.1 %collective-permute-start.24 = (f32[32,384]{1,0:T(8,128)}, f32[32,384]{1,0:T(8,128)S(1)}, u32[]{:S(2)}, u32[]{:S(2)}) collective-permute-start(f32[32,384]{1,0:T(8,128)} %get-tuple-element.212), channel_id=1, source_target_pairs={{0,3},{1,0},{2,1},{3,2},{4,7},{5,4},{6,5},{7,6},{8,11},{9,8},{10,9... | collective-permute-start | bytes 147464 | tf_op jit(solution)/shard_map/ppermute | solution.py:31
  156.5 8.3 %collective-permute-start.25 = (f32[64,384]{1,0:T(8,128)}, f32[64,384]{1,0:T(8,128)S(1)}, u32[]{:S(2)}, u32[]{:S(2)}) collective-permute-start(f32[64,384]{1,0:T(8,128)} %get-tuple-element.213), channel_id=1, source_target_pairs={{0,12},{1,13},{2,14},{3,15},{4,0},{5,1},{6,2},{7,3},{8,4},{9,5},{1... | collective-permute-start | bytes 294920 | tf_op jit(solution)/shard_map/ppermute | solution.py:31
  159.0 9.4 %collective-permute-start.28 = (f32[64,384]{1,0:T(8,128)}, f32[64,384]{1,0:T(8,128)S(1)}, u32[]{:S(2)}, u32[]{:S(2)}) collective-permute-start(f32[64,384]{1,0:T(8,128)} %get-tuple-element.216), channel_id=1, source_target_pairs={{0,8},{1,9},{2,10},{3,11},{4,12},{5,13},{6,14},{7,15},{8,0},{9,1},... | collective-permute-start | bytes 294920 | tf_op jit(solution)/shard_map/ppermute | solution.py:31
  162.0 5.8 %collective-permute-start.27 = (f32[32,384]{1,0:T(8,128)}, f32[32,384]{1,0:T(8,128)S(1)}, u32[]{:S(2)}, u32[]{:S(2)}) collective-permute-start(f32[32,384]{1,0:T(8,128)} %get-tuple-element.215), channel_id=1, source_target_pairs={{0,2},{1,3},{2,0},{3,1},{4,6},{5,7},{6,4},{7,5},{8,10},{9,11},{10,... | collective-permute-start | bytes 147464 | tf_op jit(solution)/shard_map/ppermute | solution.py:31
  162.6 5.8 %collective-permute-start.29 = (f32[32,384]{1,0:T(8,128)}, f32[32,384]{1,0:T(8,128)S(1)}, u32[]{:S(2)}, u32[]{:S(2)}) collective-permute-start(f32[32,384]{1,0:T(8,128)} %get-tuple-element.217), channel_id=1, source_target_pairs={{0,32},{1,33},{2,34},{3,35},{4,36},{5,37},{6,38},{7,39},{8,40},{9,... | collective-permute-start | bytes 147464 | tf_op jit(solution)/shard_map/ppermute | solution.py:31
  171.2 17.6 %all-to-all-start.1 = ((f32[32,2,16,128]{3,2,1,0:T(8,128)}), f32[32,2,16,128]{3,2,1,0:T(8,128)S(1)}, u32[]{:S(2)}, u32[]{:S(2)}) async-start(f32[32,2,16,128]{3,2,1,0:T(8,128)} %get-tuple-element.230), calls=%async_computation.1 | async-start | bytes 1048576 | tf_op jit(solution)/shard_map/all_to_all | solution.py:422
  191.6 9.5 %collective-permute-start.33 = (f32[32,16,128]{2,1,0:T(8,128)}, f32[32,16,128]{2,1,0:T(8,128)S(1)}, u32[]{:S(2)}, u32[]{:S(2)}) collective-permute-start(f32[32,16,128]{2,1,0:T(8,128)} %select.7.q0), channel_id=1, source_target_pairs={{0,3},{1,0},{2,1},{3,2},{4,7},{5,4},{6,5},{7,6},{8,11},{9,8},{10,9... | collective-permute-start | bytes 786440 | tf_op jit(solution)/shard_map/ppermute | solution.py:31
  192.3 10.2 %collective-permute-start.32 = (f32[32,16,128]{2,1,0:T(8,128)}, f32[32,16,128]{2,1,0:T(8,128)S(1)}, u32[]{:S(2)}, u32[]{:S(2)}) collective-permute-start(f32[32,16,128]{2,1,0:T(8,128)} %select.7.q0), channel_id=1, source_target_pairs={{0,2},{1,3},{2,0},{3,1},{4,6},{5,7},{6,4},{7,5},{8,10},{9,11},{10,... | collective-permute-start | bytes 786440 | tf_op jit(solution)/shard_map/ppermute | solution.py:31
  195.1 11.2 %collective-permute-start.31 = (f32[32,16,128]{2,1,0:T(8,128)}, f32[32,16,128]{2,1,0:T(8,128)S(1)}, u32[]{:S(2)}, u32[]{:S(2)}) collective-permute-start(f32[32,16,128]{2,1,0:T(8,128)} %select.7.q0), channel_id=1, source_target_pairs={{0,1},{1,2},{2,3},{3,0},{4,5},{5,6},{6,7},{7,4},{8,9},{9,10},{10,1... | collective-permute-start | bytes 786440 | tf_op jit(solution)/shard_map/ppermute | solution.py:31
  (38 other events, 308.3 us)

commit v3 on v2

v3 whole, which is shorter than its diff:
```python
import functools

import jax
import jax.numpy as jnp
from jax import lax
from jax.experimental import pallas as pl
from jax.experimental.pallas import tpu as pltpu
from jax.sharding import PartitionSpec as P

F32 = jnp.float32
BF16 = jnp.bfloat16
VMEM_LIMIT = 58 * 1024 * 1024

SWAP = [(0, 1), (1, 0)]


def device(h, y, x, z):
    return (h * 16 + y % 4 * 4 + x % 4) * 4 + z % 4


def stepper(axis):
    def step(v, d):
        pairs = []
        for h in range(2):
            by = d if h == 0 else -d
            move = [by if name == axis else 0 for name in "yxz"]
            for y in range(4):
                for x in range(4):
                    for z in range(4):
                        pairs.append((device(h, y, x, z), device(h, y + move[0], x + move[1], z + move[2])))
        return lax.ppermute(v, ("gx", "gy", "gz"), pairs)

    return step


shift_x, shift_y, shift_z = stepper("x"), stepper("y"), stepper("z")


def swapper(axis):
    def swap(v, turn):
        pairs = []
        for h in range(2):
            mask = 1 if h == turn else 3
            for y in range(4):
                for x in range(4):
                    for z in range(4):
                        to = [c ^ mask if name == axis else c for name, c in zip("yxz", (y, x, z))]
                        pairs.append((device(h, y, x, z), device(h, *to)))
        return lax.ppermute(v, ("gx", "gy", "gz"), pairs)

    return swap


swap_x, swap_y, swap_z = swapper("x"), swapper("y"), swapper("z")


def ahead(place, axis, d):
    return lax.rem(place[axis] + d * place[4], 4)


def owner_masks(place):
    return ((0, 0, 0), (1, 0, place[4]), (1, 1, 2), (0, 1, 4 - place[4]))


def split(v):
    high = v.astype(BF16)
    return high, (v - high.astype(F32)).astype(BF16)


def dot3(a_high, a_low, b_high, b_low, dims):
    dot = functools.partial(lax.dot_general, dimension_numbers=(dims, ((), ())), preferred_element_type=F32)
    return dot(a_high, b_high) + (dot(a_high, b_low) + dot(a_low, b_high))


def project_kernel(place, field, basis, own, other, land, x_land, x_high, x_low, f_high, f_low, sems):
    def load(k):
        part = pl.ds(k * 2, 2)
        return pltpu.make_async_copy(field.at[part], land.at[part], sems.at[k])

    x_load = pltpu.make_async_copy(basis, x_land, sems.at[6])
    x_load.start()
    for k in range(6):
        load(k).start()
    x_load.wait()
    turned = x_land[...].T
    for half in range(2):
        rows = pl.ds(pl.multiple_of((place[0] ^ half) * 128, 128), 128)
        x_high[rows, :], x_low[rows, :] = split(turned[half * 128 : half * 128 + 128])
    for k in range(6):
        load(k).wait()
        for s in (2 * k, 2 * k + 1):
            f_high[:, s * 128 : s * 128 + 128], f_low[:, s * 128 : s * 128 + 128] = split(land[s])
    out = dot3(x_high[...], x_low[...], f_high[...], f_low[...], ((1,), (0,)))
    own[...] = out[:128]
    other[...] = out[128:]


def project(place, field, basis):
    out = jax.ShapeDtypeStruct((128, 1536), F32)
    return pl.pallas_call(
        project_kernel,
        in_specs=[pl.BlockSpec(memory_space=pltpu.SMEM)] + [pl.BlockSpec(memory_space=pl.ANY)] * 2,
        out_specs=[pl.BlockSpec(memory_space=pltpu.VMEM)] * 2,
        out_shape=[out, out],
        scratch_shapes=[
            pltpu.VMEM((12, 1024, 128), F32),
            pltpu.VMEM((1024, 256), F32),
            pltpu.VMEM((256, 1024), BF16),
            pltpu.VMEM((256, 1024), BF16),
            pltpu.VMEM((1024, 1536), BF16),
            pltpu.VMEM((1024, 1536), BF16),
            pltpu.SemaphoreType.DMA((7,)),
        ],
        compiler_params=pltpu.CompilerParams(vmem_limit_bytes=VMEM_LIMIT),
        cost_estimate=pl.CostEstimate(flops=2400000000, bytes_accessed=9000000, transcendentals=0),
        name="project",
    )(place, field, basis)


def send_out(place, buf, b, lane_of, refs, sems):
    def piece(x, row, rows, third):
        row = pl.multiple_of(x * 64 + row, 16)
        return buf.at[pl.ds(row, rows), pl.ds(pl.multiple_of(lane_of(x) + third * 384, 128), 384)]

    rows = pl.ds(0, 64)
    for sent, slot, mask in owner_masks(place):
        x, z = place[1] ^ mask, place[3] ^ mask
        pltpu.make_async_copy(piece(x, 0, 64, 0), refs[sent].at[slot, b, rows], sems.at[sent]).start()

        @pl.when(place[2] ^ mask == b)
        def _():
            for x in range(4):
                pltpu.make_async_copy(piece(x, 0, 64, 1), refs[2 + sent].at[slot, x, rows], sems.at[2 + sent]).start()

        for x in range(4):
            to = refs[4 + sent].at[slot, b * 4 + x]
            pltpu.make_async_copy(piece(x, z * 16, 16, 2), to, sems.at[4 + sent]).start()


def wait_out(refs, sems):
    for i, ref in enumerate(refs):
        part = ref.at[:, :, pl.ds(0, 64)] if i < 4 else ref
        pltpu.make_async_copy(part, part, sems.at[i]).wait()


def core_copies(place, buf, refs, sems):
    copies = []
    for sent, slot, mask in owner_masks(place):
        for other in range(4):
            for half in range(2):
                rows = pl.ds(64 + half * 16, 16)
                q = pl.multiple_of((other * 4 + (place[1] ^ mask)) * 16, 16)
                src = buf.at[pl.ds(q, 16), pl.ds(half * 384, 384)]
                copies.append(pltpu.make_async_copy(src, refs[sent].at[slot, other, rows], sems.at[sent]))
                q = pl.multiple_of(((place[2] ^ mask) * 4 + other) * 16, 16)
                src = buf.at[pl.ds(q, 16), pl.ds(768 + half * 384, 384)]
                copies.append(pltpu.make_async_copy(src, refs[2 + sent].at[slot, other, rows], sems.at[2 + sent]))
    return copies


def gram_x_kernel(place, own, other, reduced, y_basis, *refs):
    high, low, buf, land, core, out_sems, sems, core_sems = refs[6:]

    def load(k):
        src = own if k < 6 else other
        part = pl.ds(k % 6 * 2, 2)
        return pltpu.make_async_copy(src.at[part], land.at[pl.ds(k * 2, 2)], sems.at[k])

    for k in range(12):
        load(k).start()
    y_high, y_low = split(y_basis[...].T)
    for s in range(12):
        r_high, r_low = split(reduced[:, s * 128 : s * 128 + 128])
        core[:, s * 128 : s * 128 + 128] = dot3(y_high, y_low, r_high, r_low, ((1,), (1,)))
    for copy in core_copies(place, core, refs, core_sems):
        copy.start()
    for k in range(12):
        load(k).wait()
        for s in (2 * k, 2 * k + 1):
            rows, cols = slice(s // 12 * 1024, s // 12 * 1024 + 1024), slice(s % 12 * 128, s % 12 * 128 + 128)
            high[rows, cols], low[rows, cols] = split(land[s])
    for b in range(4):
        rows, cols = slice(b * 256, b * 256 + 256), slice(b * 256, b * 256 + 1280)
        buf[b] = dot3(high[rows, :], low[rows, :], high[cols, :], low[cols, :], ((1,), (1,)))
        send_out(place, buf.at[b], b, lambda x: (x // 2) * 128, refs, out_sems)
    wait_out(refs[:6], out_sems)
    for i in range(4):
        part = refs[i].at[:, :, pl.ds(64, 32)]
        pltpu.make_async_copy(part, part, core_sems.at[i]).wait()


def gram_y_kernel(place, own, other, *refs):
    high, low, buf, out_sems = refs[6:]
    for j in range(16):
        tiles = [src[j, :, s * 128 : s * 128 + 128] for src in (own, other) for s in range(12)]
        v = jnp.concatenate(tiles + [jnp.zeros((64, 128), F32)], axis=0).T
        v_high, v_low = split(v)
        for start in (j * 128, 2048 + j * 128):
            if start < 3072:
                high[start : start + 128, :] = v_high
                low[start : start + 128, :] = v_low
    h = place[0]
    for b in range(4):
        starts = [pl.multiple_of((b * 4 + x) * 128 + h * 64, 64) for x in range(4)]
        l_high = jnp.concatenate([high[pl.ds(r, 64), :] for r in starts], axis=0)
        l_low = jnp.concatenate([low[pl.ds(r, 64), :] for r in starts], axis=0)
        cols = slice(b * 512, b * 512 + 1536)
        buf[b] = dot3(l_high, l_low, high[cols, :], low[cols, :], ((1,), (1,)))
        send_out(place, buf.at[b], b, lambda x: x * 128, refs, out_sems)
    wait_out(refs[:6], out_sems)


def gram_pieces(kernel, name, rows, place, args, spaces, scratch, flops):
    ab = jax.ShapeDtypeStruct((2, 4, rows, 384), F32)
    c = jax.ShapeDtypeStruct((2, 16, 16, 384), F32)
    return pl.pallas_call(
        kernel,
        in_specs=[pl.BlockSpec(memory_space=space) for space in (pltpu.SMEM,) + spaces],
        out_specs=[pl.BlockSpec(memory_space=pl.ANY)] * 6,
        out_shape=[ab] * 4 + [c] * 2,
        scratch_shapes=scratch,
        compiler_params=pltpu.CompilerParams(vmem_limit_bytes=VMEM_LIMIT),
        cost_estimate=pl.CostEstimate(flops=flops, bytes_accessed=20000000, transcendentals=0),
        name=name,
    )(place, *args)


GRAM_X_SCRATCH = [
    pltpu.VMEM((2048, 1536), BF16),
    pltpu.VMEM((2048, 1536), BF16),
    pltpu.VMEM((4, 256, 1280), F32),
    pltpu.VMEM((24, 1024, 128), F32),
    pltpu.VMEM((256, 1536), F32),
    pltpu.SemaphoreType.DMA((6,)),
    pltpu.SemaphoreType.DMA((12,)),
    pltpu.SemaphoreType.DMA((4,)),
]
GRAM_Y_SCRATCH = [
    pltpu.VMEM((3072, 256), BF16),
    pltpu.VMEM((3072, 256), BF16),
    pltpu.VMEM((4, 256, 1536), F32),
    pltpu.SemaphoreType.DMA((12,)),
]


def sum4(terms, index):
    return (terms[0][index] + terms[1][index]) + (terms[2][index] + terms[3][index])


def add_kernel(*refs):
    *terms, out = refs
    at = 0
    for kept, came in zip(terms[0::2], terms[1::2]):
        rows = kept.shape[2]
        out[:, at : at + rows, :] = kept[0] + came[0]
        at += rows


def slab_of(v, k):
    return pl.BlockSpec((1,) + v.shape[1:], lambda i: (k, 0, 0, 0))


def add_for_second(terms):
    shape = (terms[0].shape[1], sum(v.shape[2] for v in terms[0::2]), 384)
    return pl.pallas_call(
        add_kernel,
        grid=(1,),
        in_specs=[slab_of(v, 1) for v in terms],
        out_specs=pl.BlockSpec(shape, lambda i: (0, 0, 0)),
        out_shape=jax.ShapeDtypeStruct(shape, F32),
        compiler_params=pltpu.CompilerParams(vmem_limit_bytes=VMEM_LIMIT),
        cost_estimate=pl.CostEstimate(flops=200000, bytes_accessed=3000000, transcendentals=0),
        name="add",
    )(*terms)


def sum_first_kernel(axis, place, *refs):
    terms, last, outs = refs[:4], refs[4], refs[5:]
    at = 0
    for kept, came in zip(terms[0::2], terms[1::2]):
        rows = slice(at, at + kept.shape[2])
        if axis is None:
            outs[0][:, rows, :] = (kept[0] + came[0]) + last[:, rows, :]
        else:
            for d, out in enumerate(outs):
                k = ahead(place, axis, d)
                out[rows, :] = (kept[0, k] + came[0, k]) + last[k, rows, :]
        at = rows.stop


def sum_first(place, axis, terms, last):
    shapes = [last.shape] if axis is None else [last.shape[1:]] * 4
    return pl.pallas_call(
        functools.partial(sum_first_kernel, axis),
        grid=(1,),
        in_specs=[pl.BlockSpec(memory_space=pltpu.SMEM)]
        + [slab_of(v, 0) for v in terms]
        + [pl.BlockSpec(last.shape, lambda i: (0, 0, 0))],
        out_specs=[pl.BlockSpec(out, lambda i, n=len(out): (0,) * n) for out in shapes],
        out_shape=[jax.ShapeDtypeStruct(out, F32) for out in shapes],
        compiler_params=pltpu.CompilerParams(vmem_limit_bytes=VMEM_LIMIT),
        cost_estimate=pl.CostEstimate(flops=1000000, bytes_accessed=4000000, transcendentals=0),
        name="sum_first",
    )(place, *terms, last)


def sum_second_kernel(place, *refs):
    outs = refs[8:]
    for part in range(2):
        terms = refs[part * 4 : part * 4 + 4]
        for d in range(4):
            for g in range(2):
                rows = pl.ds(pl.multiple_of(g * 96 + ahead(place, 3, d) * 16, 16), 16)
                to = part * 32 + g * 16
                outs[d][to : to + 16, :] = sum4(terms, (rows, slice(None)))
        outs[4][part * 32 : part * 32 + 32, :] = sum4(terms, (slice(64, 96), slice(None)))


def sum_last_kernel(place, *refs):
    slots, direct_x, keep, give, wide = refs[5:]
    h = place[0]
    j = place[2] * 4 + place[1]
    block_x = h * 8 + j // 2
    parts = [sum4(refs[:4], (slice(0, 32), slice(None))), sum4(refs[:4], (slice(32, 64), slice(None))), refs[4][...]]
    zero = jnp.zeros((16, 128), F32)
    for k in range(16):
        lane = k % 3 * 128
        tile_x = parts[k // 3][:16, lane : lane + 128] if k < 9 else zero
        tile_y = parts[k // 3][16:, lane : lane + 128] if k < 9 else zero
        to_x, to_y = lax.rem(block_x + k, 16), lax.rem(j + k, 16)
        direct_x[to_x] = tile_x
        wide[lax.rem(to_y + 8 * h, 16)] = tile_y
        slots[2 * to_x, 0] = tile_x
        slots[2 * to_x + 1, 0] = tile_x
        slots[to_y, 1] = tile_y
        slots[16 + to_y, 1] = tile_y
    keep[...] = wide[:8]
    give[...] = wide[8:]


def select_kernel(place, got, direct_x, keep, come, out):
    h = place[0]
    j = place[2] * 4 + place[1]
    block_x = h * 8 + j // 2
    for block in range(16):
        first, second = got[2 * block, 0], got[2 * block + 1, 0]
        even = jnp.concatenate([first[:, :64], second[:, :64]], axis=1)
        odd = jnp.concatenate([first[:, 64:], second[:, 64:]], axis=1)
        turned = jnp.where(lax.rem(j, 2) == 0, even, odd)
        out[block] = jnp.where(lax.rem(block - block_x + 16, 16) <= 8, direct_x[block], turned)
    for block in range(8):
        is_direct = lax.rem(h * 8 + block - j + 16, 16) <= 8
        for half in range(2):
            direct = jnp.where(h == half, keep[block], come[block])
            out[16 + 2 * block + half] = jnp.where(is_direct, direct, got[half * 16 + h * 8 + block, 1])


def assemble_kernel(scale_x, scale_y, place, q0, q1, q2, q3, gram_x, gram_y, rows):
    h = place[0]
    j = place[2] * 4 + place[1]
    block_x = h * 8 + j // 2
    for d, quarter in enumerate((q0, q1, q2, q3)):
        z = ahead(place, 3, 4 - d)
        rows[:, pl.ds(pl.multiple_of(z * 16, 16), 16), :] = quarter[...]
    for block in range(16):
        direct = rows[block]
        turned = direct.T
        turned = jnp.concatenate([turned[:64], turned[64:]], axis=1)
        is_direct = lax.rem(block - block_x + 16, 16) <= 8
        gram_x[:, block * 128 : block * 128 + 128] = jnp.where(is_direct, direct, turned) * scale_x
    for block in range(8):
        direct = jnp.concatenate([rows[16 + 2 * block], rows[17 + 2 * block]], axis=0)
        is_direct = lax.rem(h * 8 + block - j + 16, 16) <= 8
        gram_y[:, block * 128 : block * 128 + 128] = jnp.where(is_direct, direct, direct.T) * scale_y


def add_two_kernel(place, first, second, out):
    out[...] = first[...] + second[...]


def small_kernel(kernel, name, out_shape, scratch, *args):
    return pl.pallas_call(
        kernel,
        in_specs=[pl.BlockSpec(memory_space=pltpu.SMEM)] + [pl.BlockSpec(memory_space=pltpu.VMEM)] * (len(args) - 1),
        out_shape=out_shape,
        scratch_shapes=scratch,
        compiler_params=pltpu.CompilerParams(vmem_limit_bytes=VMEM_LIMIT),
        name=name,
    )(*args)


def per_device(species_field, x_mode_basis, y_mode_basis):
    h, j, z0 = lax.axis_index("gx"), lax.axis_index("gy"), lax.axis_index("gz")
    x0, y0 = j % 4, j // 4
    place = jnp.stack([h, x0, y0, z0, 1 + 2 * h]).astype(jnp.int32)
    nx = 2 * species_field.shape[1]
    ny = 16 * species_field.shape[2]
    slices = 4 * species_field.shape[0]
    ranks = x_mode_basis.shape[1]

    other_field = lax.ppermute(species_field, "gx", SWAP)
    mine, theirs = project(place, species_field, x_mode_basis)
    reduced = small_kernel(
        add_two_kernel, "add_two", jax.ShapeDtypeStruct((128, 1536), F32), [], place, mine, lax.ppermute(theirs, "gx", SWAP)
    )
    fibers = lax.all_to_all(reduced.reshape(16, 8, 1536), "gy", 0, 0, tiled=True)

    def first_swaps(pieces):
        return [swap(pieces[2 * i + 1], 0) for i, swap in enumerate((swap_x, swap_y, swap_z))]

    px = gram_pieces(
        gram_x_kernel, "gram_x", 96, place, (species_field, other_field, reduced, y_mode_basis),
        (pl.ANY, pl.ANY, pltpu.VMEM, pltpu.VMEM), GRAM_X_SCRATCH, 12000000000,
    )
    px, fibers = lax.optimization_barrier((px, fibers))
    other_fibers = lax.ppermute(fibers, "gx", SWAP)
    came_x = first_swaps(px)
    py = gram_pieces(
        gram_y_kernel, "gram_y", 64, place, (fibers, other_fibers), (pltpu.VMEM, pltpu.VMEM), GRAM_Y_SCRATCH, 2400000000
    )
    came_y = first_swaps(py)

    def ring(terms, shift):
        up, down = shift(terms[1], 1), shift(terms[3], 3)
        far, up = lax.optimization_barrier((terms[2], up))
        return [terms[0], up, down, shift(far, 2)]

    terms_a, terms_b, terms_c = [(px[2 * i], came_x[i], py[2 * i], came_y[i]) for i in range(3)]
    add_c = add_for_second(terms_c)
    add_c, terms_a, terms_b = lax.optimization_barrier((add_c, terms_a, terms_b))
    (c,) = sum_first(place, None, terms_c, swap_z(add_c, 1))
    a = sum_first(place, 2, terms_a, swap_x(add_for_second(terms_a), 1))
    b = sum_first(place, 1, terms_b, swap_y(add_for_second(terms_b), 1))
    a, b = ring(a, shift_y), ring(b, shift_x)
    a, b, c = lax.optimization_barrier((a, b, c))
    c = lax.all_to_all(c, "gy", 0, 0, tiled=True).sum(axis=0)
    part = jax.ShapeDtypeStruct((64, 384), F32)
    *quarters, core = small_kernel(
        sum_second_kernel, "sum_second", [part] * 5, [], place, *a, *b
    )
    blocks = jax.ShapeDtypeStruct((8, 16, 128), F32)
    slots, direct_x, keep, give = small_kernel(
        sum_last_kernel, "sum_last",
        [jax.ShapeDtypeStruct((32, 2, 16, 128), F32), jax.ShapeDtypeStruct((16, 16, 128), F32), blocks, blocks],
        [pltpu.VMEM((16, 16, 128), F32)],
        place, *[quarters[0]] + [shift_z(quarters[d], d) for d in (1, 2, 3)], c,
    )
    core = core.reshape(2, 2, 16, 3, 128).transpose(4, 0, 1, 3, 2).reshape(128, 12, 16)

    got = lax.all_to_all(slots, ("gx", "gy"), 0, 0, tiled=True)
    come = lax.ppermute(give, "gx", SWAP)
    part = small_kernel(
        select_kernel, "select", jax.ShapeDtypeStruct((32, 16, 128), F32), [], place, got, direct_x, keep, come
    )
    quarters = [part] + [shift_z(part, d) for d in (1, 2, 3)]
    gram_x, gram_y = small_kernel(
        functools.partial(assemble_kernel, 1.0 / (ny * slices), 1.0 / (ranks * slices)),
        "assemble",
        [jax.ShapeDtypeStruct((64, nx), F32), jax.ShapeDtypeStruct((128, ny // 2), F32)],
        [pltpu.VMEM((32, 64, 128), F32)],
        place, *quarters,
    )
    return (gram_x, gram_y, core)


def solution(mesh):
    in_specs = (P("gz", "gx", "gy"), P("gx", None), P("gy", None))
    out_specs = (P(("gx", "gy"), None), P("gy", "gx"), P("gx", "gz", "gy"))
    return jax.shard_map(
        per_device, mesh=mesh, in_specs=in_specs, out_specs=out_specs, check_vma=False
    )
```

time: 211 us -> 183 us (0.87)
  waiting for transfers between devices: 72 us -> 50 us
  starting transfers between devices: 72.7 us -> 58.2 us
  Pallas kernels: 55.1 us -> 62.1 us
  local copies, waits for them, and re-layouts: 6.85 us -> 10.8 us
    ppermute x30 -> x12, waiting for transfers between devices: 56.1 us -> 15.8 us  [step(): return lax.ppermute(v, ('gx', 'gy', 'gz'), pairs)]
    ppermute x30 -> x12, starting transfers between devices: 58.6 us -> 21.5 us  [step(): return lax.ppermute(v, ('gx', 'gy', 'gz'), pairs)]
    ppermute x1 -> x10, waiting for transfers between devices: 2.12 us -> 20.1 us  [the longest x9 17.5 us: swap(): return lax.ppermute(v, ('gx', 'gy', 'gz'), pairs)]
    ppermute x1 -> x10, starting transfers between devices: 0.55 us -> 15.4 us  [the longest x9 14.8 us: swap(): return lax.ppermute(v, ('gx', 'gy', 'gz'), pairs)]
    pallas_call x3 -> x8, Pallas kernels: 36 us -> 42.8 us  [the longest x2 27 us: gram_pieces(): pl.pallas_call(kernel, in_specs=[pl.BlockSpec(memory_space=space) for spa...]
    all_to_all x0 -> x1, starting transfers between devices: none -> 6.42 us  [per_device(): c = lax.all_to_all(c, 'gy', 0, 0, tiled=True).sum(axis=0)]
    unnamed x68 -> x60, local copies, waits for them, and re-layouts: 4.67 us -> 9.4 us
    all_to_all x0 -> x1, waiting for transfers between devices: none -> 2.43 us  [per_device(): c = lax.all_to_all(c, 'gy', 0, 0, tiled=True).sum(axis=0)]
  transfers between devices with their start and end apart: 36 -> 28, of which waited for: 20 -> 13; matrix products, arithmetic and copies ran while one was open for 2% -> 1% of each run, Pallas kernels for 15% -> 29%
where the time goes in v3:
time: 183 us
  Pallas kernels  62.1 us (34%)
  starting transfers between devices  58.2 us (32%)
  waiting for transfers between devices  50 us (27%)
  local copies, waits for them, and re-layouts  10.8 us (6%)
    pallas_call x2, Pallas kernels, gram_pieces(): pl.pallas_call(kernel, in_specs=[pl.BlockSpec(memory_space=space) for spa...  27 us
    ppermute x12, starting transfers between devices, step(): return lax.ppermute(v, ('gx', 'gy', 'gz'), pairs)  21.5 us
    ppermute x9, waiting for transfers between devices, swap(): return lax.ppermute(v, ('gx', 'gy', 'gz'), pairs)  17.5 us
    ppermute x12, waiting for transfers between devices, step(): return lax.ppermute(v, ('gx', 'gy', 'gz'), pairs)  15.8 us
    ppermute x9, starting transfers between devices, swap(): return lax.ppermute(v, ('gx', 'gy', 'gz'), pairs)  14.8 us
    pallas_call x5, Pallas kernels, small_kernel(): pl.pallas_call(kernel, in_specs=[pl.BlockSpec(memory_space=pltpu.SMEM)] +...  11.7 us
    all_to_all x1, waiting for transfers between devices, per_device(): got = lax.all_to_all(slots, ('gx', 'gy'), 0, 0, tiled=True)  10.4 us
    unnamed x60, local copies, waits for them, and re-layouts  9.4 us
  transfers between devices with their start and end apart: 28, of which 13 were waited for; matrix products, arithmetic and copies ran while one was open for 1% of the time, Pallas kernels for 29%

profile of v3, /device:TPU:0, one launch (start us, length us, event | category | flops | bytes accessed | tf_op | source)
XLA Modules:
  0.0 182.6 jit_solution(13167111430815803267)
XLA Ops:
  1.4 7.6 %project.1 = (f32[128,1536]{1,0:T(8,128)}, f32[128,1536]{1,0:T(8,128)}) custom-call(s32[5]{0:T(128)} %stack.23.place, f32[12,1024,128]{2,1,0:T(8,128)} %own.1, f32[1024,256]{1,0:T(8,128)} %basis.1), custom_call_target="tpu_custom_call" | custom-call | flops 2400000000 | bytes 9000000 | tf_op jit(solution)/shard_map/project/pallas_call | solution.py:100
  9.6 2.6 %collective-permute-done.1.second = f32[128,1536]{1,0:T(8,128)S(1)} collective-permute-done((f32[128,1536]{1,0:T(8,128)}, f32[128,1536]{1,0:T(8,128)S(1)}, u32[]{:S(2)}, u32[]{:S(2)}) %collective-permute-start.1) | collective-permute-done | bytes 786464 | tf_op jit(solution)/shard_map/ppermute | solution.py:404
  13.2 2.4 %add_two.1.reduced = f32[128,1536]{1,0:T(8,128)} custom-call(s32[5]{0:T(128)} %stack.23.place, f32[128,1536]{1,0:T(8,128)} %get-tuple-element.65.first, f32[128,1536]{1,0:T(8,128)} %copy-done.10), custom_call_target="tpu_custom_call" | custom-call | tf_op jit(solution)/shard_map/add_two/pallas_call | solution.py:382
  15.5 7.3 %all-to-all-start = ((f32[16,8,1536]{2,1,0:T(8,128)}), f32[16,8,1536]{2,1,0:T(8,128)S(1)}, u32[]{:S(2)}, u32[]{:S(2)}) async-start(f32[16,8,1536]{2,1,0:T(8,128)} %bitcast.8), calls=%async_computation | async-start | bytes 1572864 | tf_op jit(solution)/shard_map/all_to_all | solution.py:406
  22.8 21.1 %gram_x.1 = (f32[2,4,96,384]{3,2,1,0:T(8,128)}, f32[2,4,96,384]{3,2,1,0:T(8,128)}, f32[2,4,96,384]{3,2,1,0:T(8,128)}, f32[2,4,96,384]{3,2,1,0:T(8,128)}, f32[2,1...) custom-call(s32[5]{0:T(128)} %stack.23.place, f32[12,1024,128]{2,1,0:T(8,128)} %own.1, ...), custom_call_target="tpu_custom_call" | custom-call | flops 12000000000 | bytes 20000000 | tf_op jit(solution)/shard_map/gram_x/pallas_call | solution.py:216
  50.2 5.9 %gram_y.1 = (f32[2,4,64,384]{3,2,1,0:T(8,128)}, f32[2,4,64,384]{3,2,1,0:T(8,128)}, f32[2,4,64,384]{3,2,1,0:T(8,128)}, f32[2,4,64,384]{3,2,1,0:T(8,128)}, f32[2,1...) custom-call(s32[5]{0:T(128)} %stack.23.place, f32[16,8,1536]{2,1,0:T(8,128)} %copy-done.11, f32[16,8,1536]{2,1,0:T(8,128)} %copy-done.27), custom_call_target="tpu_custom_call" | custom-call | flops 2400000000 | bytes 20000000 | tf_op jit(solution)/shard_map/gram_y/pallas_call | solution.py:216
  58.3 10.0 %collective-permute-done.4.refs_3_ = f32[2,16,16,384]{3,2,1,0:T(8,128)S(1)} collective-permute-done((f32[2,16,16,384]{3,2,1,0:T(8,128)}, f32[2,16,16,384]{3,2,1,0:T(8,128)S(1)}, u32[]{:S(2)}, u32[]{:S(2)}) %collective-permute-start.4) | collective-permute-done | bytes 786464 | tf_op jit(solution)/shard_map/ppermute | solution.py:49
  69.3 2.3 %add.9 = f32[16,32,384]{2,1,0:T(8,128)} custom-call(f32[2,16,16,384]{3,2,1,0:T(8,128)} %get-tuple-element.73.refs_0_, f32[2,16,16,384]{3,2,1,0:T(8,128)} %copy-done.4, f32[2,16,16,384]{3,2,1,0:T(8,128)} %get-tuple-element.76.refs_2_, f32[2,16,16,384]{3,2,1,0:T(8,128)} %copy-done.5), custom_call_target="tpu_custom_call" | custom-call | flops 200000 | bytes 3000000 | tf_op jit(solution)/shard_map/add/pallas_call | solution.py:265
  73.6 2.5 %add.11 = f32[4,160,384]{2,1,0:T(8,128)} custom-call(f32[2,4,96,384]{3,2,1,0:T(8,128)} %get-tuple-element.96.refs_0_, f32[2,4,96,384]{3,2,1,0:T(8,128)} %copy-done.1, f32[2,4,64,384]{3,2,1,0:T(8,128)} %get-tuple-element.98.refs_2_, f32[2,4,64,384]{3,2,1,0:T(8,128)} %copy-done.3), custom_call_target="tpu_custom_call" | custom-call | flops 200000 | bytes 3000000 | tf_op jit(solution)/shard_map/add/pallas_call | solution.py:265
  76.1 2.8 %collective-permute-start.13 = (f32[4,160,384]{2,1,0:T(8,128)}, f32[4,160,384]{2,1,0:T(8,128)S(1)}, u32[]{:S(2)}, u32[]{:S(2)}) collective-permute-start(f32[4,160,384]{2,1,0:T(8,128)} %add.11), channel_id=1, source_target_pairs={{0,48},{1,49},{2,50},{3,51},{4,52},{5,53},{6,54},{7,55},{8,56},{9,... | collective-permute-start | bytes 2949128 | tf_op jit(solution)/shard_map/ppermute | solution.py:49
  78.8 2.5 %add.10 = f32[4,160,384]{2,1,0:T(8,128)} custom-call(f32[2,4,96,384]{3,2,1,0:T(8,128)} %get-tuple-element.86.refs_0_, f32[2,4,96,384]{3,2,1,0:T(8,128)} %copy-done, f32[2,4,64,384]{3,2,1,0:T(8,128)} %get-tuple-element.88.refs_2_, f32[2,4,64,384]{3,2,1,0:T(8,128)} %copy-done.2), custom_call_target="tpu_custom_call" | custom-call | flops 200000 | bytes 3000000 | tf_op jit(solution)/shard_map/add/pallas_call | solution.py:265
  81.4 2.1 %collective-permute-start.9 = (f32[4,160,384]{2,1,0:T(8,128)}, f32[4,160,384]{2,1,0:T(8,128)S(1)}, u32[]{:S(2)}, u32[]{:S(2)}) collective-permute-start(f32[4,160,384]{2,1,0:T(8,128)} %add.10), channel_id=1, source_target_pairs={{0,12},{1,13},{2,14},{3,15},{4,8},{5,9},{6,10},{7,11},{8,4},{9,5},... | collective-permute-start | bytes 2949128 | tf_op jit(solution)/shard_map/ppermute | solution.py:49
  83.5 2.5 %collective-permute-start.17 = (f32[16,32,384]{2,1,0:T(8,128)S(1)}, f32[16,32,384]{2,1,0:T(8,128)S(1)}, u32[]{:S(2)}, u32[]{:S(2)}) collective-permute-start(f32[16,32,384]{2,1,0:T(8,128)S(1)} %copy-done.12), channel_id=1, source_target_pairs={{0,3},{1,2},{2,1},{3,0},{4,7},{5,6},{6,5},{7,4},{8,11},{9,10},{10,... | collective-permute-start | bytes 2359304 | tf_op jit(solution)/shard_map/ppermute | solution.py:49
  86.0 5.7 %collective-permute-done.13.refs_4_ = f32[4,160,384]{2,1,0:T(8,128)S(1)} collective-permute-done((f32[4,160,384]{2,1,0:T(8,128)}, f32[4,160,384]{2,1,0:T(8,128)S(1)}, u32[]{:S(2)}, u32[]{:S(2)}) %collective-permute-start.13) | collective-permute-done | bytes 983072 | tf_op jit(solution)/shard_map/ppermute | solution.py:49
  92.6 2.9 %sum_first.4 = (f32[160,384]{1,0:T(8,128)}, f32[160,384]{1,0:T(8,128)}, f32[160,384]{1,0:T(8,128)}, f32[160,384]{1,0:T(8,128)}) custom-call(s32[5]{0:T(128)} %stack.23.place, f32[2,4,96,384]{3,2,1,0:T(8,128)} %get-tuple-element.96.refs_0_, f32[2,4,96,384]{3,2,1,0:T(8,128)} %copy-done.1, f32[2,4,64,384]{3,2,1,0:T(8,128)} %get-tuple-element.98.refs_2_, ...), custom_call_target="tpu_custom_call" | custom-call | flops 1000000 | bytes 4000000 | tf_op jit(solution)/shard_map/sum_first/pallas_call | solution.py:293
  97.9 2.9 %sum_first.3 = (f32[160,384]{1,0:T(8,128)}, f32[160,384]{1,0:T(8,128)}, f32[160,384]{1,0:T(8,128)}, f32[160,384]{1,0:T(8,128)}) custom-call(s32[5]{0:T(128)} %stack.23.place, f32[2,4,96,384]{3,2,1,0:T(8,128)} %get-tuple-element.86.refs_0_, f32[2,4,96,384]{3,2,1,0:T(8,128)} %copy-done, f32[2,4,64,384]{3,2,1,0:T(8,128)} %get-tuple-element.88.refs_2_, ...), custom_call_target="tpu_custom_call" | custom-call | flops 1000000 | bytes 4000000 | tf_op jit(solution)/shard_map/sum_first/pallas_call | solution.py:293
  101.0 2.1 %collective-permute-start.15 = (f32[160,384]{1,0:T(8,128)S(1)}, f32[160,384]{1,0:T(8,128)S(1)}, u32[]{:S(2)}, u32[]{:S(2)}) collective-permute-start(f32[160,384]{1,0:T(8,128)S(1)} %copy-done.29), channel_id=1, source_target_pairs={{0,12},{1,13},{2,14},{3,15},{4,0},{5,1},{6,2},{7,3},{8,4},{9,5},{1... | collective-permute-start | bytes 737288 | tf_op jit(solution)/shard_map/ppermute | solution.py:31
  103.1 3.0 %collective-permute-start.11 = (f32[160,384]{1,0:T(8,128)}, f32[160,384]{1,0:T(8,128)S(1)}, u32[]{:S(2)}, u32[]{:S(2)}) collective-permute-start(f32[160,384]{1,0:T(8,128)} %get-tuple-element.94), channel_id=1, source_target_pairs={{0,48},{1,49},{2,50},{3,51},{4,52},{5,53},{6,54},{7,55},{8,56},{9,... | collective-permute-start | bytes 737288 | tf_op jit(solution)/shard_map/ppermute | solution.py:31
  110.5 2.6 %sum_first.5 = f32[16,32,384]{2,1,0:T(8,128)} custom-call(s32[5]{0:T(128)} %stack.23.place, f32[2,16,16,384]{3,2,1,0:T(8,128)} %get-tuple-element.73.refs_0_, f32[2,16,16,384]{3,2,1,0:T(8,128)} %copy-done.4, f32[2,16,16,384]{3,2,1,0:T(8,128)} %get-tuple-element.76.refs_2_, f32[2,16,16,384]{3,2,1,0:T(8,128)} %copy-done.5, f32[16,32,384]{2,1,0:T(8,128)} %copy-done.9), custom_call_target="tpu_custom_call" | custom-call | flops 1000000 | bytes 4000000 | tf_op jit(solution)/shard_map/sum_first/pallas_call | solution.py:293
  114.2 2.2 %collective-permute-done.12.refs_3_ = f32[160,384]{1,0:T(8,128)S(1)} collective-permute-done((f32[160,384]{1,0:T(8,128)}, f32[160,384]{1,0:T(8,128)S(1)}, u32[]{:S(2)}, u32[]{:S(2)}) %collective-permute-start.12) | collective-permute-done | bytes 245792 | tf_op jit(solution)/shard_map/ppermute | solution.py:31
  116.5 6.4 %all-to-all-start.1 = ((f32[16,32,384]{2,1,0:T(8,128)}), f32[16,32,384]{2,1,0:T(8,128)S(1)}, u32[]{:S(2)}, u32[]{:S(2)}) async-start(f32[16,32,384]{2,1,0:T(8,128)} %sum_first.5), calls=%async_computation.1 | async-start | bytes 1572864 | tf_op jit(solution)/shard_map/all_to_all | solution.py:436
  123.0 2.5 %sum_second.1 = (f32[64,384]{1,0:T(8,128)}, f32[64,384]{1,0:T(8,128)}, f32[64,384]{1,0:T(8,128)}, f32[64,384]{1,0:T(8,128)}, f32[64,384]{1,0:T(8,128)}) custom-call(s32[5]{0:T(128)} %stack.23.place, f32[160,384]{1,0:T(8,128)} %get-tuple-element.107.refs_0_, f32[160,384]{1,0:T(8,128)} %copy-done.17, f32[160,384]{1,0:T(8,128)} %copy-done.19, ...), custom_call_target="tpu_custom_call" | custom-call | tf_op jit(solution)/shard_map/sum_second/pallas_call | solution.py:382
  125.6 5.7 %collective-permute-start.19 = (f32[64,384]{1,0:T(8,128)}, f32[64,384]{1,0:T(8,128)S(1)}, u32[]{:S(2)}, u32[]{:S(2)}) collective-permute-start(f32[64,384]{1,0:T(8,128)} %get-tuple-element.117), channel_id=1, source_target_pairs={{0,2},{1,3},{2,0},{3,1},{4,6},{5,7},{6,4},{7,5},{8,10},{9,11},{10,... | collective-permute-start | bytes 294920 | tf_op jit(solution)/shard_map/ppermute | solution.py:31
  131.3 2.0 %collective-permute-start.20 = (f32[64,384]{1,0:T(8,128)}, f32[64,384]{1,0:T(8,128)S(1)}, u32[]{:S(2)}, u32[]{:S(2)}) collective-permute-start(f32[64,384]{1,0:T(8,128)} %get-tuple-element.118), channel_id=1, source_target_pairs={{0,3},{1,0},{2,1},{3,2},{4,7},{5,4},{6,5},{7,6},{8,11},{9,8},{10,9... | collective-permute-start | bytes 294920 | tf_op jit(solution)/shard_map/ppermute | solution.py:31
  133.3 2.4 %all-to-all-done.1 = f32[16,32,384]{2,1,0:T(8,128)S(1)} async-done(((f32[16,32,384]{2,1,0:T(8,128)}), f32[16,32,384]{2,1,0:T(8,128)S(1)}, u32[]{:S(2)}, u32[]{:S(2)}) %all-to-all-start.1) | async-done | bytes 786464 | tf_op jit(solution)/shard_map/all_to_all | solution.py:436
  137.1 2.0 %sum_last.1 = (f32[32,2,16,128]{3,2,1,0:T(8,128)}, f32[16,16,128]{2,1,0:T(8,128)}, f32[8,16,128]{2,1,0:T(8,128)}, f32[8,16,128]{2,1,0:T(8,128)}) custom-call(s32[5]{0:T(128)} %stack.23.place, f32[64,384]{1,0:T(8,128)} %get-tuple-element.115.refs_0_, f32[64,384]{1,0:T(8,128)} %copy-done.23, f32[64,384]{1,0:T(8,128)} %copy-done.24, f32[64,384]{1,0:T(8,128)} %copy-done.25, ...), custom_call_target="tpu_custom_call" | custom-call | tf_op jit(solution)/shard_map/sum_last/pallas_call | solution.py:382
  139.1 7.1 %all-to-all-start.2 = ((f32[32,2,16,128]{3,2,1,0:T(8,128)}), f32[32,2,16,128]{3,2,1,0:T(8,128)S(1)}, u32[]{:S(2)}, u32[]{:S(2)}) async-start(f32[32,2,16,128]{3,2,1,0:T(8,128)} %get-tuple-element.120), calls=%async_computation.2 | async-start | bytes 1048576 | tf_op jit(solution)/shard_map/all_to_all | solution.py:450
  147.8 10.4 %all-to-all-done.2.got = f32[32,2,16,128]{3,2,1,0:T(8,128)S(1)} async-done(((f32[32,2,16,128]{3,2,1,0:T(8,128)}), f32[32,2,16,128]{3,2,1,0:T(8,128)S(1)}, u32[]{:S(2)}, u32[]{:S(2)}) %all-to-all-start.2) | async-done | bytes 524320 | tf_op jit(solution)/shard_map/all_to_all | solution.py:450
  161.9 3.8 %collective-permute-start.23 = (f32[32,16,128]{2,1,0:T(8,128)}, f32[32,16,128]{2,1,0:T(8,128)S(1)}, u32[]{:S(2)}, u32[]{:S(2)}) collective-permute-start(f32[32,16,128]{2,1,0:T(8,128)} %select.7.q0), channel_id=1, source_target_pairs={{0,2},{1,3},{2,0},{3,1},{4,6},{5,7},{6,4},{7,5},{8,10},{9,11},{10,... | collective-permute-start | bytes 786440 | tf_op jit(solution)/shard_map/ppermute | solution.py:31
  166.8 6.0 %collective-permute-done.22.q1 = f32[32,16,128]{2,1,0:T(8,128)S(1)} collective-permute-done((f32[32,16,128]{2,1,0:T(8,128)}, f32[32,16,128]{2,1,0:T(8,128)S(1)}, u32[]{:S(2)}, u32[]{:S(2)}) %collective-permute-start.22) | collective-permute-done | bytes 262176 | tf_op jit(solution)/shard_map/ppermute | solution.py:31
  172.8 5.6 %collective-permute-done.23.q2 = f32[32,16,128]{2,1,0:T(8,128)S(1)} collective-permute-done((f32[32,16,128]{2,1,0:T(8,128)}, f32[32,16,128]{2,1,0:T(8,128)S(1)}, u32[]{:S(2)}, u32[]{:S(2)}) %collective-permute-start.23) | collective-permute-done | bytes 262176 | tf_op jit(solution)/shard_map/ppermute | solution.py:31
  179.8 2.8 %assemble.1 = (f32[64,2048]{1,0:T(8,128)}, f32[128,1024]{1,0:T(8,128)}) custom-call(s32[5]{0:T(128)} %stack.23.place, f32[32,16,128]{2,1,0:T(8,128)} %select.7.q0, f32[32,16,128]{2,1,0:T(8,128)} %copy-done.13, f32[32,16,128]{2,1,0:T(8,128)} %copy-done.14, f32[32,16,128]{2,1,0:T(8,128)} %copy-done.15), custom_call_target="tpu_custom_call" | custom-call | tf_op jit(solution)/shard_map/assemble/pallas_call | solution.py:382
  (102 shorter events, 31.8 us)
Async XLA Ops:
  0.6 22.2 %collective-permute-start = (f32[12,1024,128]{2,1,0:T(8,128)}, f32[12,1024,128]{2,1,0:T(8,128)}, u32[]{:S(2)}, u32[]{:S(2)}) collective-permute-start(f32[12,1024,128]{2,1,0:T(8,128)} %own.1), channel_id=1, source_target_pairs={{0,64},{64,0},{1,65},{65,1},{2,66},{66,2},{3,67},{67,3},{4,68},{68... | collective-permute-start | bytes 18874376 | tf_op jit(solution)/shard_map/ppermute | solution.py:401
  9.1 3.1 %collective-permute-start.1 = (f32[128,1536]{1,0:T(8,128)}, f32[128,1536]{1,0:T(8,128)S(1)}, u32[]{:S(2)}, u32[]{:S(2)}) collective-permute-start(f32[128,1536]{1,0:T(8,128)} %get-tuple-element.66), channel_id=1, source_target_pairs={{0,64},{64,0},{1,65},{65,1},{2,66},{66,2},{3,67},{67,3},{4,68},{68... | collective-permute-start | bytes 2359304 | tf_op jit(solution)/shard_map/ppermute | solution.py:404
  15.5 28.5 %all-to-all-start = ((f32[16,8,1536]{2,1,0:T(8,128)}), f32[16,8,1536]{2,1,0:T(8,128)S(1)}, u32[]{:S(2)}, u32[]{:S(2)}) async-start(f32[16,8,1536]{2,1,0:T(8,128)} %bitcast.8), calls=%async_computation | async-start | bytes 1572864 | tf_op jit(solution)/shard_map/all_to_all | solution.py:406
  44.0 5.3 %collective-permute-start.3 = (f32[16,8,1536]{2,1,0:T(8,128)S(1)}, f32[16,8,1536]{2,1,0:T(8,128)S(1)}, u32[]{:S(2)}, u32[]{:S(2)}) collective-permute-start(f32[16,8,1536]{2,1,0:T(8,128)S(1)} %all-to-all-done.own), channel_id=1, source_target_pairs={{0,64},{64,0},{1,65},{65,1},{2,66},{66,2},{3,67},{67,3},{4,68},{68... | collective-permute-start | bytes 2359304 | tf_op jit(solution)/shard_map/ppermute | solution.py:416
  44.1 12.8 %collective-permute-start.2 = (f32[2,16,16,384]{3,2,1,0:T(8,128)}, f32[2,16,16,384]{3,2,1,0:T(8,128)S(1)}, u32[]{:S(2)}, u32[]{:S(2)}) collective-permute-start(f32[2,16,16,384]{3,2,1,0:T(8,128)} %get-tuple-element.74), channel_id=1, source_target_pairs={{0,1},{1,0},{2,3},{3,2},{4,5},{5,4},{6,7},{7,6},{8,9},{9,8},{10,11... | collective-permute-start | bytes 2359304 | tf_op jit(solution)/shard_map/ppermute | solution.py:49
  46.1 25.5 %collective-permute-start.5 = (f32[2,4,96,384]{3,2,1,0:T(8,128)}, f32[2,4,96,384]{3,2,1,0:T(8,128)S(1)}, u32[]{:S(2)}, u32[]{:S(2)}) collective-permute-start(f32[2,4,96,384]{3,2,1,0:T(8,128)} %get-tuple-element.79), channel_id=1, source_target_pairs={{0,4},{1,5},{2,6},{3,7},{4,0},{5,1},{6,2},{7,3},{8,12},{9,13},{10,... | collective-permute-start | bytes 3538952 | tf_op jit(solution)/shard_map/ppermute | solution.py:49
  47.8 23.8 %collective-permute-start.7 = (f32[2,4,96,384]{3,2,1,0:T(8,128)}, f32[2,4,96,384]{3,2,1,0:T(8,128)S(1)}, u32[]{:S(2)}, u32[]{:S(2)}) collective-permute-start(f32[2,4,96,384]{3,2,1,0:T(8,128)} %get-tuple-element.83), channel_id=1, source_target_pairs={{0,16},{1,17},{2,18},{3,19},{4,20},{5,21},{6,22},{7,23},{8,24},{9,... | collective-permute-start | bytes 3538952 | tf_op jit(solution)/shard_map/ppermute | solution.py:49
  56.1 12.3 %collective-permute-start.4 = (f32[2,16,16,384]{3,2,1,0:T(8,128)}, f32[2,16,16,384]{3,2,1,0:T(8,128)S(1)}, u32[]{:S(2)}, u32[]{:S(2)}) collective-permute-start(f32[2,16,16,384]{3,2,1,0:T(8,128)} %get-tuple-element.77), channel_id=1, source_target_pairs={{0,1},{1,0},{2,3},{3,2},{4,5},{5,4},{6,7},{7,6},{8,9},{9,8},{10,11... | collective-permute-start | bytes 2359304 | tf_op jit(solution)/shard_map/ppermute | solution.py:49
  56.2 15.4 %collective-permute-start.6 = (f32[2,4,64,384]{3,2,1,0:T(8,128)}, f32[2,4,64,384]{3,2,1,0:T(8,128)S(1)}, u32[]{:S(2)}, u32[]{:S(2)}) collective-permute-start(f32[2,4,64,384]{3,2,1,0:T(8,128)} %get-tuple-element.81), channel_id=1, source_target_pairs={{0,4},{1,5},{2,6},{3,7},{4,0},{5,1},{6,2},{7,3},{8,12},{9,13},{10,... | collective-permute-start | bytes 2359304 | tf_op jit(solution)/shard_map/ppermute | solution.py:49
  56.9 11.5 %copy-start.4 = (f32[2,16,16,384]{3,2,1,0:T(8,128)}, f32[2,16,16,384]{3,2,1,0:T(8,128)S(1)}, u32[]{:S(2)}) copy-start(f32[2,16,16,384]{3,2,1,0:T(8,128)S(1)} %collective-permute-done.2.refs_1_) | copy-start | bytes 2359300
  56.9 15.8 %collective-permute-start.8 = (f32[2,4,64,384]{3,2,1,0:T(8,128)}, f32[2,4,64,384]{3,2,1,0:T(8,128)S(1)}, u32[]{:S(2)}, u32[]{:S(2)}) collective-permute-start(f32[2,4,64,384]{3,2,1,0:T(8,128)} %get-tuple-element.85), channel_id=1, source_target_pairs={{0,16},{1,17},{2,18},{3,19},{4,20},{5,21},{6,22},{7,23},{8,24},{9,... | collective-permute-start | bytes 2359304 | tf_op jit(solution)/shard_map/ppermute | solution.py:49
  76.1 15.6 %collective-permute-start.13 = (f32[4,160,384]{2,1,0:T(8,128)}, f32[4,160,384]{2,1,0:T(8,128)S(1)}, u32[]{:S(2)}, u32[]{:S(2)}) collective-permute-start(f32[4,160,384]{2,1,0:T(8,128)} %add.11), channel_id=1, source_target_pairs={{0,48},{1,49},{2,50},{3,51},{4,52},{5,53},{6,54},{7,55},{8,56},{9,... | collective-permute-start | bytes 2949128 | tf_op jit(solution)/shard_map/ppermute | solution.py:49
  81.4 15.5 %collective-permute-start.9 = (f32[4,160,384]{2,1,0:T(8,128)}, f32[4,160,384]{2,1,0:T(8,128)S(1)}, u32[]{:S(2)}, u32[]{:S(2)}) collective-permute-start(f32[4,160,384]{2,1,0:T(8,128)} %add.10), channel_id=1, source_target_pairs={{0,12},{1,13},{2,14},{3,15},{4,8},{5,9},{6,10},{7,11},{8,4},{9,5},... | collective-permute-start | bytes 2949128 | tf_op jit(solution)/shard_map/ppermute | solution.py:49
  83.5 26.2 %collective-permute-start.17 = (f32[16,32,384]{2,1,0:T(8,128)S(1)}, f32[16,32,384]{2,1,0:T(8,128)S(1)}, u32[]{:S(2)}, u32[]{:S(2)}) collective-permute-start(f32[16,32,384]{2,1,0:T(8,128)S(1)} %copy-done.12), channel_id=1, source_target_pairs={{0,3},{1,2},{2,1},{3,0},{4,7},{5,6},{6,5},{7,4},{8,11},{9,10},{10,... | collective-permute-start | bytes 2359304 | tf_op jit(solution)/shard_map/ppermute | solution.py:49
  95.6 10.5 %collective-permute-start.14 = (f32[160,384]{1,0:T(8,128)}, f32[160,384]{1,0:T(8,128)S(1)}, u32[]{:S(2)}, u32[]{:S(2)}) collective-permute-start(f32[160,384]{1,0:T(8,128)} %get-tuple-element.102), channel_id=1, source_target_pairs={{0,4},{1,5},{2,6},{3,7},{4,8},{5,9},{6,10},{7,11},{8,12},{9,13},{1... | collective-permute-start | bytes 737288 | tf_op jit(solution)/shard_map/ppermute | solution.py:31
  100.8 7.6 %collective-permute-start.10 = (f32[160,384]{1,0:T(8,128)}, f32[160,384]{1,0:T(8,128)S(1)}, u32[]{:S(2)}, u32[]{:S(2)}) collective-permute-start(f32[160,384]{1,0:T(8,128)} %get-tuple-element.92), channel_id=1, source_target_pairs={{0,16},{1,17},{2,18},{3,19},{4,20},{5,21},{6,22},{7,23},{8,24},{9,... | collective-permute-start | bytes 737288 | tf_op jit(solution)/shard_map/ppermute | solution.py:31
  101.0 12.1 %collective-permute-start.15 = (f32[160,384]{1,0:T(8,128)S(1)}, f32[160,384]{1,0:T(8,128)S(1)}, u32[]{:S(2)}, u32[]{:S(2)}) collective-permute-start(f32[160,384]{1,0:T(8,128)S(1)} %copy-done.29), channel_id=1, source_target_pairs={{0,12},{1,13},{2,14},{3,15},{4,0},{5,1},{6,2},{7,3},{8,4},{9,5},{1... | collective-permute-start | bytes 737288 | tf_op jit(solution)/shard_map/ppermute | solution.py:31
  103.1 10.1 %collective-permute-start.11 = (f32[160,384]{1,0:T(8,128)}, f32[160,384]{1,0:T(8,128)S(1)}, u32[]{:S(2)}, u32[]{:S(2)}) collective-permute-start(f32[160,384]{1,0:T(8,128)} %get-tuple-element.94), channel_id=1, source_target_pairs={{0,48},{1,49},{2,50},{3,51},{4,52},{5,53},{6,54},{7,55},{8,56},{9,... | collective-permute-start | bytes 737288 | tf_op jit(solution)/shard_map/ppermute | solution.py:31
  106.1 16.8 %copy-start.16 = (f32[160,384]{1,0:T(8,128)}, f32[160,384]{1,0:T(8,128)S(1)}, u32[]{:S(2)}) copy-start(f32[160,384]{1,0:T(8,128)S(1)} %collective-permute-done.14.refs_5_) | copy-start | bytes 737284
  106.1 8.1 %collective-permute-start.16 = (f32[160,384]{1,0:T(8,128)S(1)}, f32[160,384]{1,0:T(8,128)S(1)}, u32[]{:S(2)}, u32[]{:S(2)}) collective-permute-start(f32[160,384]{1,0:T(8,128)S(1)} %copy-done.28), channel_id=1, source_target_pairs={{0,8},{1,9},{2,10},{3,11},{4,12},{5,13},{6,14},{7,15},{8,0},{9,1},... | collective-permute-start | bytes 737288 | tf_op jit(solution)/shard_map/ppermute | solution.py:31
  108.4 14.5 %copy-start.17 = (f32[160,384]{1,0:T(8,128)}, f32[160,384]{1,0:T(8,128)S(1)}, u32[]{:S(2)}) copy-start(f32[160,384]{1,0:T(8,128)S(1)} %collective-permute-done.10.refs_1_) | copy-start | bytes 737284
  108.4 8.1 %collective-permute-start.12 = (f32[160,384]{1,0:T(8,128)}, f32[160,384]{1,0:T(8,128)S(1)}, u32[]{:S(2)}, u32[]{:S(2)}) collective-permute-start(f32[160,384]{1,0:T(8,128)} %get-tuple-element.95), channel_id=1, source_target_pairs={{0,32},{1,33},{2,34},{3,35},{4,36},{5,37},{6,38},{7,39},{8,40},{9,... | collective-permute-start | bytes 737288 | tf_op jit(solution)/shard_map/ppermute | solution.py:31
  116.5 19.3 %all-to-all-start.1 = ((f32[16,32,384]{2,1,0:T(8,128)}), f32[16,32,384]{2,1,0:T(8,128)S(1)}, u32[]{:S(2)}, u32[]{:S(2)}) async-start(f32[16,32,384]{2,1,0:T(8,128)} %sum_first.5), calls=%async_computation.1 | async-start | bytes 1572864 | tf_op jit(solution)/shard_map/all_to_all | solution.py:436
  125.4 11.0 %collective-permute-start.18 = (f32[64,384]{1,0:T(8,128)}, f32[64,384]{1,0:T(8,128)S(1)}, u32[]{:S(2)}, u32[]{:S(2)}) collective-permute-start(f32[64,384]{1,0:T(8,128)} %get-tuple-element.116), channel_id=1, source_target_pairs={{0,1},{1,2},{2,3},{3,0},{4,5},{5,6},{6,7},{7,4},{8,9},{9,10},{10,1... | collective-permute-start | bytes 294920 | tf_op jit(solution)/shard_map/ppermute | solution.py:31
  125.6 10.8 %collective-permute-start.19 = (f32[64,384]{1,0:T(8,128)}, f32[64,384]{1,0:T(8,128)S(1)}, u32[]{:S(2)}, u32[]{:S(2)}) collective-permute-start(f32[64,384]{1,0:T(8,128)} %get-tuple-element.117), channel_id=1, source_target_pairs={{0,2},{1,3},{2,0},{3,1},{4,6},{5,7},{6,4},{7,5},{8,10},{9,11},{10,... | collective-permute-start | bytes 294920 | tf_op jit(solution)/shard_map/ppermute | solution.py:31
  131.3 5.1 %collective-permute-start.20 = (f32[64,384]{1,0:T(8,128)}, f32[64,384]{1,0:T(8,128)S(1)}, u32[]{:S(2)}, u32[]{:S(2)}) collective-permute-start(f32[64,384]{1,0:T(8,128)} %get-tuple-element.118), channel_id=1, source_target_pairs={{0,3},{1,0},{2,1},{3,2},{4,7},{5,4},{6,5},{7,6},{8,11},{9,8},{10,9... | collective-permute-start | bytes 294920 | tf_op jit(solution)/shard_map/ppermute | solution.py:31
  137.1 29.0 %copy-start.22 = (f32[64,384]{1,0:T(8,128)S(1)}, f32[64,384]{1,0:T(8,128)}, u32[]{:S(2)}) copy-start(f32[64,384]{1,0:T(8,128)} %get-tuple-element.126) | copy-start | bytes 294916
  139.1 19.1 %all-to-all-start.2 = ((f32[32,2,16,128]{3,2,1,0:T(8,128)}), f32[32,2,16,128]{3,2,1,0:T(8,128)S(1)}, u32[]{:S(2)}, u32[]{:S(2)}) async-start(f32[32,2,16,128]{3,2,1,0:T(8,128)} %get-tuple-element.120), calls=%async_computation.2 | async-start | bytes 1048576 | tf_op jit(solution)/shard_map/all_to_all | solution.py:450
  146.3 1.5 collective-permute-start.21
  161.0 11.8 %collective-permute-start.22 = (f32[32,16,128]{2,1,0:T(8,128)}, f32[32,16,128]{2,1,0:T(8,128)S(1)}, u32[]{:S(2)}, u32[]{:S(2)}) collective-permute-start(f32[32,16,128]{2,1,0:T(8,128)} %select.7.q0), channel_id=1, source_target_pairs={{0,1},{1,2},{2,3},{3,0},{4,5},{5,6},{6,7},{7,4},{8,9},{9,10},{10,1... | collective-permute-start | bytes 786440 | tf_op jit(solution)/shard_map/ppermute | solution.py:31
  161.9 16.6 %collective-permute-start.23 = (f32[32,16,128]{2,1,0:T(8,128)}, f32[32,16,128]{2,1,0:T(8,128)S(1)}, u32[]{:S(2)}, u32[]{:S(2)}) collective-permute-start(f32[32,16,128]{2,1,0:T(8,128)} %select.7.q0), channel_id=1, source_target_pairs={{0,2},{1,3},{2,0},{3,1},{4,6},{5,7},{6,4},{7,5},{8,10},{9,11},{10,... | collective-permute-start | bytes 786440 | tf_op jit(solution)/shard_map/ppermute | solution.py:31
  165.7 12.8 %collective-permute-start.24 = (f32[32,16,128]{2,1,0:T(8,128)}, f32[32,16,128]{2,1,0:T(8,128)S(1)}, u32[]{:S(2)}, u32[]{:S(2)}) collective-permute-start(f32[32,16,128]{2,1,0:T(8,128)} %select.7.q0), channel_id=1, source_target_pairs={{0,3},{1,0},{2,1},{3,2},{4,7},{5,4},{6,5},{7,6},{8,11},{9,8},{10,9... | collective-permute-start | bytes 786440 | tf_op jit(solution)/shard_map/ppermute | solution.py:31
  (26 other events, 100.0 us)

commit v4 on v3

--- a/solution.py
+++ b/solution.py
@@ -72,7 +72,7 @@
     return dot(a_high, b_high) + (dot(a_high, b_low) + dot(a_low, b_high))
 
 
-def project_kernel(place, field, basis, own, other, land, x_land, x_high, x_low, f_high, f_low, sems):
+def project_kernel(place, field, basis, own, other, both, land, x_land, x_high, x_low, f_high, f_low, sems):
     def load(k):
         part = pl.ds(k * 2, 2)
         return pltpu.make_async_copy(field.at[part], land.at[part], sems.at[k])
@@ -93,6 +93,9 @@
     out = dot3(x_high[...], x_low[...], f_high[...], f_low[...], ((1,), (0,)))
     own[...] = out[:128]
     other[...] = out[128:]
+    for j in range(16):
+        both[j, :8] = out[j * 8 : j * 8 + 8]
+        both[j, 8:] = out[128 + j * 8 : 136 + j * 8]
 
 
 def project(place, field, basis):
@@ -100,8 +103,8 @@
     return pl.pallas_call(
         project_kernel,
         in_specs=[pl.BlockSpec(memory_space=pltpu.SMEM)] + [pl.BlockSpec(memory_space=pl.ANY)] * 2,
-        out_specs=[pl.BlockSpec(memory_space=pltpu.VMEM)] * 2,
-        out_shape=[out, out],
+        out_specs=[pl.BlockSpec(memory_space=pltpu.VMEM)] * 3,
+        out_shape=[out, out, jax.ShapeDtypeStruct((16, 16, 1536), F32)],
         scratch_shapes=[
             pltpu.VMEM((12, 1024, 128), F32),
             pltpu.VMEM((1024, 256), F32),
@@ -158,7 +161,7 @@
     return copies
 
 
-def gram_x_kernel(place, own, other, reduced, y_basis, *refs):
+def gram_x_kernel(place, own, other, mine, theirs, y_basis, *refs):
     high, low, buf, land, core, out_sems, sems, core_sems = refs[6:]
 
     def load(k):
@@ -170,8 +173,9 @@
         load(k).start()
     y_high, y_low = split(y_basis[...].T)
     for s in range(12):
-        r_high, r_low = split(reduced[:, s * 128 : s * 128 + 128])
-        core[:, s * 128 : s * 128 + 128] = dot3(y_high, y_low, r_high, r_low, ((1,), (1,)))
+        cols = slice(s * 128, s * 128 + 128)
+        r_high, r_low = split(mine[:, cols] + theirs[:, cols])
+        core[:, cols] = dot3(y_high, y_low, r_high, r_low, ((1,), (1,)))
     for copy in core_copies(place, core, refs, core_sems):
         copy.start()
     for k in range(12):
@@ -192,7 +196,11 @@
 def gram_y_kernel(place, own, other, *refs):
     high, low, buf, out_sems = refs[6:]
     for j in range(16):
-        tiles = [src[j, :, s * 128 : s * 128 + 128] for src in (own, other) for s in range(12)]
+        tiles = [
+            own[j, half : half + 8, s * 128 : s * 128 + 128] + other[j, 8 - half : 16 - half, s * 128 : s * 128 + 128]
+            for half in (0, 8)
+            for s in range(12)
+        ]
         v = jnp.concatenate(tiles + [jnp.zeros((64, 128), F32)], axis=0).T
         v_high, v_low = split(v)
         for start in (j * 128, 2048 + j * 128):
@@ -248,72 +256,99 @@
 
 
 def add_kernel(*refs):
-    *terms, out = refs
-    at = 0
-    for kept, came in zip(terms[0::2], terms[1::2]):
-        rows = kept.shape[2]
-        out[:, at : at + rows, :] = kept[0] + came[0]
-        at += rows
+    for i, out in enumerate(refs[12:]):
+        terms = refs[4 * i : 4 * i + 4]
+        at = 0
+        for kept, came in zip(terms[0::2], terms[1::2]):
+            rows = kept.shape[2]
+            out[:, at : at + rows, :] = kept[0] + came[0]
+            at += rows
 
 
 def slab_of(v, k):
     return pl.BlockSpec((1,) + v.shape[1:], lambda i: (k, 0, 0, 0))
 
 
-def add_for_second(terms):
-    shape = (terms[0].shape[1], sum(v.shape[2] for v in terms[0::2]), 384)
+def add_for_second(*thirds):
+    shapes = [(t[0].shape[1], sum(v.shape[2] for v in t[0::2]), 384) for t in thirds]
+    terms = [v for t in thirds for v in t]
     return pl.pallas_call(
         add_kernel,
         grid=(1,),
         in_specs=[slab_of(v, 1) for v in terms],
-        out_specs=pl.BlockSpec(shape, lambda i: (0, 0, 0)),
-        out_shape=jax.ShapeDtypeStruct(shape, F32),
-        compiler_params=pltpu.CompilerParams(vmem_limit_bytes=VMEM_LIMIT),
-        cost_estimate=pl.CostEstimate(flops=200000, bytes_accessed=3000000, transcendentals=0),
+        out_specs=[pl.BlockSpec(shape, lambda i: (0, 0, 0)) for shape in shapes],
+        out_shape=[jax.ShapeDtypeStruct(shape, F32) for shape in shapes],
+        compiler_params=pltpu.CompilerParams(vmem_limit_bytes=VMEM_LIMIT),
+        cost_estimate=pl.CostEstimate(flops=700000, bytes_accessed=9000000, transcendentals=0),
         name="add",
     )(*terms)
 
 
-def sum_first_kernel(axis, place, *refs):
-    terms, last, outs = refs[:4], refs[4], refs[5:]
-    at = 0
-    for kept, came in zip(terms[0::2], terms[1::2]):
-        rows = slice(at, at + kept.shape[2])
-        if axis is None:
-            outs[0][:, rows, :] = (kept[0] + came[0]) + last[:, rows, :]
-        else:
-            for d, out in enumerate(outs):
-                k = ahead(place, axis, d)
-                out[rows, :] = (kept[0, k] + came[0, k]) + last[k, rows, :]
-        at = rows.stop
-
-
-def sum_first(place, axis, terms, last):
-    shapes = [last.shape] if axis is None else [last.shape[1:]] * 4
-    return pl.pallas_call(
-        functools.partial(sum_first_kernel, axis),
+def sum_last_third_kernel(k_x, c_x, k_y, c_y, last, out):
+    out[:, :16, :] = (k_x[0] + c_x[0]) + last[:, :16, :]
+    out[:, 16:, :] = (k_y[0] + c_y[0]) + last[:, 16:, :]
+
+
+def sum_last_third(terms, last):
+    whole = pl.BlockSpec(last.shape, lambda i: (0, 0, 0))
+    return pl.pallas_call(
+        sum_last_third_kernel,
+        grid=(1,),
+        in_specs=[slab_of(v, 0) for v in terms] + [whole],
+        out_specs=whole,
+        out_shape=jax.ShapeDtypeStruct(last.shape, F32),
+        compiler_params=pltpu.CompilerParams(vmem_limit_bytes=VMEM_LIMIT),
+        cost_estimate=pl.CostEstimate(flops=1000000, bytes_accessed=4000000, transcendentals=0),
+        name="sum_last_third",
+    )(*terms, last)
+
+
+def sum_first_kernel(place, *refs):
+    for third, axis in enumerate((2, 1)):
+        k_x, c_x, k_y, c_y, last = refs[5 * third : 5 * third + 5]
+        outs = refs[10 + 2 * third : 12 + 2 * third]
+        for sent, slot, mask in owner_masks(place):
+            k = place[axis] ^ mask
+            outs[sent][slot, :96, :] = (k_x[0, k] + c_x[0, k]) + last[k, :96, :]
+            outs[sent][slot, 96:, :] = (k_y[0, k] + c_y[0, k]) + last[k, 96:, :]
+
+
+def sum_first(place, terms_a, last_a, terms_b, last_b):
+    whole = pl.BlockSpec(last_a.shape, lambda i: (0, 0, 0))
+    shape = (2, 160, 384)
+    return pl.pallas_call(
+        sum_first_kernel,
         grid=(1,),
         in_specs=[pl.BlockSpec(memory_space=pltpu.SMEM)]
-        + [slab_of(v, 0) for v in terms]
-        + [pl.BlockSpec(last.shape, lambda i: (0, 0, 0))],
-        out_specs=[pl.BlockSpec(out, lambda i, n=len(out): (0,) * n) for out in shapes],
-        out_shape=[jax.ShapeDtypeStruct(out, F32) for out in shapes],
-        compiler_params=pltpu.CompilerParams(vmem_limit_bytes=VMEM_LIMIT),
-        cost_estimate=pl.CostEstimate(flops=1000000, bytes_accessed=4000000, transcendentals=0),
+        + [slab_of(v, 0) for v in terms_a] + [whole]
+        + [slab_of(v, 0) for v in terms_b] + [whole],
+        out_specs=[pl.BlockSpec(shape, lambda i: (0, 0, 0))] * 4,
+        out_shape=[jax.ShapeDtypeStruct(shape, F32)] * 4,
+        compiler_params=pltpu.CompilerParams(vmem_limit_bytes=VMEM_LIMIT),
+        cost_estimate=pl.CostEstimate(flops=1000000, bytes_accessed=8000000, transcendentals=0),
         name="sum_first",
-    )(place, *terms, last)
+    )(place, *terms_a, last_a, *terms_b, last_b)
+
+
+def add_second_kernel(place, k_a, c_a, k_b, c_b, out_a, out_b):
+    out_a[...] = k_a[1] + c_a[1]
+    out_b[...] = k_b[1] + c_b[1]
 
 
 def sum_second_kernel(place, *refs):
-    outs = refs[8:]
+    outs = refs[6:]
     for part in range(2):
-        terms = refs[part * 4 : part * 4 + 4]
+        kept, came, last = refs[part * 3 : part * 3 + 3]
+
+        def total(rows):
+            return (kept[0, rows, :] + came[0, rows, :]) + last[rows, :]
+
         for d in range(4):
             for g in range(2):
+                to = part * 32 + g * 16
                 rows = pl.ds(pl.multiple_of(g * 96 + ahead(place, 3, d) * 16, 16), 16)
-                to = part * 32 + g * 16
-                outs[d][to : to + 16, :] = sum4(terms, (rows, slice(None)))
-        outs[4][part * 32 : part * 32 + 32, :] = sum4(terms, (slice(64, 96), slice(None)))
+                outs[d][to : to + 16, :] = total(rows)
+        outs[4][part * 32 : part * 32 + 32, :] = total(slice(64, 96))
 
 
 def sum_last_kernel(place, *refs):
@@ -330,10 +365,10 @@
         to_x, to_y = lax.rem(block_x + k, 16), lax.rem(j + k, 16)
         direct_x[to_x] = tile_x
         wide[lax.rem(to_y + 8 * h, 16)] = tile_y
-        slots[2 * to_x, 0] = tile_x
-        slots[2 * to_x + 1, 0] = tile_x
-        slots[to_y, 1] = tile_y
-        slots[16 + to_y, 1] = tile_y
+        for e in range(2):
+            half = tile_x[:, e * 64 : e * 64 + 64]
+            slots[2 * to_x + e, 16:] = jnp.concatenate([half[:8], half[8:]], axis=1)
+            slots[16 * e + to_y, :16] = tile_y
     keep[...] = wide[:8]
     give[...] = wide[8:]
 
@@ -343,24 +378,25 @@
     j = place[2] * 4 + place[1]
     block_x = h * 8 + j // 2
     for block in range(16):
-        first, second = got[2 * block, 0], got[2 * block + 1, 0]
-        even = jnp.concatenate([first[:, :64], second[:, :64]], axis=1)
-        odd = jnp.concatenate([first[:, 64:], second[:, 64:]], axis=1)
-        turned = jnp.where(lax.rem(j, 2) == 0, even, odd)
+        first, second = got[2 * block, 16:], got[2 * block + 1, 16:]
+        turned = jnp.concatenate(
+            [jnp.concatenate([t[:, :64] for t in (first, second)], axis=1), jnp.concatenate([t[:, 64:] for t in (first, second)], axis=1)],
+            axis=0,
+        )
         out[block] = jnp.where(lax.rem(block - block_x + 16, 16) <= 8, direct_x[block], turned)
     for block in range(8):
         is_direct = lax.rem(h * 8 + block - j + 16, 16) <= 8
         for half in range(2):
             direct = jnp.where(h == half, keep[block], come[block])
-            out[16 + 2 * block + half] = jnp.where(is_direct, direct, got[half * 16 + h * 8 + block, 1])
+            out[16 + 2 * block + half] = jnp.where(is_direct, direct, got[half * 16 + h * 8 + block, :16])
 
 
 def assemble_kernel(scale_x, scale_y, place, q0, q1, q2, q3, gram_x, gram_y, rows):
     h = place[0]
     j = place[2] * 4 + place[1]
     block_x = h * 8 + j // 2
-    for d, quarter in enumerate((q0, q1, q2, q3)):
-        z = ahead(place, 3, 4 - d)
+    for quarter, mask in zip((q0, q1, q2, q3), (0, place[4], 4 - place[4], 2)):
+        z = place[3] ^ mask
         rows[:, pl.ds(pl.multiple_of(z * 16, 16), 16), :] = quarter[...]
     for block in range(16):
         direct = rows[block]
@@ -374,10 +410,6 @@
         gram_y[:, block * 128 : block * 128 + 128] = jnp.where(is_direct, direct, direct.T) * scale_y
 
 
-def add_two_kernel(place, first, second, out):
-    out[...] = first[...] + second[...]
-
-
 def small_kernel(kernel, name, out_shape, scratch, *args):
     return pl.pallas_call(
         kernel,
@@ -399,18 +431,16 @@
     ranks = x_mode_basis.shape[1]
 
     other_field = lax.ppermute(species_field, "gx", SWAP)
-    mine, theirs = project(place, species_field, x_mode_basis)
-    reduced = small_kernel(
-        add_two_kernel, "add_two", jax.ShapeDtypeStruct((128, 1536), F32), [], place, mine, lax.ppermute(theirs, "gx", SWAP)
-    )
-    fibers = lax.all_to_all(reduced.reshape(16, 8, 1536), "gy", 0, 0, tiled=True)
+    mine, give, both = project(place, species_field, x_mode_basis)
+    theirs = lax.ppermute(give, "gx", SWAP)
+    fibers = lax.all_to_all(both, "gy", 0, 0, tiled=True)
 
     def first_swaps(pieces):
         return [swap(pieces[2 * i + 1], 0) for i, swap in enumerate((swap_x, swap_y, swap_z))]
 
     px = gram_pieces(
-        gram_x_kernel, "gram_x", 96, place, (species_field, other_field, reduced, y_mode_basis),
-        (pl.ANY, pl.ANY, pltpu.VMEM, pltpu.VMEM), GRAM_X_SCRATCH, 12000000000,
+        gram_x_kernel, "gram_x", 96, place, (species_field, other_field, mine, theirs, y_mode_basis),
+        (pl.ANY, pl.ANY, pltpu.VMEM, pltpu.VMEM, pltpu.VMEM), GRAM_X_SCRATCH, 12000000000,
     )
     px, fibers = lax.optimization_barrier((px, fibers))
     other_fibers = lax.ppermute(fibers, "gx", SWAP)
@@ -420,28 +450,25 @@
     )
     came_y = first_swaps(py)
 
-    def ring(terms, shift):
-        up, down = shift(terms[1], 1), shift(terms[3], 3)
-        far, up = lax.optimization_barrier((terms[2], up))
-        return [terms[0], up, down, shift(far, 2)]
-
     terms_a, terms_b, terms_c = [(px[2 * i], came_x[i], py[2 * i], came_y[i]) for i in range(3)]
-    add_c = add_for_second(terms_c)
-    add_c, terms_a, terms_b = lax.optimization_barrier((add_c, terms_a, terms_b))
-    (c,) = sum_first(place, None, terms_c, swap_z(add_c, 1))
-    a = sum_first(place, 2, terms_a, swap_x(add_for_second(terms_a), 1))
-    b = sum_first(place, 1, terms_b, swap_y(add_for_second(terms_b), 1))
-    a, b = ring(a, shift_y), ring(b, shift_x)
-    a, b, c = lax.optimization_barrier((a, b, c))
-    c = lax.all_to_all(c, "gy", 0, 0, tiled=True).sum(axis=0)
+    last_a, last_b, last_c = add_for_second(terms_a, terms_b, terms_c)
+    kept_a, sent_a, kept_b, sent_b = sum_first(place, terms_a, swap_x(last_a, 1), terms_b, swap_y(last_b, 1))
+    came_a, came_b = swap_y(sent_a, 0), swap_x(sent_b, 0)
+    last_c, kept_a = lax.optimization_barrier((swap_z(last_c, 1), kept_a))
+    c = lax.all_to_all(sum_last_third(terms_c, last_c), "gy", 0, 0, tiled=True).sum(axis=0)
+    second = jax.ShapeDtypeStruct((160, 384), F32)
+    last_a, last_b = small_kernel(
+        add_second_kernel, "add_second", [second] * 2, [], place, kept_a, came_a, kept_b, came_b
+    )
     part = jax.ShapeDtypeStruct((64, 384), F32)
     *quarters, core = small_kernel(
-        sum_second_kernel, "sum_second", [part] * 5, [], place, *a, *b
+        sum_second_kernel, "sum_second", [part] * 5, [],
+        place, kept_a, came_a, swap_y(last_a, 1), kept_b, came_b, swap_x(last_b, 1),
     )
     blocks = jax.ShapeDtypeStruct((8, 16, 128), F32)
     slots, direct_x, keep, give = small_kernel(
         sum_last_kernel, "sum_last",
-        [jax.ShapeDtypeStruct((32, 2, 16, 128), F32), jax.ShapeDtypeStruct((16, 16, 128), F32), blocks, blocks],
+        [jax.ShapeDtypeStruct((32, 24, 128), F32), jax.ShapeDtypeStruct((16, 16, 128), F32), blocks, blocks],
         [pltpu.VMEM((16, 16, 128), F32)],
         place, *[quarters[0]] + [shift_z(quarters[d], d) for d in (1, 2, 3)], c,
     )
@@ -452,7 +479,8 @@
     part = small_kernel(
         select_kernel, "select", jax.ShapeDtypeStruct((32, 16, 128), F32), [], place, got, direct_x, keep, come
     )
-    quarters = [part] + [shift_z(part, d) for d in (1, 2, 3)]
+    first = swap_z(part, 0)
+    quarters = [part, first, swap_z(part, 1), swap_z(first, 1)]
     gram_x, gram_y = small_kernel(
         functools.partial(assemble_kernel, 1.0 / (ny * slices), 1.0 / (ranks * slices)),
         "assemble",

time: 183 us -> 176 us (0.962)
  starting transfers between devices: 58.2 us -> 50.7 us
  waiting for transfers between devices: 50 us -> 54.9 us
  Pallas kernels: 62.1 us -> 58.2 us
    ppermute x9 -> x16, waiting for transfers between devices: 17.5 us -> 39.7 us  [swap(): return lax.ppermute(v, ('gx', 'gy', 'gz'), pairs)]
    ppermute x12 -> x3, starting transfers between devices: 21.5 us -> 5.49 us  [step(): return lax.ppermute(v, ('gx', 'gy', 'gz'), pairs)]
    ppermute x12 -> x3, waiting for transfers between devices: 15.8 us -> 2.29 us  [step(): return lax.ppermute(v, ('gx', 'gy', 'gz'), pairs)]
    ppermute x9 -> x16, starting transfers between devices: 14.8 us -> 25 us  [swap(): return lax.ppermute(v, ('gx', 'gy', 'gz'), pairs)]
    pallas_call x3 -> x1, Pallas kernels: 7.38 us -> 4.18 us  [add_for_second(): pl.pallas_call(add_kernel, grid=(1,), in_specs=[slab_of(v, 1) for v in te...]
    ppermute x1, waiting for transfers between devices: 2.6 us -> 0.01 us  [per_device(): theirs = lax.ppermute(give, 'gx', SWAP)]
    all_to_all x1, starting transfers between devices: 7.14 us -> 5.24 us  [per_device(): got = lax.all_to_all(slots, ('gx', 'gy'), 0, 0, tiled=True)]
    pallas_call x3 -> x2, Pallas kernels: 8.47 us -> 6.87 us  [the longest x1 4.25 us: sum_first(): pl.pallas_call(sum_first_kernel, grid=(1,), in_specs=[pl.BlockSpec(memory...]
  transfers between devices with their start and end apart: 28 -> 26, of which waited for: 13 -> 13; matrix products, arithmetic and copies ran while one was open for 1% -> 1% of each run, Pallas kernels for 29% -> 27%
where the time goes in v4:
time: 176 us; the launch traced here: 175 us
  Pallas kernels  58.2 us (33%)
  waiting for transfers between devices  54.9 us (31%)
  starting transfers between devices  50.7 us (29%)
  local copies, waits for them, and re-layouts  10.1 us (6%)
    ppermute x16, waiting for transfers between devices, swap(): return lax.ppermute(v, ('gx', 'gy', 'gz'), pairs)  39.7 us
    pallas_call x2, Pallas kernels, gram_pieces(): pl.pallas_call(kernel, in_specs=[pl.BlockSpec(memory_space=space) for spa...  27.7 us
    ppermute x16, starting transfers between devices, swap(): return lax.ppermute(v, ('gx', 'gy', 'gz'), pairs)  25 us
    pallas_call x5, Pallas kernels, small_kernel(): pl.pallas_call(kernel, in_specs=[pl.BlockSpec(memory_space=pltpu.SMEM)] +...  11.3 us
    all_to_all x1, waiting for transfers between devices, per_device(): got = lax.all_to_all(slots, ('gx', 'gy'), 0, 0, tiled=True)  8.98 us
    unnamed x48, local copies, waits for them, and re-layouts  8.72 us
    pallas_call x1, Pallas kernels, project(): pl.pallas_call(project_kernel, in_specs=[pl.BlockSpec(memory_space=pltpu....  8.1 us
    all_to_all x1, starting transfers between devices, per_device(): fibers = lax.all_to_all(both, 'gy', 0, 0, tiled=True)  7.3 us
  transfers between devices with their start and end apart: 26, of which 13 were waited for; matrix products, arithmetic and copies ran while one was open for 1% of the time, Pallas kernels for 27%

profile of v4, /device:TPU:0, one launch (start us, length us, event | category | flops | bytes accessed | tf_op | source)
XLA Modules:
  0.0 175.5 jit_solution(2582896991271970955)
XLA Ops:
  1.4 8.1 %project.1 = (f32[128,1536]{1,0:T(8,128)}, f32[128,1536]{1,0:T(8,128)}, f32[16,16,1536]{2,1,0:T(8,128)}) custom-call(s32[5]{0:T(128)} %stack.23.place, f32[12,1024,128]{2,1,0:T(8,128)} %own.1, f32[1024,256]{1,0:T(8,128)} %basis.1), custom_call_target="tpu_custom_call" | custom-call | flops 2400000000 | bytes 9000000 | tf_op jit(solution)/shard_map/project/pallas_call | solution.py:103
  10.1 7.3 %all-to-all-start = ((f32[16,16,1536]{2,1,0:T(8,128)}), f32[16,16,1536]{2,1,0:T(8,128)S(1)}, u32[]{:S(2)}, u32[]{:S(2)}) async-start(f32[16,16,1536]{2,1,0:T(8,128)} %get-tuple-element.55), calls=%async_computation | async-start | bytes 3145728 | tf_op jit(solution)/shard_map/all_to_all | solution.py:436
  18.3 21.4 %gram_x.1 = (f32[2,4,96,384]{3,2,1,0:T(8,128)}, f32[2,4,96,384]{3,2,1,0:T(8,128)}, f32[2,4,96,384]{3,2,1,0:T(8,128)}, f32[2,4,96,384]{3,2,1,0:T(8,128)}, f32[2,1...) custom-call(s32[5]{0:T(128)} %stack.23.place, f32[12,1024,128]{2,1,0:T(8,128)} %own.1, ...), custom_call_target="tpu_custom_call" | custom-call | flops 12000000000 | bytes 20000000 | tf_op jit(solution)/shard_map/gram_x/pallas_call | solution.py:224
  39.7 2.3 %all-to-all-done.own = f32[16,16,1536]{2,1,0:T(8,128)S(1)} async-done(((f32[16,16,1536]{2,1,0:T(8,128)}), f32[16,16,1536]{2,1,0:T(8,128)S(1)}, u32[]{:S(2)}, u32[]{:S(2)}) %all-to-all-start) | async-done | bytes 1572896 | tf_op jit(solution)/shard_map/all_to_all | solution.py:436
  42.0 1.9 %collective-permute-start.7 = (f32[2,16,16,384]{3,2,1,0:T(8,128)}, f32[2,16,16,384]{3,2,1,0:T(8,128)S(1)}, u32[]{:S(2)}, u32[]{:S(2)}) collective-permute-start(f32[2,16,16,384]{3,2,1,0:T(8,128)} %get-tuple-element.66), channel_id=1, source_target_pairs={{0,1},{1,0},{2,3},{3,2},{4,5},{5,4},{6,7},{7,6},{8,9},{9,8},{10,11... | collective-permute-start | bytes 2359304 | tf_op jit(solution)/shard_map/ppermute | solution.py:49
  45.6 6.3 %gram_y.1 = (f32[2,4,64,384]{3,2,1,0:T(8,128)}, f32[2,4,64,384]{3,2,1,0:T(8,128)}, f32[2,4,64,384]{3,2,1,0:T(8,128)}, f32[2,4,64,384]{3,2,1,0:T(8,128)}, f32[2,1...) custom-call(s32[5]{0:T(128)} %stack.23.place, f32[16,16,1536]{2,1,0:T(8,128)} %copy-done.8, ...), custom_call_target="tpu_custom_call" | custom-call | flops 2400000000 | bytes 20000000 | tf_op jit(solution)/shard_map/gram_y/pallas_call | solution.py:224
  52.4 2.0 %collective-permute-start.6 = (f32[2,4,64,384]{3,2,1,0:T(8,128)}, f32[2,4,64,384]{3,2,1,0:T(8,128)S(1)}, u32[]{:S(2)}, u32[]{:S(2)}) collective-permute-start(f32[2,4,64,384]{3,2,1,0:T(8,128)} %get-tuple-element.64), channel_id=1, source_target_pairs={{0,16},{1,17},{2,18},{3,19},{4,20},{5,21},{6,22},{7,23},{8,24},{9,... | collective-permute-start | bytes 2359304 | tf_op jit(solution)/shard_map/ppermute | solution.py:49
  54.4 1.7 collective-permute-start.8
  56.1 4.2 %collective-permute-done.2.refs_1_ = f32[2,4,96,384]{3,2,1,0:T(8,128)S(1)} collective-permute-done((f32[2,4,96,384]{3,2,1,0:T(8,128)}, f32[2,4,96,384]{3,2,1,0:T(8,128)S(1)}, u32[]{:S(2)}, u32[]{:S(2)}) %collective-permute-start.2) | collective-permute-done | bytes 1179680 | tf_op jit(solution)/shard_map/ppermute | solution.py:49
  60.4 8.4 %collective-permute-done.4.refs_3_ = f32[2,4,64,384]{3,2,1,0:T(8,128)S(1)} collective-permute-done((f32[2,4,64,384]{3,2,1,0:T(8,128)}, f32[2,4,64,384]{3,2,1,0:T(8,128)S(1)}, u32[]{:S(2)}, u32[]{:S(2)}) %collective-permute-start.4) | collective-permute-done | bytes 786464 | tf_op jit(solution)/shard_map/ppermute | solution.py:49
  70.2 4.2 %add.7 = (f32[4,160,384]{2,1,0:T(8,128)}, f32[4,160,384]{2,1,0:T(8,128)}, f32[16,32,384]{2,1,0:T(8,128)}) custom-call(f32[2,4,96,384]{3,2,1,0:T(8,128)} %get-tuple-element.56.refs_0_, f32[2,4,96,384]{3,2,1,0:T(8,128)} %copy-done, f32[2,4,64,384]{3,2,1,0:T(8,128)} %get-tuple-element.59.refs_2_, f32[2,4,64,384]{3,2,1,0:T(8,128)} %copy-done.4, ...), custom_call_target="tpu_custom_call" | custom-call | flops 700000 | bytes 9000000 | tf_op jit(solution)/shard_map/add/pallas_call | solution.py:275
  75.8 2.7 %collective-permute-start.11 = (f32[4,160,384]{2,1,0:T(8,128)}, f32[4,160,384]{2,1,0:T(8,128)S(1)}, u32[]{:S(2)}, u32[]{:S(2)}) collective-permute-start(f32[4,160,384]{2,1,0:T(8,128)} %get-tuple-element.71), channel_id=1, source_target_pairs={{0,48},{1,49},{2,50},{3,51},{4,52},{5,53},{6,54},{7,55},{8,56},{9,... | collective-permute-start | bytes 2949128 | tf_op jit(solution)/shard_map/ppermute | solution.py:49
  78.5 2.5 %collective-permute-start.9 = (f32[16,32,384]{2,1,0:T(8,128)}, f32[16,32,384]{2,1,0:T(8,128)S(1)}, u32[]{:S(2)}, u32[]{:S(2)}) collective-permute-start(f32[16,32,384]{2,1,0:T(8,128)} %get-tuple-element.69), channel_id=1, source_target_pairs={{0,3},{1,2},{2,1},{3,0},{4,7},{5,6},{6,5},{7,4},{8,11},{9,10},{10,... | collective-permute-start | bytes 2359304 | tf_op jit(solution)/shard_map/ppermute | solution.py:49
  81.0 8.9 %collective-permute-done.10.refs_4_ = f32[4,160,384]{2,1,0:T(8,128)S(1)} collective-permute-done((f32[4,160,384]{2,1,0:T(8,128)}, f32[4,160,384]{2,1,0:T(8,128)S(1)}, u32[]{:S(2)}, u32[]{:S(2)}) %collective-permute-start.10) | collective-permute-done | bytes 983072 | tf_op jit(solution)/shard_map/ppermute | solution.py:49
  92.3 4.2 %sum_first.1 = (f32[2,160,384]{2,1,0:T(8,128)}, f32[2,160,384]{2,1,0:T(8,128)}, f32[2,160,384]{2,1,0:T(8,128)}, f32[2,160,384]{2,1,0:T(8,128)}) custom-call(s32[5]{0:T(128)} %stack.23.place, f32[2,4,96,384]{3,2,1,0:T(8,128)} %get-tuple-element.56.refs_0_, f32[2,4,96,384]{3,2,1,0:T(8,128)} %copy-done, f32[2,4,64,384]{3,2,1,0:T(8,128)} %get-tuple-element.59.refs_2_, ...), custom_call_target="tpu_custom_call" | custom-call | flops 1000000 | bytes 8000000 | tf_op jit(solution)/shard_map/sum_first/pallas_call | solution.py:319
  98.3 2.6 %sum_last_third.1 = f32[16,32,384]{2,1,0:T(8,128)} custom-call(f32[2,16,16,384]{3,2,1,0:T(8,128)} %get-tuple-element.65.refs_8_.k_x, f32[2,16,16,384]{3,2,1,0:T(8,128)} %copy-done.2, f32[2,16,16,384]{3,2,1,0:T(8,128)} %get-tuple-element.67.refs_10_.k_y, f32[2,16,16,384]{3,2,1,0:T(8,128)} %copy-done.3, f32[16,32,384]{2,1,0:T(8,128)} %copy-done.12), custom_call_target="tpu_custom_call" | custom-call | flops 1000000 | bytes 4000000 | tf_op jit(solution)/shard_map/sum_last_third/pallas_call | solution.py:294
  100.9 6.7 %all-to-all-start.1 = ((f32[16,32,384]{2,1,0:T(8,128)}), f32[16,32,384]{2,1,0:T(8,128)S(1)}, u32[]{:S(2)}, u32[]{:S(2)}) async-start(f32[16,32,384]{2,1,0:T(8,128)} %sum_last_third.1), calls=%async_computation.1 | async-start | bytes 1572864 | tf_op jit(solution)/shard_map/all_to_all | solution.py:458
  108.7 2.3 %add_second.1 = (f32[160,384]{1,0:T(8,128)}, f32[160,384]{1,0:T(8,128)}) custom-call(s32[5]{0:T(128)} %stack.23.place, f32[2,160,384]{2,1,0:T(8,128)} %get-tuple-element.73.k_a.refs_0_, f32[2,160,384]{2,1,0:T(8,128)} %copy-done.6, f32[2,160,384]{2,1,0:T(8,128)} %get-tuple-element.75.k_b.refs_3_, f32[2,160,384]{2,1,0:T(8,128)} %copy-done.7), custom_call_target="tpu_custom_call" | custom-call | tf_op jit(solution)/shard_map/add_second/pallas_call | solution.py:414
  111.0 3.1 %collective-permute-start.14 = (f32[160,384]{1,0:T(8,128)}, f32[160,384]{1,0:T(8,128)S(1)}, u32[]{:S(2)}, u32[]{:S(2)}) collective-permute-start(f32[160,384]{1,0:T(8,128)} %get-tuple-element.77), channel_id=1, source_target_pairs={{0,48},{1,49},{2,50},{3,51},{4,52},{5,53},{6,54},{7,55},{8,56},{9,... | collective-permute-start | bytes 737288 | tf_op jit(solution)/shard_map/ppermute | solution.py:49
  114.1 2.7 %collective-permute-start.15 = (f32[160,384]{1,0:T(8,128)}, f32[160,384]{1,0:T(8,128)S(1)}, u32[]{:S(2)}, u32[]{:S(2)}) collective-permute-start(f32[160,384]{1,0:T(8,128)} %get-tuple-element.78), channel_id=1, source_target_pairs={{0,12},{1,13},{2,14},{3,15},{4,8},{5,9},{6,10},{7,11},{8,4},{9,5},... | collective-permute-start | bytes 737288 | tf_op jit(solution)/shard_map/ppermute | solution.py:49
  116.8 5.5 %collective-permute-done.14.refs_2_ = f32[160,384]{1,0:T(8,128)S(1)} collective-permute-done((f32[160,384]{1,0:T(8,128)}, f32[160,384]{1,0:T(8,128)S(1)}, u32[]{:S(2)}, u32[]{:S(2)}) %collective-permute-start.14) | collective-permute-done | bytes 245792 | tf_op jit(solution)/shard_map/ppermute | solution.py:49
  123.7 2.4 %sum_second.1 = (f32[64,384]{1,0:T(8,128)}, f32[64,384]{1,0:T(8,128)}, f32[64,384]{1,0:T(8,128)}, f32[64,384]{1,0:T(8,128)}, f32[64,384]{1,0:T(8,128)}) custom-call(s32[5]{0:T(128)} %stack.23.place, f32[2,160,384]{2,1,0:T(8,128)} %get-tuple-element.73.k_a.refs_0_, f32[2,160,384]{2,1,0:T(8,128)} %copy-done.6, f32[160,384]{1,0:T(8,128)} %copy-done.16, ...), custom_call_target="tpu_custom_call" | custom-call | tf_op jit(solution)/shard_map/sum_second/pallas_call | solution.py:414
  126.2 3.3 %collective-permute-start.17 = (f32[64,384]{1,0:T(8,128)}, f32[64,384]{1,0:T(8,128)S(1)}, u32[]{:S(2)}, u32[]{:S(2)}) collective-permute-start(f32[64,384]{1,0:T(8,128)} %get-tuple-element.81), channel_id=1, source_target_pairs={{0,2},{1,3},{2,0},{3,1},{4,6},{5,7},{6,4},{7,5},{8,10},{9,11},{10,... | collective-permute-start | bytes 294920 | tf_op jit(solution)/shard_map/ppermute | solution.py:31
  129.4 2.2 %collective-permute-start.18 = (f32[64,384]{1,0:T(8,128)}, f32[64,384]{1,0:T(8,128)S(1)}, u32[]{:S(2)}, u32[]{:S(2)}) collective-permute-start(f32[64,384]{1,0:T(8,128)} %get-tuple-element.82), channel_id=1, source_target_pairs={{0,3},{1,0},{2,1},{3,2},{4,7},{5,4},{6,5},{7,6},{8,11},{9,8},{10,9... | collective-permute-start | bytes 294920 | tf_op jit(solution)/shard_map/ppermute | solution.py:31
  135.3 2.0 %sum_last.1 = (f32[32,24,128]{2,1,0:T(8,128)}, f32[16,16,128]{2,1,0:T(8,128)}, f32[8,16,128]{2,1,0:T(8,128)}, f32[8,16,128]{2,1,0:T(8,128)}) custom-call(s32[5]{0:T(128)} %stack.23.place, f32[64,384]{1,0:T(8,128)} %get-tuple-element.79.refs_0_, f32[64,384]{1,0:T(8,128)} %copy-done.19, f32[64,384]{1,0:T(8,128)} %copy-done.20, f32[64,384]{1,0:T(8,128)} %copy-done.21, ...), custom_call_target="tpu_custom_call" | custom-call | tf_op jit(solution)/shard_map/sum_last/pallas_call | solution.py:414
  137.3 5.2 %all-to-all-start.2 = ((f32[32,24,128]{2,1,0:T(8,128)}), f32[32,24,128]{2,1,0:T(8,128)S(1)}, u32[]{:S(2)}, u32[]{:S(2)}) async-start(f32[32,24,128]{2,1,0:T(8,128)} %get-tuple-element.84), calls=%async_computation.2 | async-start | bytes 786432 | tf_op jit(solution)/shard_map/all_to_all | solution.py:477
  144.1 9.0 %all-to-all-done.2.got = f32[32,24,128]{2,1,0:T(8,128)S(1)} async-done(((f32[32,24,128]{2,1,0:T(8,128)}), f32[32,24,128]{2,1,0:T(8,128)S(1)}, u32[]{:S(2)}, u32[]{:S(2)}) %all-to-all-start.2) | async-done | bytes 393248 | tf_op jit(solution)/shard_map/all_to_all | solution.py:477
  153.8 1.9 %select.7.q0 = f32[32,16,128]{2,1,0:T(8,128)} custom-call(s32[5]{0:T(128)} %stack.23.place, f32[32,24,128]{2,1,0:T(8,128)} %copy-done.9, f32[16,16,128]{2,1,0:T(8,128)} %get-tuple-element.85.direct_x, f32[8,16,128]{2,1,0:T(8,128)} %get-tuple-element.86.keep, f32[8,16,128]{2,1,0:T(8,128)} %copy-done.22), custom_call_target="tpu_custom_call" | custom-call | tf_op jit(solution)/shard_map/select/pallas_call | solution.py:414
  158.3 6.2 %collective-permute-done.20.q1 = f32[32,16,128]{2,1,0:T(8,128)S(1)} collective-permute-done((f32[32,16,128]{2,1,0:T(8,128)}, f32[32,16,128]{2,1,0:T(8,128)S(1)}, u32[]{:S(2)}, u32[]{:S(2)}) %collective-permute-start.20) | collective-permute-done | bytes 262176 | tf_op jit(solution)/shard_map/ppermute | solution.py:49
  164.5 1.9 %collective-permute-start.22 = (f32[32,16,128]{2,1,0:T(8,128)S(1)}, f32[32,16,128]{2,1,0:T(8,128)S(1)}, u32[]{:S(2)}, u32[]{:S(2)}) collective-permute-start(f32[32,16,128]{2,1,0:T(8,128)S(1)} %collective-permute-done.20.q1), channel_id=1, source_target_pairs={{0,3},{1,2},{2,1},{3,0},{4,7},{5,6},{6,5},{7,4},{8,11},{9,10},{10,... | collective-permute-start | bytes 786440 | tf_op jit(solution)/shard_map/ppermute | solution.py:49
  167.0 5.0 %collective-permute-done.22.q3 = f32[32,16,128]{2,1,0:T(8,128)S(1)} collective-permute-done((f32[32,16,128]{2,1,0:T(8,128)S(1)}, f32[32,16,128]{2,1,0:T(8,128)S(1)}, u32[]{:S(2)}, u32[]{:S(2)}) %collective-permute-start.22) | collective-permute-done | bytes 262176 | tf_op jit(solution)/shard_map/ppermute | solution.py:49
  172.7 2.7 %assemble.1 = (f32[64,2048]{1,0:T(8,128)}, f32[128,1024]{1,0:T(8,128)}) custom-call(s32[5]{0:T(128)} %stack.23.place, f32[32,16,128]{2,1,0:T(8,128)} %select.7.q0, f32[32,16,128]{2,1,0:T(8,128)} %copy-done.13, f32[32,16,128]{2,1,0:T(8,128)} %copy-done.14, f32[32,16,128]{2,1,0:T(8,128)} %copy-done.15), custom_call_target="tpu_custom_call" | custom-call | tf_op jit(solution)/shard_map/assemble/pallas_call | solution.py:414
  (83 shorter events, 23.7 us)
Async XLA Ops:
  0.6 16.8 %collective-permute-start = (f32[12,1024,128]{2,1,0:T(8,128)}, f32[12,1024,128]{2,1,0:T(8,128)}, u32[]{:S(2)}, u32[]{:S(2)}) collective-permute-start(f32[12,1024,128]{2,1,0:T(8,128)} %own.1), channel_id=1, source_target_pairs={{0,64},{64,0},{1,65},{65,1},{2,66},{66,2},{3,67},{67,3},{4,68},{68... | collective-permute-start | bytes 18874376 | tf_op jit(solution)/shard_map/ppermute | solution.py:433
  9.5 7.9 %collective-permute-start.1 = (f32[128,1536]{1,0:T(8,128)}, f32[128,1536]{1,0:T(8,128)S(1)}, u32[]{:S(2)}, u32[]{:S(2)}) collective-permute-start(f32[128,1536]{1,0:T(8,128)} %get-tuple-element.48), channel_id=1, source_target_pairs={{0,64},{64,0},{1,65},{65,1},{2,66},{66,2},{3,67},{67,3},{4,68},{68... | collective-permute-start | bytes 2359304 | tf_op jit(solution)/shard_map/ppermute | solution.py:435
  10.1 31.9 %all-to-all-start = ((f32[16,16,1536]{2,1,0:T(8,128)}), f32[16,16,1536]{2,1,0:T(8,128)S(1)}, u32[]{:S(2)}, u32[]{:S(2)}) async-start(f32[16,16,1536]{2,1,0:T(8,128)} %get-tuple-element.55), calls=%async_computation | async-start | bytes 3145728 | tf_op jit(solution)/shard_map/all_to_all | solution.py:436
  42.0 3.5 %collective-permute-start.3 = (f32[16,16,1536]{2,1,0:T(8,128)S(1)}, f32[16,16,1536]{2,1,0:T(8,128)}, u32[]{:S(2)}, u32[]{:S(2)}) collective-permute-start(f32[16,16,1536]{2,1,0:T(8,128)S(1)} %all-to-all-done.own), channel_id=1, source_target_pairs={{0,64},{64,0},{1,65},{65,1},{2,66},{66,2},{3,67},{67,3},{4,68},{68... | collective-permute-start | bytes 4718600 | tf_op jit(solution)/shard_map/ppermute | solution.py:446
  42.0 12.4 %collective-permute-start.7 = (f32[2,16,16,384]{3,2,1,0:T(8,128)}, f32[2,16,16,384]{3,2,1,0:T(8,128)S(1)}, u32[]{:S(2)}, u32[]{:S(2)}) collective-permute-start(f32[2,16,16,384]{3,2,1,0:T(8,128)} %get-tuple-element.66), channel_id=1, source_target_pairs={{0,1},{1,0},{2,3},{3,2},{4,5},{5,4},{6,7},{7,6},{8,9},{9,8},{10,11... | collective-permute-start | bytes 2359304 | tf_op jit(solution)/shard_map/ppermute | solution.py:49
  43.9 16.4 %collective-permute-start.2 = (f32[2,4,96,384]{3,2,1,0:T(8,128)}, f32[2,4,96,384]{3,2,1,0:T(8,128)S(1)}, u32[]{:S(2)}, u32[]{:S(2)}) collective-permute-start(f32[2,4,96,384]{3,2,1,0:T(8,128)} %get-tuple-element.57), channel_id=1, source_target_pairs={{0,4},{1,5},{2,6},{3,7},{4,0},{5,1},{6,2},{7,3},{8,12},{9,13},{10,... | collective-permute-start | bytes 3538952 | tf_op jit(solution)/shard_map/ppermute | solution.py:49
  43.9 16.4 %collective-permute-start.5 = (f32[2,4,96,384]{3,2,1,0:T(8,128)}, f32[2,4,96,384]{3,2,1,0:T(8,128)S(1)}, u32[]{:S(2)}, u32[]{:S(2)}) collective-permute-start(f32[2,4,96,384]{3,2,1,0:T(8,128)} %get-tuple-element.62), channel_id=1, source_target_pairs={{0,16},{1,17},{2,18},{3,19},{4,20},{5,21},{6,22},{7,23},{8,24},{9,... | collective-permute-start | bytes 3538952 | tf_op jit(solution)/shard_map/ppermute | solution.py:49
  51.9 16.9 %collective-permute-start.4 = (f32[2,4,64,384]{3,2,1,0:T(8,128)}, f32[2,4,64,384]{3,2,1,0:T(8,128)S(1)}, u32[]{:S(2)}, u32[]{:S(2)}) collective-permute-start(f32[2,4,64,384]{3,2,1,0:T(8,128)} %get-tuple-element.60), channel_id=1, source_target_pairs={{0,4},{1,5},{2,6},{3,7},{4,0},{5,1},{6,2},{7,3},{8,12},{9,13},{10,... | collective-permute-start | bytes 2359304 | tf_op jit(solution)/shard_map/ppermute | solution.py:49
  52.4 16.4 %collective-permute-start.6 = (f32[2,4,64,384]{3,2,1,0:T(8,128)}, f32[2,4,64,384]{3,2,1,0:T(8,128)S(1)}, u32[]{:S(2)}, u32[]{:S(2)}) collective-permute-start(f32[2,4,64,384]{3,2,1,0:T(8,128)} %get-tuple-element.64), channel_id=1, source_target_pairs={{0,16},{1,17},{2,18},{3,19},{4,20},{5,21},{6,22},{7,23},{8,24},{9,... | collective-permute-start | bytes 2359304 | tf_op jit(solution)/shard_map/ppermute | solution.py:49
  54.4 14.4 %copy-start.2 = (f32[2,16,16,384]{3,2,1,0:T(8,128)}, f32[2,16,16,384]{3,2,1,0:T(8,128)S(1)}, u32[]{:S(2)}) copy-start(f32[2,16,16,384]{3,2,1,0:T(8,128)S(1)} %collective-permute-done.7.refs_9_.c_x) | copy-start | bytes 2359300
  54.4 14.4 %collective-permute-start.8 = (f32[2,16,16,384]{3,2,1,0:T(8,128)}, f32[2,16,16,384]{3,2,1,0:T(8,128)S(1)}, u32[]{:S(2)}, u32[]{:S(2)}) collective-permute-start(f32[2,16,16,384]{3,2,1,0:T(8,128)} %get-tuple-element.68), channel_id=1, source_target_pairs={{0,1},{1,0},{2,3},{3,2},{4,5},{5,4},{6,7},{7,6},{8,9},{9,8},{10,11... | collective-permute-start | bytes 2359304 | tf_op jit(solution)/shard_map/ppermute | solution.py:49
  60.3 8.5 %copy-start = (f32[2,4,96,384]{3,2,1,0:T(8,128)}, f32[2,4,96,384]{3,2,1,0:T(8,128)S(1)}, u32[]{:S(2)}) copy-start(f32[2,4,96,384]{3,2,1,0:T(8,128)S(1)} %collective-permute-done.2.refs_1_) | copy-start | bytes 3538948
  60.4 8.5 %copy-start.1 = (f32[2,4,96,384]{3,2,1,0:T(8,128)}, f32[2,4,96,384]{3,2,1,0:T(8,128)S(1)}, u32[]{:S(2)}) copy-start(f32[2,4,96,384]{3,2,1,0:T(8,128)S(1)} %collective-permute-done.5.refs_5_.refs_6_) | copy-start | bytes 3538948
  74.4 15.5 %collective-permute-start.10 = (f32[4,160,384]{2,1,0:T(8,128)}, f32[4,160,384]{2,1,0:T(8,128)S(1)}, u32[]{:S(2)}, u32[]{:S(2)}) collective-permute-start(f32[4,160,384]{2,1,0:T(8,128)} %get-tuple-element.70), channel_id=1, source_target_pairs={{0,12},{1,13},{2,14},{3,15},{4,8},{5,9},{6,10},{7,11},{8,4},{9,5},... | collective-permute-start | bytes 2949128 | tf_op jit(solution)/shard_map/ppermute | solution.py:49
  75.8 15.5 %collective-permute-start.11 = (f32[4,160,384]{2,1,0:T(8,128)}, f32[4,160,384]{2,1,0:T(8,128)S(1)}, u32[]{:S(2)}, u32[]{:S(2)}) collective-permute-start(f32[4,160,384]{2,1,0:T(8,128)} %get-tuple-element.71), channel_id=1, source_target_pairs={{0,48},{1,49},{2,50},{3,51},{4,52},{5,53},{6,54},{7,55},{8,56},{9,... | collective-permute-start | bytes 2949128 | tf_op jit(solution)/shard_map/ppermute | solution.py:49
  78.5 18.9 %collective-permute-start.9 = (f32[16,32,384]{2,1,0:T(8,128)}, f32[16,32,384]{2,1,0:T(8,128)S(1)}, u32[]{:S(2)}, u32[]{:S(2)}) collective-permute-start(f32[16,32,384]{2,1,0:T(8,128)} %get-tuple-element.69), channel_id=1, source_target_pairs={{0,3},{1,2},{2,1},{3,0},{4,7},{5,6},{6,5},{7,4},{8,11},{9,10},{10,... | collective-permute-start | bytes 2359304 | tf_op jit(solution)/shard_map/ppermute | solution.py:49
  96.6 11.1 %collective-permute-start.12 = (f32[2,160,384]{2,1,0:T(8,128)}, f32[2,160,384]{2,1,0:T(8,128)S(1)}, u32[]{:S(2)}, u32[]{:S(2)}) collective-permute-start(f32[2,160,384]{2,1,0:T(8,128)} %get-tuple-element.74), channel_id=1, source_target_pairs={{0,16},{1,17},{2,18},{3,19},{4,20},{5,21},{6,22},{7,23},{8,24},{9,... | collective-permute-start | bytes 1474568 | tf_op jit(solution)/shard_map/ppermute | solution.py:49
  96.9 10.8 %collective-permute-start.13 = (f32[2,160,384]{2,1,0:T(8,128)}, f32[2,160,384]{2,1,0:T(8,128)S(1)}, u32[]{:S(2)}, u32[]{:S(2)}) collective-permute-start(f32[2,160,384]{2,1,0:T(8,128)} %get-tuple-element.76), channel_id=1, source_target_pairs={{0,4},{1,5},{2,6},{3,7},{4,0},{5,1},{6,2},{7,3},{8,12},{9,13},{10,... | collective-permute-start | bytes 1474568 | tf_op jit(solution)/shard_map/ppermute | solution.py:49
  100.9 30.7 %all-to-all-start.1 = ((f32[16,32,384]{2,1,0:T(8,128)}), f32[16,32,384]{2,1,0:T(8,128)S(1)}, u32[]{:S(2)}, u32[]{:S(2)}) async-start(f32[16,32,384]{2,1,0:T(8,128)} %sum_last_third.1), calls=%async_computation.1 | async-start | bytes 1572864 | tf_op jit(solution)/shard_map/all_to_all | solution.py:458
  111.0 11.3 %collective-permute-start.14 = (f32[160,384]{1,0:T(8,128)}, f32[160,384]{1,0:T(8,128)S(1)}, u32[]{:S(2)}, u32[]{:S(2)}) collective-permute-start(f32[160,384]{1,0:T(8,128)} %get-tuple-element.77), channel_id=1, source_target_pairs={{0,48},{1,49},{2,50},{3,51},{4,52},{5,53},{6,54},{7,55},{8,56},{9,... | collective-permute-start | bytes 737288 | tf_op jit(solution)/shard_map/ppermute | solution.py:49
  114.1 8.2 %collective-permute-start.15 = (f32[160,384]{1,0:T(8,128)}, f32[160,384]{1,0:T(8,128)S(1)}, u32[]{:S(2)}, u32[]{:S(2)}) collective-permute-start(f32[160,384]{1,0:T(8,128)} %get-tuple-element.78), channel_id=1, source_target_pairs={{0,12},{1,13},{2,14},{3,15},{4,8},{5,9},{6,10},{7,11},{8,4},{9,5},... | collective-permute-start | bytes 737288 | tf_op jit(solution)/shard_map/ppermute | solution.py:49
  126.2 7.7 %collective-permute-start.16 = (f32[64,384]{1,0:T(8,128)}, f32[64,384]{1,0:T(8,128)S(1)}, u32[]{:S(2)}, u32[]{:S(2)}) collective-permute-start(f32[64,384]{1,0:T(8,128)} %get-tuple-element.80), channel_id=1, source_target_pairs={{0,1},{1,2},{2,3},{3,0},{4,5},{5,6},{6,7},{7,4},{8,9},{9,10},{10,1... | collective-permute-start | bytes 294920 | tf_op jit(solution)/shard_map/ppermute | solution.py:31
  126.2 8.4 %collective-permute-start.17 = (f32[64,384]{1,0:T(8,128)}, f32[64,384]{1,0:T(8,128)S(1)}, u32[]{:S(2)}, u32[]{:S(2)}) collective-permute-start(f32[64,384]{1,0:T(8,128)} %get-tuple-element.81), channel_id=1, source_target_pairs={{0,2},{1,3},{2,0},{3,1},{4,6},{5,7},{6,4},{7,5},{8,10},{9,11},{10,... | collective-permute-start | bytes 294920 | tf_op jit(solution)/shard_map/ppermute | solution.py:31
  129.4 5.2 %collective-permute-start.18 = (f32[64,384]{1,0:T(8,128)}, f32[64,384]{1,0:T(8,128)S(1)}, u32[]{:S(2)}, u32[]{:S(2)}) collective-permute-start(f32[64,384]{1,0:T(8,128)} %get-tuple-element.82), channel_id=1, source_target_pairs={{0,3},{1,0},{2,1},{3,2},{4,7},{5,4},{6,5},{7,6},{8,11},{9,8},{10,9... | collective-permute-start | bytes 294920 | tf_op jit(solution)/shard_map/ppermute | solution.py:31
  132.3 34.0 %copy-start.18 = (f32[64,384]{1,0:T(8,128)S(1)}, f32[64,384]{1,0:T(8,128)}, u32[]{:S(2)}) copy-start(f32[64,384]{1,0:T(8,128)} %get-tuple-element.90) | copy-start | bytes 294916
  137.3 15.8 %all-to-all-start.2 = ((f32[32,24,128]{2,1,0:T(8,128)}), f32[32,24,128]{2,1,0:T(8,128)S(1)}, u32[]{:S(2)}, u32[]{:S(2)}) async-start(f32[32,24,128]{2,1,0:T(8,128)} %get-tuple-element.84), calls=%async_computation.2 | async-start | bytes 786432 | tf_op jit(solution)/shard_map/all_to_all | solution.py:477
  142.5 1.5 collective-permute-start.19
  144.1 9.0 %copy-start.22 = (f32[8,16,128]{2,1,0:T(8,128)}, f32[8,16,128]{2,1,0:T(8,128)S(1)}, u32[]{:S(2)}) copy-start(f32[8,16,128]{2,1,0:T(8,128)S(1)} %collective-permute-done.19.come) | copy-start | bytes 196612
  155.7 8.8 %collective-permute-start.20 = (f32[32,16,128]{2,1,0:T(8,128)}, f32[32,16,128]{2,1,0:T(8,128)S(1)}, u32[]{:S(2)}, u32[]{:S(2)}) collective-permute-start(f32[32,16,128]{2,1,0:T(8,128)} %select.7.q0), channel_id=1, source_target_pairs={{0,1},{1,0},{2,3},{3,2},{4,5},{5,4},{6,7},{7,6},{8,9},{9,8},{10,11... | collective-permute-start | bytes 786440 | tf_op jit(solution)/shard_map/ppermute | solution.py:49
  156.9 10.2 %collective-permute-start.21 = (f32[32,16,128]{2,1,0:T(8,128)}, f32[32,16,128]{2,1,0:T(8,128)S(1)}, u32[]{:S(2)}, u32[]{:S(2)}) collective-permute-start(f32[32,16,128]{2,1,0:T(8,128)} %select.7.q0), channel_id=1, source_target_pairs={{0,3},{1,2},{2,1},{3,0},{4,7},{5,6},{6,5},{7,4},{8,11},{9,10},{10,... | collective-permute-start | bytes 786440 | tf_op jit(solution)/shard_map/ppermute | solution.py:49
  164.5 7.6 %copy-start.13 = (f32[32,16,128]{2,1,0:T(8,128)}, f32[32,16,128]{2,1,0:T(8,128)S(1)}, u32[]{:S(2)}) copy-start(f32[32,16,128]{2,1,0:T(8,128)S(1)} %collective-permute-done.20.q1) | copy-start | bytes 786436
  164.5 7.6 %collective-permute-start.22 = (f32[32,16,128]{2,1,0:T(8,128)S(1)}, f32[32,16,128]{2,1,0:T(8,128)S(1)}, u32[]{:S(2)}, u32[]{:S(2)}) collective-permute-start(f32[32,16,128]{2,1,0:T(8,128)S(1)} %collective-permute-done.20.q1), channel_id=1, source_target_pairs={{0,3},{1,2},{2,1},{3,0},{4,7},{5,6},{6,5},{7,4},{8,11},{9,10},{10,... | collective-permute-start | bytes 786440 | tf_op jit(solution)/shard_map/ppermute | solution.py:49
  (18 other events, 23.0 us)

commit v5 on v4

--- a/solution.py
+++ b/solution.py
@@ -255,79 +255,86 @@
     return (terms[0][index] + terms[1][index]) + (terms[2][index] + terms[3][index])
 
 
-def add_kernel(*refs):
-    for i, out in enumerate(refs[12:]):
-        terms = refs[4 * i : 4 * i + 4]
-        at = 0
-        for kept, came in zip(terms[0::2], terms[1::2]):
-            rows = kept.shape[2]
-            out[:, at : at + rows, :] = kept[0] + came[0]
-            at += rows
-
-
 def slab_of(v, k):
     return pl.BlockSpec((1,) + v.shape[1:], lambda i: (k, 0, 0, 0))
 
 
-def add_for_second(*thirds):
-    shapes = [(t[0].shape[1], sum(v.shape[2] for v in t[0::2]), 384) for t in thirds]
-    terms = [v for t in thirds for v in t]
+def shapes_of(px, py):
+    return [jax.ShapeDtypeStruct((v.shape[1], v.shape[2] + w.shape[2], 384), F32) for v, w in zip(px, py)]
+
+
+def add_x_kernel(*refs):
+    for kept, came, out in zip(refs[0:3], refs[3:6], refs[6:9]):
+        out[...] = kept[0] + came[0]
+
+
+def add_x(kept, came, shapes):
     return pl.pallas_call(
-        add_kernel,
+        add_x_kernel,
         grid=(1,),
-        in_specs=[slab_of(v, 1) for v in terms],
-        out_specs=[pl.BlockSpec(shape, lambda i: (0, 0, 0)) for shape in shapes],
-        out_shape=[jax.ShapeDtypeStruct(shape, F32) for shape in shapes],
+        in_specs=[slab_of(v, 1) for v in kept + came],
+        out_specs=[pl.BlockSpec(v.shape[1:], lambda i: (0, 0, 0)) for v in kept],
+        out_shape=shapes,
+        compiler_params=pltpu.CompilerParams(vmem_limit_bytes=VMEM_LIMIT),
+        cost_estimate=pl.CostEstimate(flops=400000, bytes_accessed=5000000, transcendentals=0),
+        name="add_x",
+    )(*kept, *came)
+
+
+def add_y_kernel(*refs):
+    for kept, came, out in zip(refs[0:3], refs[3:6], refs[9:12]):
+        out[...] = kept[0] + came[0]
+
+
+def add_y(kept, came, sums):
+    ins, outs = [], []
+    for v, total in zip(kept, sums):
+        rows = v.shape[2] // 2
+        first = total.shape[1] // rows - 2
+        ins.append(pl.BlockSpec((1, v.shape[1], rows, 384), lambda i: (1, 0, i, 0)))
+        outs.append(pl.BlockSpec((v.shape[1], rows, 384), lambda i, first=first: (0, first + i, 0)))
+    return pl.pallas_call(
+        add_y_kernel,
+        grid=(2,),
+        in_specs=ins + ins + [pl.BlockSpec(memory_space=pl.ANY)] * 3,
+        out_specs=outs,
+        out_shape=[jax.ShapeDtypeStruct(v.shape, F32) for v in sums],
+        input_output_aliases={6: 0, 7: 1, 8: 2},
+        compiler_params=pltpu.CompilerParams(vmem_limit_bytes=VMEM_LIMIT),
+        cost_estimate=pl.CostEstimate(flops=300000, bytes_accessed=4000000, transcendentals=0),
+        name="add_y",
+    )(*kept, *came, *sums)
+
+
+def add_own_kernel(*refs):
+    for k_x, c_x, k_y, c_y, out in zip(refs[0:3], refs[3:6], refs[6:9], refs[9:12], refs[12:15]):
+        rows = k_x.shape[2]
+        out[:, :rows, :] = k_x[0] + c_x[0]
+        out[:, rows:, :] = k_y[0] + c_y[0]
+
+
+def add_own(terms, shapes):
+    return pl.pallas_call(
+        add_own_kernel,
+        grid=(1,),
+        in_specs=[slab_of(v, 0) for v in terms],
+        out_specs=[pl.BlockSpec(v.shape, lambda i: (0, 0, 0)) for v in shapes],
+        out_shape=shapes,
         compiler_params=pltpu.CompilerParams(vmem_limit_bytes=VMEM_LIMIT),
         cost_estimate=pl.CostEstimate(flops=700000, bytes_accessed=9000000, transcendentals=0),
-        name="add",
+        name="add_own",
     )(*terms)
 
 
-def sum_last_third_kernel(k_x, c_x, k_y, c_y, last, out):
-    out[:, :16, :] = (k_x[0] + c_x[0]) + last[:, :16, :]
-    out[:, 16:, :] = (k_y[0] + c_y[0]) + last[:, 16:, :]
-
-
-def sum_last_third(terms, last):
-    whole = pl.BlockSpec(last.shape, lambda i: (0, 0, 0))
-    return pl.pallas_call(
-        sum_last_third_kernel,
-        grid=(1,),
-        in_specs=[slab_of(v, 0) for v in terms] + [whole],
-        out_specs=whole,
-        out_shape=jax.ShapeDtypeStruct(last.shape, F32),
-        compiler_params=pltpu.CompilerParams(vmem_limit_bytes=VMEM_LIMIT),
-        cost_estimate=pl.CostEstimate(flops=1000000, bytes_accessed=4000000, transcendentals=0),
-        name="sum_last_third",
-    )(*terms, last)
-
-
-def sum_first_kernel(place, *refs):
-    for third, axis in enumerate((2, 1)):
-        k_x, c_x, k_y, c_y, last = refs[5 * third : 5 * third + 5]
-        outs = refs[10 + 2 * third : 12 + 2 * third]
+def sum_first_kernel(place, own_a, last_a, own_b, last_b, *outs):
+    for axis, own, last, out in ((2, own_a, last_a, outs[0:2]), (1, own_b, last_b, outs[2:4])):
         for sent, slot, mask in owner_masks(place):
             k = place[axis] ^ mask
-            outs[sent][slot, :96, :] = (k_x[0, k] + c_x[0, k]) + last[k, :96, :]
-            outs[sent][slot, 96:, :] = (k_y[0, k] + c_y[0, k]) + last[k, 96:, :]
-
-
-def sum_first(place, terms_a, last_a, terms_b, last_b):
-    whole = pl.BlockSpec(last_a.shape, lambda i: (0, 0, 0))
-    shape = (2, 160, 384)
-    return pl.pallas_call(
-        sum_first_kernel,
-        grid=(1,),
-        in_specs=[pl.BlockSpec(memory_space=pltpu.SMEM)]
-        + [slab_of(v, 0) for v in terms_a] + [whole]
-        + [slab_of(v, 0) for v in terms_b] + [whole],
-        out_specs=[pl.BlockSpec(shape, lambda i: (0, 0, 0))] * 4,
-        out_shape=[jax.ShapeDtypeStruct(shape, F32)] * 4,
-        compiler_params=pltpu.CompilerParams(vmem_limit_bytes=VMEM_LIMIT),
-        cost_estimate=pl.CostEstimate(flops=1000000, bytes_accessed=8000000, transcendentals=0),
-        name="sum_first",
-    )(place, *terms_a, last_a, *terms_b, last_b)
+            out[sent][slot] = own[k] + last[k]
+
+
+def add_two_kernel(place, first, second, out):
+    out[...] = first[...] + second[...]
 
 
 def add_second_kernel(place, k_a, c_a, k_b, c_b, out_a, out_b):
@@ -450,12 +457,20 @@
     )
     came_y = first_swaps(py)
 
-    terms_a, terms_b, terms_c = [(px[2 * i], came_x[i], py[2 * i], came_y[i]) for i in range(3)]
-    last_a, last_b, last_c = add_for_second(terms_a, terms_b, terms_c)
-    kept_a, sent_a, kept_b, sent_b = sum_first(place, terms_a, swap_x(last_a, 1), terms_b, swap_y(last_b, 1))
+    kept_x, kept_y = list(px[0::2]), list(py[0::2])
+    shapes = shapes_of(kept_x, kept_y)
+    last = add_y(kept_y, came_y, add_x(kept_x, came_x, shapes))
+    *terms, last = lax.optimization_barrier((*kept_x, *came_x, *kept_y, *came_y, last))
+    own_a, own_b, own_c = add_own(terms, shapes)
+    last_a, last_b, last_c = [swap(v, 1) for v, swap in zip(last, (swap_x, swap_y, swap_z))]
+    halves = jax.ShapeDtypeStruct((2, 160, 384), F32)
+    kept_a, sent_a, kept_b, sent_b = small_kernel(
+        sum_first_kernel, "sum_first", [halves] * 4, [], place, own_a, last_a, own_b, last_b
+    )
     came_a, came_b = swap_y(sent_a, 0), swap_x(sent_b, 0)
-    last_c, kept_a = lax.optimization_barrier((swap_z(last_c, 1), kept_a))
-    c = lax.all_to_all(sum_last_third(terms_c, last_c), "gy", 0, 0, tiled=True).sum(axis=0)
+    last_c, kept_a = lax.optimization_barrier((last_c, kept_a))
+    c = small_kernel(add_two_kernel, "sum_last_third", shapes[2], [], place, own_c, last_c)
+    c = lax.all_to_all(c, "gy", 0, 0, tiled=True).sum(axis=0)
     second = jax.ShapeDtypeStruct((160, 384), F32)
     last_a, last_b = small_kernel(
         add_second_kernel, "add_second", [second] * 2, [], place, kept_a, came_a, kept_b, came_b

time: 176 us -> 173 us (0.983)
  waiting for transfers between devices: 54.9 us -> 45.2 us
  Pallas kernels: 58.2 us -> 63.2 us
    ppermute x16, waiting for transfers between devices: 39.7 us -> 29.8 us  [swap(): return lax.ppermute(v, ('gx', 'gy', 'gz'), pairs)]
    pallas_call x5 -> x7, Pallas kernels: 11.3 us -> 17.3 us  [small_kernel(): pl.pallas_call(kernel, in_specs=[pl.BlockSpec(memory_space=pltpu.SMEM)] +...]
  transfers between devices with their start and end apart: 26 -> 26, of which waited for: 13 -> 14; matrix products, arithmetic and copies ran while one was open for 1% -> 1% of each run, Pallas kernels for 27% -> 31%
where the time goes in v5:
time: 173 us
  Pallas kernels  63.2 us (37%)
  starting transfers between devices  51.2 us (30%)
  waiting for transfers between devices  45.2 us (26%)
  local copies, waits for them, and re-layouts  11.4 us (7%)
    ppermute x16, waiting for transfers between devices, swap(): return lax.ppermute(v, ('gx', 'gy', 'gz'), pairs)  29.8 us
    pallas_call x2, Pallas kernels, gram_pieces(): pl.pallas_call(kernel, in_specs=[pl.BlockSpec(memory_space=space) for spa...  27.8 us
    ppermute x16, starting transfers between devices, swap(): return lax.ppermute(v, ('gx', 'gy', 'gz'), pairs)  25.2 us
    pallas_call x7, Pallas kernels, small_kernel(): pl.pallas_call(kernel, in_specs=[pl.BlockSpec(memory_space=pltpu.SMEM)] +...  17.3 us
    unnamed x48, local copies, waits for them, and re-layouts  10.2 us
    all_to_all x1, waiting for transfers between devices, per_device(): got = lax.all_to_all(slots, ('gx', 'gy'), 0, 0, tiled=True)  8.98 us
    pallas_call x1, Pallas kernels, project(): pl.pallas_call(project_kernel, in_specs=[pl.BlockSpec(memory_space=pltpu....  8.16 us
    all_to_all x1, starting transfers between devices, per_device(): fibers = lax.all_to_all(both, 'gy', 0, 0, tiled=True)  7.3 us
  transfers between devices with their start and end apart: 26, of which 14 were waited for; matrix products, arithmetic and copies ran while one was open for 1% of the time, Pallas kernels for 31%

profile of v5, /device:TPU:0, one launch (start us, length us, event | category | flops | bytes accessed | tf_op | source)
XLA Modules:
  0.0 172.6 jit_solution(2661096367383191881)
XLA Ops:
  1.4 8.2 %project.1 = (f32[128,1536]{1,0:T(8,128)}, f32[128,1536]{1,0:T(8,128)}, f32[16,16,1536]{2,1,0:T(8,128)}) custom-call(s32[5]{0:T(128)} %stack.23.place, f32[12,1024,128]{2,1,0:T(8,128)} %own.1, f32[1024,256]{1,0:T(8,128)} %basis.1), custom_call_target="tpu_custom_call" | custom-call | flops 2400000000 | bytes 9000000 | tf_op jit(solution)/shard_map/project/pallas_call | solution.py:103
  10.1 7.3 %all-to-all-start = ((f32[16,16,1536]{2,1,0:T(8,128)}), f32[16,16,1536]{2,1,0:T(8,128)S(1)}, u32[]{:S(2)}, u32[]{:S(2)}) async-start(f32[16,16,1536]{2,1,0:T(8,128)} %get-tuple-element.76), calls=%async_computation | async-start | bytes 3145728 | tf_op jit(solution)/shard_map/all_to_all | solution.py:443
  18.3 21.3 %gram_x.1 = (f32[2,4,96,384]{3,2,1,0:T(8,128)}, f32[2,4,96,384]{3,2,1,0:T(8,128)}, f32[2,4,96,384]{3,2,1,0:T(8,128)}, f32[2,4,96,384]{3,2,1,0:T(8,128)}, f32[2,1...) custom-call(s32[5]{0:T(128)} %stack.23.place, f32[12,1024,128]{2,1,0:T(8,128)} %own.1, ...), custom_call_target="tpu_custom_call" | custom-call | flops 12000000000 | bytes 20000000 | tf_op jit(solution)/shard_map/gram_x/pallas_call | solution.py:224
  39.6 2.4 %all-to-all-done.own = f32[16,16,1536]{2,1,0:T(8,128)S(1)} async-done(((f32[16,16,1536]{2,1,0:T(8,128)}), f32[16,16,1536]{2,1,0:T(8,128)S(1)}, u32[]{:S(2)}, u32[]{:S(2)}) %all-to-all-start) | async-done | bytes 1572896 | tf_op jit(solution)/shard_map/all_to_all | solution.py:443
  42.0 1.9 %collective-permute-start.4 = (f32[2,16,16,384]{3,2,1,0:T(8,128)}, f32[2,16,16,384]{3,2,1,0:T(8,128)S(1)}, u32[]{:S(2)}, u32[]{:S(2)}) collective-permute-start(f32[2,16,16,384]{3,2,1,0:T(8,128)} %get-tuple-element.82), channel_id=1, source_target_pairs={{0,1},{1,0},{2,3},{3,2},{4,5},{5,4},{6,7},{7,6},{8,9},{9,8},{10,11... | collective-permute-start | bytes 2359304 | tf_op jit(solution)/shard_map/ppermute | solution.py:49
  45.5 6.4 %gram_y.1 = (f32[2,4,64,384]{3,2,1,0:T(8,128)}, f32[2,4,64,384]{3,2,1,0:T(8,128)}, f32[2,4,64,384]{3,2,1,0:T(8,128)}, f32[2,4,64,384]{3,2,1,0:T(8,128)}, f32[2,1...) custom-call(s32[5]{0:T(128)} %stack.23.place, f32[16,16,1536]{2,1,0:T(8,128)} %copy-done.8, ...), custom_call_target="tpu_custom_call" | custom-call | flops 2400000000 | bytes 20000000 | tf_op jit(solution)/shard_map/gram_y/pallas_call | solution.py:224
  52.5 2.0 %collective-permute-start.7 = (f32[2,4,64,384]{3,2,1,0:T(8,128)}, f32[2,4,64,384]{3,2,1,0:T(8,128)S(1)}, u32[]{:S(2)}, u32[]{:S(2)}) collective-permute-start(f32[2,4,64,384]{3,2,1,0:T(8,128)} %get-tuple-element.88), channel_id=1, source_target_pairs={{0,16},{1,17},{2,18},{3,19},{4,20},{5,21},{6,22},{7,23},{8,24},{9,... | collective-permute-start | bytes 2359304 | tf_op jit(solution)/shard_map/ppermute | solution.py:49
  56.1 4.2 %collective-permute-done.2.refs_3_ = f32[2,4,96,384]{3,2,1,0:T(8,128)S(1)} collective-permute-done((f32[2,4,96,384]{3,2,1,0:T(8,128)}, f32[2,4,96,384]{3,2,1,0:T(8,128)S(1)}, u32[]{:S(2)}, u32[]{:S(2)}) %collective-permute-start.2) | collective-permute-done | bytes 1179680 | tf_op jit(solution)/shard_map/ppermute | solution.py:49
  62.3 3.2 %add_x.1 = (f32[4,160,384]{2,1,0:T(8,128)}, f32[4,160,384]{2,1,0:T(8,128)}, f32[16,32,384]{2,1,0:T(8,128)}) custom-call(f32[2,4,96,384]{3,2,1,0:T(8,128)} %get-tuple-element.97.refs_0_, f32[2,4,96,384]{3,2,1,0:T(8,128)} %get-tuple-element.98.refs_1_, f32[2,16,16,384]{3,2,1,0:T(8,128)} %get-tuple-element.99.refs_2_, f32[2,4,96,384]{3,2,1,0:T(8,128)} %copy-done, ...), custom_call_target="tpu_custom_call" | custom-call | flops 400000 | bytes 5000000 | tf_op jit(solution)/shard_map/add_x/pallas_call | solution.py:272
  65.5 3.3 %collective-permute-done.6.refs_3_.refs_9_ = f32[2,4,64,384]{3,2,1,0:T(8,128)S(1)} collective-permute-done((f32[2,4,64,384]{3,2,1,0:T(8,128)}, f32[2,4,64,384]{3,2,1,0:T(8,128)S(1)}, u32[]{:S(2)}, u32[]{:S(2)}) %collective-permute-start.6) | collective-permute-done | bytes 786464 | tf_op jit(solution)/shard_map/ppermute | solution.py:49
  70.2 2.7 %add_y.1 = (f32[4,160,384]{2,1,0:T(8,128)}, f32[4,160,384]{2,1,0:T(8,128)}, f32[16,32,384]{2,1,0:T(8,128)}) custom-call(f32[2,4,64,384]{3,2,1,0:T(8,128)} %get-tuple-element.103.refs_0_.refs_6_, f32[2,4,64,384]{3,2,1,0:T(8,128)} %get-tuple-element.104.refs_1_.refs_7_, ...), custom_call_target="tpu_custom_call", output_to_operand_aliasing={{0}: (6, {}), {1}: (7, {}), {2}: (8, {})} | custom-call | flops 300000 | bytes 4000000 | tf_op jit(solution)/shard_map/add_y/pallas_call | solution.py:296
  74.2 2.8 %collective-permute-start.11 = (f32[4,160,384]{2,1,0:T(8,128)}, f32[4,160,384]{2,1,0:T(8,128)S(1)}, u32[]{:S(2)}, u32[]{:S(2)}) collective-permute-start(f32[4,160,384]{2,1,0:T(8,128)} %get-tuple-element.112), channel_id=1, source_target_pairs={{0,48},{1,49},{2,50},{3,51},{4,52},{5,53},{6,54},{7,55},{8,56},{9,... | collective-permute-start | bytes 2949128 | tf_op jit(solution)/shard_map/ppermute | solution.py:49
  77.0 2.5 %collective-permute-start.9 = (f32[16,32,384]{2,1,0:T(8,128)}, f32[16,32,384]{2,1,0:T(8,128)S(1)}, u32[]{:S(2)}, u32[]{:S(2)}) collective-permute-start(f32[16,32,384]{2,1,0:T(8,128)} %get-tuple-element.96), channel_id=1, source_target_pairs={{0,3},{1,2},{2,1},{3,0},{4,7},{5,6},{6,5},{7,4},{8,11},{9,10},{10,... | collective-permute-start | bytes 2359304 | tf_op jit(solution)/shard_map/ppermute | solution.py:49
  79.5 4.2 %add_own.1 = (f32[4,160,384]{2,1,0:T(8,128)}, f32[4,160,384]{2,1,0:T(8,128)}, f32[16,32,384]{2,1,0:T(8,128)}) custom-call(f32[2,4,96,384]{3,2,1,0:T(8,128)} %get-tuple-element.97.refs_0_, f32[2,4,96,384]{3,2,1,0:T(8,128)} %get-tuple-element.98.refs_1_, f32[2,16,16,384]{3,2,1,0:T(8,128)} %get-tuple-element.99.refs_2_, f32[2,4,96,384]{3,2,1,0:T(8,128)} %copy-done, ...), custom_call_target="tpu_custom_call" | custom-call | flops 700000 | bytes 9000000 | tf_op jit(solution)/shard_map/add_own/pallas_call | solution.py:317
  83.7 4.7 %collective-permute-done.10.last_a = f32[4,160,384]{2,1,0:T(8,128)S(1)} collective-permute-done((f32[4,160,384]{2,1,0:T(8,128)}, f32[4,160,384]{2,1,0:T(8,128)S(1)}, u32[]{:S(2)}, u32[]{:S(2)}) %collective-permute-start.10) | collective-permute-done | bytes 983072 | tf_op jit(solution)/shard_map/ppermute | solution.py:49
  90.7 3.6 %sum_first.1 = (f32[2,160,384]{2,1,0:T(8,128)}, f32[2,160,384]{2,1,0:T(8,128)}, f32[2,160,384]{2,1,0:T(8,128)}, f32[2,160,384]{2,1,0:T(8,128)}) custom-call(s32[5]{0:T(128)} %stack.23.place, f32[4,160,384]{2,1,0:T(8,128)} %get-tuple-element.109.own_a, f32[4,160,384]{2,1,0:T(8,128)} %copy-done.10, f32[4,160,384]{2,1,0:T(8,128)} %get-tuple-element.111.own_b, ...), custom_call_target="tpu_custom_call" | custom-call | tf_op jit(solution)/shard_map/sum_first/pallas_call | solution.py:421
  96.0 2.4 %sum_last_third.1 = f32[16,32,384]{2,1,0:T(8,128)} custom-call(s32[5]{0:T(128)} %stack.23.place, f32[16,32,384]{2,1,0:T(8,128)} %get-tuple-element.124.first, f32[16,32,384]{2,1,0:T(8,128)} %copy-done.12), custom_call_target="tpu_custom_call" | custom-call | tf_op jit(solution)/shard_map/sum_last_third/pallas_call | solution.py:421
  98.3 6.8 %all-to-all-start.1 = ((f32[16,32,384]{2,1,0:T(8,128)}), f32[16,32,384]{2,1,0:T(8,128)S(1)}, u32[]{:S(2)}, u32[]{:S(2)}) async-start(f32[16,32,384]{2,1,0:T(8,128)} %sum_last_third.1), calls=%async_computation.1 | async-start | bytes 1572864 | tf_op jit(solution)/shard_map/all_to_all | solution.py:473
  106.1 2.3 %add_second.1 = (f32[160,384]{1,0:T(8,128)}, f32[160,384]{1,0:T(8,128)}) custom-call(s32[5]{0:T(128)} %stack.23.place, f32[2,160,384]{2,1,0:T(8,128)} %get-tuple-element.114.k_a.refs_0_, f32[2,160,384]{2,1,0:T(8,128)} %copy-done.6, f32[2,160,384]{2,1,0:T(8,128)} %get-tuple-element.116.k_b.refs_3_, f32[2,160,384]{2,1,0:T(8,128)} %copy-done.7), custom_call_target="tpu_custom_call" | custom-call | tf_op jit(solution)/shard_map/add_second/pallas_call | solution.py:421
  108.4 3.1 %collective-permute-start.14 = (f32[160,384]{1,0:T(8,128)}, f32[160,384]{1,0:T(8,128)S(1)}, u32[]{:S(2)}, u32[]{:S(2)}) collective-permute-start(f32[160,384]{1,0:T(8,128)} %get-tuple-element.118), channel_id=1, source_target_pairs={{0,48},{1,49},{2,50},{3,51},{4,52},{5,53},{6,54},{7,55},{8,56},{9,... | collective-permute-start | bytes 737288 | tf_op jit(solution)/shard_map/ppermute | solution.py:49
  111.6 2.7 %collective-permute-start.15 = (f32[160,384]{1,0:T(8,128)}, f32[160,384]{1,0:T(8,128)S(1)}, u32[]{:S(2)}, u32[]{:S(2)}) collective-permute-start(f32[160,384]{1,0:T(8,128)} %get-tuple-element.119), channel_id=1, source_target_pairs={{0,12},{1,13},{2,14},{3,15},{4,8},{5,9},{6,10},{7,11},{8,4},{9,5},... | collective-permute-start | bytes 737288 | tf_op jit(solution)/shard_map/ppermute | solution.py:49
  114.2 5.0 %collective-permute-done.14.refs_2_ = f32[160,384]{1,0:T(8,128)S(1)} collective-permute-done((f32[160,384]{1,0:T(8,128)}, f32[160,384]{1,0:T(8,128)S(1)}, u32[]{:S(2)}, u32[]{:S(2)}) %collective-permute-start.14) | collective-permute-done | bytes 245792 | tf_op jit(solution)/shard_map/ppermute | solution.py:49
  120.7 2.5 %sum_second.1 = (f32[64,384]{1,0:T(8,128)}, f32[64,384]{1,0:T(8,128)}, f32[64,384]{1,0:T(8,128)}, f32[64,384]{1,0:T(8,128)}, f32[64,384]{1,0:T(8,128)}) custom-call(s32[5]{0:T(128)} %stack.23.place, f32[2,160,384]{2,1,0:T(8,128)} %get-tuple-element.114.k_a.refs_0_, f32[2,160,384]{2,1,0:T(8,128)} %copy-done.6, f32[160,384]{1,0:T(8,128)} %copy-done.16, ...), custom_call_target="tpu_custom_call" | custom-call | tf_op jit(solution)/shard_map/sum_second/pallas_call | solution.py:421
  123.2 3.7 %collective-permute-start.17 = (f32[64,384]{1,0:T(8,128)}, f32[64,384]{1,0:T(8,128)S(1)}, u32[]{:S(2)}, u32[]{:S(2)}) collective-permute-start(f32[64,384]{1,0:T(8,128)} %get-tuple-element.122), channel_id=1, source_target_pairs={{0,2},{1,3},{2,0},{3,1},{4,6},{5,7},{6,4},{7,5},{8,10},{9,11},{10,... | collective-permute-start | bytes 294920 | tf_op jit(solution)/shard_map/ppermute | solution.py:31
  126.9 1.9 %collective-permute-start.18 = (f32[64,384]{1,0:T(8,128)}, f32[64,384]{1,0:T(8,128)S(1)}, u32[]{:S(2)}, u32[]{:S(2)}) collective-permute-start(f32[64,384]{1,0:T(8,128)} %get-tuple-element.123), channel_id=1, source_target_pairs={{0,3},{1,0},{2,1},{3,2},{4,7},{5,4},{6,5},{7,6},{8,11},{9,8},{10,9... | collective-permute-start | bytes 294920 | tf_op jit(solution)/shard_map/ppermute | solution.py:31
  132.5 2.0 %sum_last.1 = (f32[32,24,128]{2,1,0:T(8,128)}, f32[16,16,128]{2,1,0:T(8,128)}, f32[8,16,128]{2,1,0:T(8,128)}, f32[8,16,128]{2,1,0:T(8,128)}) custom-call(s32[5]{0:T(128)} %stack.23.place, f32[64,384]{1,0:T(8,128)} %get-tuple-element.120.refs_0_, f32[64,384]{1,0:T(8,128)} %copy-done.19, f32[64,384]{1,0:T(8,128)} %copy-done.20, f32[64,384]{1,0:T(8,128)} %copy-done.21, ...), custom_call_target="tpu_custom_call" | custom-call | tf_op jit(solution)/shard_map/sum_last/pallas_call | solution.py:421
  134.4 5.3 %all-to-all-start.2 = ((f32[32,24,128]{2,1,0:T(8,128)}), f32[32,24,128]{2,1,0:T(8,128)S(1)}, u32[]{:S(2)}, u32[]{:S(2)}) async-start(f32[32,24,128]{2,1,0:T(8,128)} %get-tuple-element.126), calls=%async_computation.2 | async-start | bytes 786432 | tf_op jit(solution)/shard_map/all_to_all | solution.py:492
  141.3 9.0 %all-to-all-done.2.got = f32[32,24,128]{2,1,0:T(8,128)S(1)} async-done(((f32[32,24,128]{2,1,0:T(8,128)}), f32[32,24,128]{2,1,0:T(8,128)S(1)}, u32[]{:S(2)}, u32[]{:S(2)}) %all-to-all-start.2) | async-done | bytes 393248 | tf_op jit(solution)/shard_map/all_to_all | solution.py:492
  155.6 5.9 %collective-permute-done.20.q1 = f32[32,16,128]{2,1,0:T(8,128)S(1)} collective-permute-done((f32[32,16,128]{2,1,0:T(8,128)}, f32[32,16,128]{2,1,0:T(8,128)S(1)}, u32[]{:S(2)}, u32[]{:S(2)}) %collective-permute-start.20) | collective-permute-done | bytes 262176 | tf_op jit(solution)/shard_map/ppermute | solution.py:49
  161.5 2.0 %collective-permute-start.22 = (f32[32,16,128]{2,1,0:T(8,128)S(1)}, f32[32,16,128]{2,1,0:T(8,128)S(1)}, u32[]{:S(2)}, u32[]{:S(2)}) collective-permute-start(f32[32,16,128]{2,1,0:T(8,128)S(1)} %collective-permute-done.20.q1), channel_id=1, source_target_pairs={{0,3},{1,2},{2,1},{3,0},{4,7},{5,6},{6,5},{7,4},{8,11},{9,10},{10,... | collective-permute-start | bytes 786440 | tf_op jit(solution)/shard_map/ppermute | solution.py:49
  164.3 4.9 %collective-permute-done.22.q3 = f32[32,16,128]{2,1,0:T(8,128)S(1)} collective-permute-done((f32[32,16,128]{2,1,0:T(8,128)S(1)}, f32[32,16,128]{2,1,0:T(8,128)S(1)}, u32[]{:S(2)}, u32[]{:S(2)}) %collective-permute-start.22) | collective-permute-done | bytes 262176 | tf_op jit(solution)/shard_map/ppermute | solution.py:49
  169.8 2.7 %assemble.1 = (f32[64,2048]{1,0:T(8,128)}, f32[128,1024]{1,0:T(8,128)}) custom-call(s32[5]{0:T(128)} %stack.23.place, f32[32,16,128]{2,1,0:T(8,128)} %select.7.q0, f32[32,16,128]{2,1,0:T(8,128)} %copy-done.13, f32[32,16,128]{2,1,0:T(8,128)} %copy-done.14, f32[32,16,128]{2,1,0:T(8,128)} %copy-done.15), custom_call_target="tpu_custom_call" | custom-call | tf_op jit(solution)/shard_map/assemble/pallas_call | solution.py:421
  (85 shorter events, 29.0 us)
Async XLA Ops:
  0.6 16.8 %collective-permute-start = (f32[12,1024,128]{2,1,0:T(8,128)}, f32[12,1024,128]{2,1,0:T(8,128)}, u32[]{:S(2)}, u32[]{:S(2)}) collective-permute-start(f32[12,1024,128]{2,1,0:T(8,128)} %own.1), channel_id=1, source_target_pairs={{0,64},{64,0},{1,65},{65,1},{2,66},{66,2},{3,67},{67,3},{4,68},{68... | collective-permute-start | bytes 18874376 | tf_op jit(solution)/shard_map/ppermute | solution.py:440
  9.5 7.9 %collective-permute-start.1 = (f32[128,1536]{1,0:T(8,128)}, f32[128,1536]{1,0:T(8,128)S(1)}, u32[]{:S(2)}, u32[]{:S(2)}) collective-permute-start(f32[128,1536]{1,0:T(8,128)} %get-tuple-element.69), channel_id=1, source_target_pairs={{0,64},{64,0},{1,65},{65,1},{2,66},{66,2},{3,67},{67,3},{4,68},{68... | collective-permute-start | bytes 2359304 | tf_op jit(solution)/shard_map/ppermute | solution.py:442
  10.1 31.9 %all-to-all-start = ((f32[16,16,1536]{2,1,0:T(8,128)}), f32[16,16,1536]{2,1,0:T(8,128)S(1)}, u32[]{:S(2)}, u32[]{:S(2)}) async-start(f32[16,16,1536]{2,1,0:T(8,128)} %get-tuple-element.76), calls=%async_computation | async-start | bytes 3145728 | tf_op jit(solution)/shard_map/all_to_all | solution.py:443
  42.0 3.5 %copy-start.8 = (f32[16,16,1536]{2,1,0:T(8,128)}, f32[16,16,1536]{2,1,0:T(8,128)S(1)}, u32[]{:S(2)}) copy-start(f32[16,16,1536]{2,1,0:T(8,128)S(1)} %all-to-all-done.own) | copy-start | bytes 4718596
  42.0 3.5 %collective-permute-start.5 = (f32[16,16,1536]{2,1,0:T(8,128)S(1)}, f32[16,16,1536]{2,1,0:T(8,128)}, u32[]{:S(2)}, u32[]{:S(2)}) collective-permute-start(f32[16,16,1536]{2,1,0:T(8,128)S(1)} %all-to-all-done.own), channel_id=1, source_target_pairs={{0,64},{64,0},{1,65},{65,1},{2,66},{66,2},{3,67},{67,3},{4,68},{68... | collective-permute-start | bytes 4718600 | tf_op jit(solution)/shard_map/ppermute | solution.py:453
  42.0 12.5 %collective-permute-start.4 = (f32[2,16,16,384]{3,2,1,0:T(8,128)}, f32[2,16,16,384]{3,2,1,0:T(8,128)S(1)}, u32[]{:S(2)}, u32[]{:S(2)}) collective-permute-start(f32[2,16,16,384]{3,2,1,0:T(8,128)} %get-tuple-element.82), channel_id=1, source_target_pairs={{0,1},{1,0},{2,3},{3,2},{4,5},{5,4},{6,7},{7,6},{8,9},{9,8},{10,11... | collective-permute-start | bytes 2359304 | tf_op jit(solution)/shard_map/ppermute | solution.py:49
  43.9 16.4 %collective-permute-start.2 = (f32[2,4,96,384]{3,2,1,0:T(8,128)}, f32[2,4,96,384]{3,2,1,0:T(8,128)S(1)}, u32[]{:S(2)}, u32[]{:S(2)}) collective-permute-start(f32[2,4,96,384]{3,2,1,0:T(8,128)} %get-tuple-element.80), channel_id=1, source_target_pairs={{0,4},{1,5},{2,6},{3,7},{4,0},{5,1},{6,2},{7,3},{8,12},{9,13},{10,... | collective-permute-start | bytes 3538952 | tf_op jit(solution)/shard_map/ppermute | solution.py:49
  43.9 16.4 %collective-permute-start.3 = (f32[2,4,96,384]{3,2,1,0:T(8,128)}, f32[2,4,96,384]{3,2,1,0:T(8,128)S(1)}, u32[]{:S(2)}, u32[]{:S(2)}) collective-permute-start(f32[2,4,96,384]{3,2,1,0:T(8,128)} %get-tuple-element.81), channel_id=1, source_target_pairs={{0,16},{1,17},{2,18},{3,19},{4,20},{5,21},{6,22},{7,23},{8,24},{9,... | collective-permute-start | bytes 3538952 | tf_op jit(solution)/shard_map/ppermute | solution.py:49
  52.0 16.8 %collective-permute-start.6 = (f32[2,4,64,384]{3,2,1,0:T(8,128)}, f32[2,4,64,384]{3,2,1,0:T(8,128)S(1)}, u32[]{:S(2)}, u32[]{:S(2)}) collective-permute-start(f32[2,4,64,384]{3,2,1,0:T(8,128)} %get-tuple-element.87), channel_id=1, source_target_pairs={{0,4},{1,5},{2,6},{3,7},{4,0},{5,1},{6,2},{7,3},{8,12},{9,13},{10,... | collective-permute-start | bytes 2359304 | tf_op jit(solution)/shard_map/ppermute | solution.py:49
  52.5 16.2 %collective-permute-start.7 = (f32[2,4,64,384]{3,2,1,0:T(8,128)}, f32[2,4,64,384]{3,2,1,0:T(8,128)S(1)}, u32[]{:S(2)}, u32[]{:S(2)}) collective-permute-start(f32[2,4,64,384]{3,2,1,0:T(8,128)} %get-tuple-element.88), channel_id=1, source_target_pairs={{0,16},{1,17},{2,18},{3,19},{4,20},{5,21},{6,22},{7,23},{8,24},{9,... | collective-permute-start | bytes 2359304 | tf_op jit(solution)/shard_map/ppermute | solution.py:49
  54.5 5.8 %copy-start.2 = (f32[2,16,16,384]{3,2,1,0:T(8,128)}, f32[2,16,16,384]{3,2,1,0:T(8,128)S(1)}, u32[]{:S(2)}) copy-start(f32[2,16,16,384]{3,2,1,0:T(8,128)S(1)} %collective-permute-done.4.refs_5_) | copy-start | bytes 2359300
  54.5 14.3 %collective-permute-start.8 = (f32[2,16,16,384]{3,2,1,0:T(8,128)}, f32[2,16,16,384]{3,2,1,0:T(8,128)S(1)}, u32[]{:S(2)}, u32[]{:S(2)}) collective-permute-start(f32[2,16,16,384]{3,2,1,0:T(8,128)} %get-tuple-element.89), channel_id=1, source_target_pairs={{0,1},{1,0},{2,3},{3,2},{4,5},{5,4},{6,7},{7,6},{8,9},{9,8},{10,11... | collective-permute-start | bytes 2359304 | tf_op jit(solution)/shard_map/ppermute | solution.py:49
  72.8 15.5 %collective-permute-start.10 = (f32[4,160,384]{2,1,0:T(8,128)}, f32[4,160,384]{2,1,0:T(8,128)S(1)}, u32[]{:S(2)}, u32[]{:S(2)}) collective-permute-start(f32[4,160,384]{2,1,0:T(8,128)} %get-tuple-element.110), channel_id=1, source_target_pairs={{0,12},{1,13},{2,14},{3,15},{4,8},{5,9},{6,10},{7,11},{8,4},{9,5},... | collective-permute-start | bytes 2949128 | tf_op jit(solution)/shard_map/ppermute | solution.py:49
  74.2 15.5 %collective-permute-start.11 = (f32[4,160,384]{2,1,0:T(8,128)}, f32[4,160,384]{2,1,0:T(8,128)S(1)}, u32[]{:S(2)}, u32[]{:S(2)}) collective-permute-start(f32[4,160,384]{2,1,0:T(8,128)} %get-tuple-element.112), channel_id=1, source_target_pairs={{0,48},{1,49},{2,50},{3,51},{4,52},{5,53},{6,54},{7,55},{8,56},{9,... | collective-permute-start | bytes 2949128 | tf_op jit(solution)/shard_map/ppermute | solution.py:49
  77.0 18.1 %collective-permute-start.9 = (f32[16,32,384]{2,1,0:T(8,128)}, f32[16,32,384]{2,1,0:T(8,128)S(1)}, u32[]{:S(2)}, u32[]{:S(2)}) collective-permute-start(f32[16,32,384]{2,1,0:T(8,128)} %get-tuple-element.96), channel_id=1, source_target_pairs={{0,3},{1,2},{2,1},{3,0},{4,7},{5,6},{6,5},{7,4},{8,11},{9,10},{10,... | collective-permute-start | bytes 2359304 | tf_op jit(solution)/shard_map/ppermute | solution.py:49
  94.2 10.9 %collective-permute-start.12 = (f32[2,160,384]{2,1,0:T(8,128)}, f32[2,160,384]{2,1,0:T(8,128)S(1)}, u32[]{:S(2)}, u32[]{:S(2)}) collective-permute-start(f32[2,160,384]{2,1,0:T(8,128)} %get-tuple-element.115), channel_id=1, source_target_pairs={{0,16},{1,17},{2,18},{3,19},{4,20},{5,21},{6,22},{7,23},{8,24},{9,... | collective-permute-start | bytes 1474568 | tf_op jit(solution)/shard_map/ppermute | solution.py:49
  94.5 10.7 %collective-permute-start.13 = (f32[2,160,384]{2,1,0:T(8,128)}, f32[2,160,384]{2,1,0:T(8,128)S(1)}, u32[]{:S(2)}, u32[]{:S(2)}) collective-permute-start(f32[2,160,384]{2,1,0:T(8,128)} %get-tuple-element.117), channel_id=1, source_target_pairs={{0,4},{1,5},{2,6},{3,7},{4,0},{5,1},{6,2},{7,3},{8,12},{9,13},{10,... | collective-permute-start | bytes 1474568 | tf_op jit(solution)/shard_map/ppermute | solution.py:49
  98.3 30.5 %all-to-all-start.1 = ((f32[16,32,384]{2,1,0:T(8,128)}), f32[16,32,384]{2,1,0:T(8,128)S(1)}, u32[]{:S(2)}, u32[]{:S(2)}) async-start(f32[16,32,384]{2,1,0:T(8,128)} %sum_last_third.1), calls=%async_computation.1 | async-start | bytes 1572864 | tf_op jit(solution)/shard_map/all_to_all | solution.py:473
  108.4 10.9 %collective-permute-start.14 = (f32[160,384]{1,0:T(8,128)}, f32[160,384]{1,0:T(8,128)S(1)}, u32[]{:S(2)}, u32[]{:S(2)}) collective-permute-start(f32[160,384]{1,0:T(8,128)} %get-tuple-element.118), channel_id=1, source_target_pairs={{0,48},{1,49},{2,50},{3,51},{4,52},{5,53},{6,54},{7,55},{8,56},{9,... | collective-permute-start | bytes 737288 | tf_op jit(solution)/shard_map/ppermute | solution.py:49
  111.6 8.1 %collective-permute-start.15 = (f32[160,384]{1,0:T(8,128)}, f32[160,384]{1,0:T(8,128)S(1)}, u32[]{:S(2)}, u32[]{:S(2)}) collective-permute-start(f32[160,384]{1,0:T(8,128)} %get-tuple-element.119), channel_id=1, source_target_pairs={{0,12},{1,13},{2,14},{3,15},{4,8},{5,9},{6,10},{7,11},{8,4},{9,5},... | collective-permute-start | bytes 737288 | tf_op jit(solution)/shard_map/ppermute | solution.py:49
  123.2 7.6 %collective-permute-start.16 = (f32[64,384]{1,0:T(8,128)}, f32[64,384]{1,0:T(8,128)S(1)}, u32[]{:S(2)}, u32[]{:S(2)}) collective-permute-start(f32[64,384]{1,0:T(8,128)} %get-tuple-element.121), channel_id=1, source_target_pairs={{0,1},{1,2},{2,3},{3,0},{4,5},{5,6},{6,7},{7,4},{8,9},{9,10},{10,1... | collective-permute-start | bytes 294920 | tf_op jit(solution)/shard_map/ppermute | solution.py:31
  123.2 8.6 %collective-permute-start.17 = (f32[64,384]{1,0:T(8,128)}, f32[64,384]{1,0:T(8,128)S(1)}, u32[]{:S(2)}, u32[]{:S(2)}) collective-permute-start(f32[64,384]{1,0:T(8,128)} %get-tuple-element.122), channel_id=1, source_target_pairs={{0,2},{1,3},{2,0},{3,1},{4,6},{5,7},{6,4},{7,5},{8,10},{9,11},{10,... | collective-permute-start | bytes 294920 | tf_op jit(solution)/shard_map/ppermute | solution.py:31
  126.9 4.9 %collective-permute-start.18 = (f32[64,384]{1,0:T(8,128)}, f32[64,384]{1,0:T(8,128)S(1)}, u32[]{:S(2)}, u32[]{:S(2)}) collective-permute-start(f32[64,384]{1,0:T(8,128)} %get-tuple-element.123), channel_id=1, source_target_pairs={{0,3},{1,0},{2,1},{3,2},{4,7},{5,4},{6,5},{7,6},{8,11},{9,8},{10,9... | collective-permute-start | bytes 294920 | tf_op jit(solution)/shard_map/ppermute | solution.py:31
  129.4 34.1 %copy-start.18 = (f32[64,384]{1,0:T(8,128)S(1)}, f32[64,384]{1,0:T(8,128)}, u32[]{:S(2)}) copy-start(f32[64,384]{1,0:T(8,128)} %get-tuple-element.132) | copy-start | bytes 294916
  134.4 15.8 %all-to-all-start.2 = ((f32[32,24,128]{2,1,0:T(8,128)}), f32[32,24,128]{2,1,0:T(8,128)S(1)}, u32[]{:S(2)}, u32[]{:S(2)}) async-start(f32[32,24,128]{2,1,0:T(8,128)} %get-tuple-element.126), calls=%async_computation.2 | async-start | bytes 786432 | tf_op jit(solution)/shard_map/all_to_all | solution.py:492
  139.7 1.5 collective-permute-start.19
  141.3 9.0 %copy-start.22 = (f32[8,16,128]{2,1,0:T(8,128)}, f32[8,16,128]{2,1,0:T(8,128)S(1)}, u32[]{:S(2)}) copy-start(f32[8,16,128]{2,1,0:T(8,128)S(1)} %collective-permute-done.19.come) | copy-start | bytes 196612
  152.9 8.6 %collective-permute-start.20 = (f32[32,16,128]{2,1,0:T(8,128)}, f32[32,16,128]{2,1,0:T(8,128)S(1)}, u32[]{:S(2)}, u32[]{:S(2)}) collective-permute-start(f32[32,16,128]{2,1,0:T(8,128)} %select.7.q0), channel_id=1, source_target_pairs={{0,1},{1,0},{2,3},{3,2},{4,5},{5,4},{6,7},{7,6},{8,9},{9,8},{10,11... | collective-permute-start | bytes 786440 | tf_op jit(solution)/shard_map/ppermute | solution.py:49
  153.9 10.4 %collective-permute-start.21 = (f32[32,16,128]{2,1,0:T(8,128)}, f32[32,16,128]{2,1,0:T(8,128)S(1)}, u32[]{:S(2)}, u32[]{:S(2)}) collective-permute-start(f32[32,16,128]{2,1,0:T(8,128)} %select.7.q0), channel_id=1, source_target_pairs={{0,3},{1,2},{2,1},{3,0},{4,7},{5,6},{6,5},{7,4},{8,11},{9,10},{10,... | collective-permute-start | bytes 786440 | tf_op jit(solution)/shard_map/ppermute | solution.py:49
  161.5 7.6 %copy-start.13 = (f32[32,16,128]{2,1,0:T(8,128)}, f32[32,16,128]{2,1,0:T(8,128)S(1)}, u32[]{:S(2)}) copy-start(f32[32,16,128]{2,1,0:T(8,128)S(1)} %collective-permute-done.20.q1) | copy-start | bytes 786436
  161.5 7.6 %collective-permute-start.22 = (f32[32,16,128]{2,1,0:T(8,128)S(1)}, f32[32,16,128]{2,1,0:T(8,128)S(1)}, u32[]{:S(2)}, u32[]{:S(2)}) collective-permute-start(f32[32,16,128]{2,1,0:T(8,128)S(1)} %collective-permute-done.20.q1), channel_id=1, source_target_pairs={{0,3},{1,2},{2,1},{3,0},{4,7},{5,6},{6,5},{7,4},{8,11},{9,10},{10,... | collective-permute-start | bytes 786440 | tf_op jit(solution)/shard_map/ppermute | solution.py:49
  164.3 4.9 %copy-start.14 = (f32[32,16,128]{2,1,0:T(8,128)}, f32[32,16,128]{2,1,0:T(8,128)S(1)}, u32[]{:S(2)}) copy-start(f32[32,16,128]{2,1,0:T(8,128)S(1)} %collective-permute-done.21.q2) | copy-start | bytes 786436
  (18 other events, 16.5 us)

commit v6 on v5

--- a/solution.py
+++ b/solution.py
@@ -171,6 +171,11 @@
 
     for k in range(12):
         load(k).start()
+    for k in range(12):
+        load(k).wait()
+        for s in (2 * k, 2 * k + 1):
+            rows, cols = slice(s // 12 * 1024, s // 12 * 1024 + 1024), slice(s % 12 * 128, s % 12 * 128 + 128)
+            high[rows, cols], low[rows, cols] = split(land[s])
     y_high, y_low = split(y_basis[...].T)
     for s in range(12):
         cols = slice(s * 128, s * 128 + 128)
@@ -178,11 +183,6 @@
         core[:, cols] = dot3(y_high, y_low, r_high, r_low, ((1,), (1,)))
     for copy in core_copies(place, core, refs, core_sems):
         copy.start()
-    for k in range(12):
-        load(k).wait()
-        for s in (2 * k, 2 * k + 1):
-            rows, cols = slice(s // 12 * 1024, s // 12 * 1024 + 1024), slice(s % 12 * 128, s % 12 * 128 + 128)
-            high[rows, cols], low[rows, cols] = split(land[s])
     for b in range(4):
         rows, cols = slice(b * 256, b * 256 + 256), slice(b * 256, b * 256 + 1280)
         buf[b] = dot3(high[rows, :], low[rows, :], high[cols, :], low[cols, :], ((1,), (1,)))
@@ -449,9 +449,9 @@
         gram_x_kernel, "gram_x", 96, place, (species_field, other_field, mine, theirs, y_mode_basis),
         (pl.ANY, pl.ANY, pltpu.VMEM, pltpu.VMEM, pltpu.VMEM), GRAM_X_SCRATCH, 12000000000,
     )
-    px, fibers = lax.optimization_barrier((px, fibers))
+    came_x = first_swaps(px)
+    _, fibers = lax.optimization_barrier((px, fibers))
     other_fibers = lax.ppermute(fibers, "gx", SWAP)
-    came_x = first_swaps(px)
     py = gram_pieces(
         gram_y_kernel, "gram_y", 64, place, (fibers, other_fibers), (pltpu.VMEM, pltpu.VMEM), GRAM_Y_SCRATCH, 2400000000
     )
@@ -495,7 +495,7 @@
         select_kernel, "select", jax.ShapeDtypeStruct((32, 16, 128), F32), [], place, got, direct_x, keep, come
     )
     first = swap_z(part, 0)
-    quarters = [part, first, swap_z(part, 1), swap_z(first, 1)]
+    quarters = [part, first, swap_z(part, 1), shift_z(part, 2)]
     gram_x, gram_y = small_kernel(
         functools.partial(assemble_kernel, 1.0 / (ny * slices), 1.0 / (ranks * slices)),
         "assemble",

time: 173 us -> 173 us (level)
  starting transfers between devices: 51.2 us -> 49.3 us
    ppermute x16 -> x15, waiting for transfers between devices: 29.8 us -> 22.9 us  [swap(): return lax.ppermute(v, ('gx', 'gy', 'gz'), pairs)]
    ppermute x3 -> x4, waiting for transfers between devices: 2.32 us -> 8.72 us  [step(): return lax.ppermute(v, ('gx', 'gy', 'gz'), pairs)]
    ppermute x16 -> x15, starting transfers between devices: 25.2 us -> 21.4 us  [swap(): return lax.ppermute(v, ('gx', 'gy', 'gz'), pairs)]
    ppermute x3 -> x4, starting transfers between devices: 5.64 us -> 7.68 us  [step(): return lax.ppermute(v, ('gx', 'gy', 'gz'), pairs)]
  transfers between devices with their start and end apart: 26 -> 26, of which waited for: 14 -> 15; matrix products, arithmetic and copies ran while one was open for 1% -> 1% of each run, Pallas kernels for 31% -> 31%
where the time goes in v6:
time: 173 us; the launch traced here: 172 us
  Pallas kernels  62.5 us (36%)
  starting transfers between devices  49.3 us (28%)
  waiting for transfers between devices  46.1 us (27%)
  local copies, waits for them, and re-layouts  12.4 us (7%)
    pallas_call x2, Pallas kernels, gram_pieces(): pl.pallas_call(kernel, in_specs=[pl.BlockSpec(memory_space=space) for spa...  27.1 us
    ppermute x15, waiting for transfers between devices, swap(): return lax.ppermute(v, ('gx', 'gy', 'gz'), pairs)  22.9 us
    ppermute x15, starting transfers between devices, swap(): return lax.ppermute(v, ('gx', 'gy', 'gz'), pairs)  21.4 us
    pallas_call x7, Pallas kernels, small_kernel(): pl.pallas_call(kernel, in_specs=[pl.BlockSpec(memory_space=pltpu.SMEM)] +...  17.3 us
    unnamed x48, local copies, waits for them, and re-layouts  11.1 us
    all_to_all x1, waiting for transfers between devices, per_device(): got = lax.all_to_all(slots, ('gx', 'gy'), 0, 0, tiled=True)  8.98 us
    ppermute x4, waiting for transfers between devices, step(): return lax.ppermute(v, ('gx', 'gy', 'gz'), pairs)  8.72 us
    pallas_call x1, Pallas kernels, project(): pl.pallas_call(project_kernel, in_specs=[pl.BlockSpec(memory_space=pltpu....  8.16 us
  transfers between devices with their start and end apart: 26, of which 15 were waited for; matrix products, arithmetic and copies ran while one was open for 1% of the time, Pallas kernels for 31%

profile of v6, /device:TPU:0, one launch (start us, length us, event | category | flops | bytes accessed | tf_op | source)
XLA Modules:
  0.0 171.8 jit_solution(14275516753424799582)
XLA Ops:
  1.4 8.2 %project.1 = (f32[128,1536]{1,0:T(8,128)}, f32[128,1536]{1,0:T(8,128)}, f32[16,16,1536]{2,1,0:T(8,128)}) custom-call(s32[5]{0:T(128)} %stack.23.place, f32[12,1024,128]{2,1,0:T(8,128)} %own.1, f32[1024,256]{1,0:T(8,128)} %basis.1), custom_call_target="tpu_custom_call" | custom-call | flops 2400000000 | bytes 9000000 | tf_op jit(solution)/shard_map/project/pallas_call | solution.py:103
  10.1 7.1 %all-to-all-start = ((f32[16,16,1536]{2,1,0:T(8,128)}), f32[16,16,1536]{2,1,0:T(8,128)S(1)}, u32[]{:S(2)}, u32[]{:S(2)}) async-start(f32[16,16,1536]{2,1,0:T(8,128)} %get-tuple-element.70), calls=%async_computation | async-start | bytes 3145728 | tf_op jit(solution)/shard_map/all_to_all | solution.py:443
  18.1 20.7 %gram_x.1 = (f32[2,4,96,384]{3,2,1,0:T(8,128)}, f32[2,4,96,384]{3,2,1,0:T(8,128)}, f32[2,4,96,384]{3,2,1,0:T(8,128)}, f32[2,4,96,384]{3,2,1,0:T(8,128)}, f32[2,1...) custom-call(s32[5]{0:T(128)} %stack.23.place, f32[12,1024,128]{2,1,0:T(8,128)} %own.1, ...), custom_call_target="tpu_custom_call" | custom-call | flops 12000000000 | bytes 20000000 | tf_op jit(solution)/shard_map/gram_x/pallas_call | solution.py:224
  38.8 3.2 %all-to-all-done.own = f32[16,16,1536]{2,1,0:T(8,128)S(1)} async-done(((f32[16,16,1536]{2,1,0:T(8,128)}), f32[16,16,1536]{2,1,0:T(8,128)S(1)}, u32[]{:S(2)}, u32[]{:S(2)}) %all-to-all-start) | async-done | bytes 1572896 | tf_op jit(solution)/shard_map/all_to_all | solution.py:443
  42.0 1.9 %collective-permute-start.4 = (f32[2,16,16,384]{3,2,1,0:T(8,128)}, f32[2,16,16,384]{3,2,1,0:T(8,128)S(1)}, u32[]{:S(2)}, u32[]{:S(2)}) collective-permute-start(f32[2,16,16,384]{3,2,1,0:T(8,128)} %get-tuple-element.69), channel_id=1, source_target_pairs={{0,1},{1,0},{2,3},{3,2},{4,5},{5,4},{6,7},{7,6},{8,9},{9,8},{10,11... | collective-permute-start | bytes 2359304 | tf_op jit(solution)/shard_map/ppermute | solution.py:49
  45.5 6.4 %gram_y.1 = (f32[2,4,64,384]{3,2,1,0:T(8,128)}, f32[2,4,64,384]{3,2,1,0:T(8,128)}, f32[2,4,64,384]{3,2,1,0:T(8,128)}, f32[2,4,64,384]{3,2,1,0:T(8,128)}, f32[2,1...) custom-call(s32[5]{0:T(128)} %stack.23.place, f32[16,16,1536]{2,1,0:T(8,128)} %copy-done.8, ...), custom_call_target="tpu_custom_call" | custom-call | flops 2400000000 | bytes 20000000 | tf_op jit(solution)/shard_map/gram_y/pallas_call | solution.py:224
  52.5 2.0 %collective-permute-start.7 = (f32[2,4,64,384]{3,2,1,0:T(8,128)}, f32[2,4,64,384]{3,2,1,0:T(8,128)S(1)}, u32[]{:S(2)}, u32[]{:S(2)}) collective-permute-start(f32[2,4,64,384]{3,2,1,0:T(8,128)} %get-tuple-element.76), channel_id=1, source_target_pairs={{0,16},{1,17},{2,18},{3,19},{4,20},{5,21},{6,22},{7,23},{8,24},{9,... | collective-permute-start | bytes 2359304 | tf_op jit(solution)/shard_map/ppermute | solution.py:49
  56.1 4.2 %collective-permute-done.2.refs_3_ = f32[2,4,96,384]{3,2,1,0:T(8,128)S(1)} collective-permute-done((f32[2,4,96,384]{3,2,1,0:T(8,128)}, f32[2,4,96,384]{3,2,1,0:T(8,128)S(1)}, u32[]{:S(2)}, u32[]{:S(2)}) %collective-permute-start.2) | collective-permute-done | bytes 1179680 | tf_op jit(solution)/shard_map/ppermute | solution.py:49
  62.4 3.2 %add_x.1 = (f32[4,160,384]{2,1,0:T(8,128)}, f32[4,160,384]{2,1,0:T(8,128)}, f32[16,32,384]{2,1,0:T(8,128)}) custom-call(f32[2,4,96,384]{3,2,1,0:T(8,128)} %get-tuple-element.85.refs_0_, f32[2,4,96,384]{3,2,1,0:T(8,128)} %get-tuple-element.86.refs_1_, f32[2,16,16,384]{3,2,1,0:T(8,128)} %get-tuple-element.87.refs_2_, f32[2,4,96,384]{3,2,1,0:T(8,128)} %copy-done, ...), custom_call_target="tpu_custom_call" | custom-call | flops 400000 | bytes 5000000 | tf_op jit(solution)/shard_map/add_x/pallas_call | solution.py:272
  65.5 3.3 %collective-permute-done.6.refs_3_.refs_9_ = f32[2,4,64,384]{3,2,1,0:T(8,128)S(1)} collective-permute-done((f32[2,4,64,384]{3,2,1,0:T(8,128)}, f32[2,4,64,384]{3,2,1,0:T(8,128)S(1)}, u32[]{:S(2)}, u32[]{:S(2)}) %collective-permute-start.6) | collective-permute-done | bytes 786464 | tf_op jit(solution)/shard_map/ppermute | solution.py:49
  70.2 2.7 %add_y.1 = (f32[4,160,384]{2,1,0:T(8,128)}, f32[4,160,384]{2,1,0:T(8,128)}, f32[16,32,384]{2,1,0:T(8,128)}) custom-call(f32[2,4,64,384]{3,2,1,0:T(8,128)} %get-tuple-element.91.refs_0_.refs_6_, f32[2,4,64,384]{3,2,1,0:T(8,128)} %get-tuple-element.92.refs_1_.refs_7_, ...), custom_call_target="tpu_custom_call", output_to_operand_aliasing={{0}: (6, {}), {1}: (7, {}), {2}: (8, {})} | custom-call | flops 300000 | bytes 4000000 | tf_op jit(solution)/shard_map/add_y/pallas_call | solution.py:296
  73.7 2.8 %collective-permute-start.11 = (f32[4,160,384]{2,1,0:T(8,128)}, f32[4,160,384]{2,1,0:T(8,128)S(1)}, u32[]{:S(2)}, u32[]{:S(2)}) collective-permute-start(f32[4,160,384]{2,1,0:T(8,128)} %get-tuple-element.100), channel_id=1, source_target_pairs={{0,48},{1,49},{2,50},{3,51},{4,52},{5,53},{6,54},{7,55},{8,56},{9,... | collective-permute-start | bytes 2949128 | tf_op jit(solution)/shard_map/ppermute | solution.py:49
  76.5 2.5 %collective-permute-start.9 = (f32[16,32,384]{2,1,0:T(8,128)}, f32[16,32,384]{2,1,0:T(8,128)S(1)}, u32[]{:S(2)}, u32[]{:S(2)}) collective-permute-start(f32[16,32,384]{2,1,0:T(8,128)} %get-tuple-element.84), channel_id=1, source_target_pairs={{0,3},{1,2},{2,1},{3,0},{4,7},{5,6},{6,5},{7,4},{8,11},{9,10},{10,... | collective-permute-start | bytes 2359304 | tf_op jit(solution)/shard_map/ppermute | solution.py:49
  79.0 4.2 %add_own.1 = (f32[4,160,384]{2,1,0:T(8,128)}, f32[4,160,384]{2,1,0:T(8,128)}, f32[16,32,384]{2,1,0:T(8,128)}) custom-call(f32[2,4,96,384]{3,2,1,0:T(8,128)} %get-tuple-element.85.refs_0_, f32[2,4,96,384]{3,2,1,0:T(8,128)} %get-tuple-element.86.refs_1_, f32[2,16,16,384]{3,2,1,0:T(8,128)} %get-tuple-element.87.refs_2_, f32[2,4,96,384]{3,2,1,0:T(8,128)} %copy-done, ...), custom_call_target="tpu_custom_call" | custom-call | flops 700000 | bytes 9000000 | tf_op jit(solution)/shard_map/add_own/pallas_call | solution.py:317
  83.2 5.1 %collective-permute-done.10.last_a = f32[4,160,384]{2,1,0:T(8,128)S(1)} collective-permute-done((f32[4,160,384]{2,1,0:T(8,128)}, f32[4,160,384]{2,1,0:T(8,128)S(1)}, u32[]{:S(2)}, u32[]{:S(2)}) %collective-permute-start.10) | collective-permute-done | bytes 983072 | tf_op jit(solution)/shard_map/ppermute | solution.py:49
  90.2 3.6 %sum_first.1 = (f32[2,160,384]{2,1,0:T(8,128)}, f32[2,160,384]{2,1,0:T(8,128)}, f32[2,160,384]{2,1,0:T(8,128)}, f32[2,160,384]{2,1,0:T(8,128)}) custom-call(s32[5]{0:T(128)} %stack.23.place, f32[4,160,384]{2,1,0:T(8,128)} %get-tuple-element.97.own_a, f32[4,160,384]{2,1,0:T(8,128)} %copy-done.10, f32[4,160,384]{2,1,0:T(8,128)} %get-tuple-element.99.own_b, ...), custom_call_target="tpu_custom_call" | custom-call | tf_op jit(solution)/shard_map/sum_first/pallas_call | solution.py:421
  95.6 2.4 %sum_last_third.1 = f32[16,32,384]{2,1,0:T(8,128)} custom-call(s32[5]{0:T(128)} %stack.23.place, f32[16,32,384]{2,1,0:T(8,128)} %get-tuple-element.112.first, f32[16,32,384]{2,1,0:T(8,128)} %copy-done.12), custom_call_target="tpu_custom_call" | custom-call | tf_op jit(solution)/shard_map/sum_last_third/pallas_call | solution.py:421
  98.0 6.7 %all-to-all-start.1 = ((f32[16,32,384]{2,1,0:T(8,128)}), f32[16,32,384]{2,1,0:T(8,128)S(1)}, u32[]{:S(2)}, u32[]{:S(2)}) async-start(f32[16,32,384]{2,1,0:T(8,128)} %sum_last_third.1), calls=%async_computation.1 | async-start | bytes 1572864 | tf_op jit(solution)/shard_map/all_to_all | solution.py:473
  105.7 2.3 %add_second.1 = (f32[160,384]{1,0:T(8,128)}, f32[160,384]{1,0:T(8,128)}) custom-call(s32[5]{0:T(128)} %stack.23.place, f32[2,160,384]{2,1,0:T(8,128)} %get-tuple-element.102.k_a.refs_0_, f32[2,160,384]{2,1,0:T(8,128)} %copy-done.6, f32[2,160,384]{2,1,0:T(8,128)} %get-tuple-element.104.k_b.refs_3_, f32[2,160,384]{2,1,0:T(8,128)} %copy-done.7), custom_call_target="tpu_custom_call" | custom-call | tf_op jit(solution)/shard_map/add_second/pallas_call | solution.py:421
  108.0 3.1 %collective-permute-start.14 = (f32[160,384]{1,0:T(8,128)}, f32[160,384]{1,0:T(8,128)S(1)}, u32[]{:S(2)}, u32[]{:S(2)}) collective-permute-start(f32[160,384]{1,0:T(8,128)} %get-tuple-element.106), channel_id=1, source_target_pairs={{0,48},{1,49},{2,50},{3,51},{4,52},{5,53},{6,54},{7,55},{8,56},{9,... | collective-permute-start | bytes 737288 | tf_op jit(solution)/shard_map/ppermute | solution.py:49
  111.1 2.7 %collective-permute-start.15 = (f32[160,384]{1,0:T(8,128)}, f32[160,384]{1,0:T(8,128)S(1)}, u32[]{:S(2)}, u32[]{:S(2)}) collective-permute-start(f32[160,384]{1,0:T(8,128)} %get-tuple-element.107), channel_id=1, source_target_pairs={{0,12},{1,13},{2,14},{3,15},{4,8},{5,9},{6,10},{7,11},{8,4},{9,5},... | collective-permute-start | bytes 737288 | tf_op jit(solution)/shard_map/ppermute | solution.py:49
  113.8 5.3 %collective-permute-done.14.refs_2_ = f32[160,384]{1,0:T(8,128)S(1)} collective-permute-done((f32[160,384]{1,0:T(8,128)}, f32[160,384]{1,0:T(8,128)S(1)}, u32[]{:S(2)}, u32[]{:S(2)}) %collective-permute-start.14) | collective-permute-done | bytes 245792 | tf_op jit(solution)/shard_map/ppermute | solution.py:49
  120.5 2.4 %sum_second.1 = (f32[64,384]{1,0:T(8,128)}, f32[64,384]{1,0:T(8,128)}, f32[64,384]{1,0:T(8,128)}, f32[64,384]{1,0:T(8,128)}, f32[64,384]{1,0:T(8,128)}) custom-call(s32[5]{0:T(128)} %stack.23.place, f32[2,160,384]{2,1,0:T(8,128)} %get-tuple-element.102.k_a.refs_0_, f32[2,160,384]{2,1,0:T(8,128)} %copy-done.6, f32[160,384]{1,0:T(8,128)} %copy-done.16, ...), custom_call_target="tpu_custom_call" | custom-call | tf_op jit(solution)/shard_map/sum_second/pallas_call | solution.py:421
  123.0 3.4 %collective-permute-start.17 = (f32[64,384]{1,0:T(8,128)}, f32[64,384]{1,0:T(8,128)S(1)}, u32[]{:S(2)}, u32[]{:S(2)}) collective-permute-start(f32[64,384]{1,0:T(8,128)} %get-tuple-element.110), channel_id=1, source_target_pairs={{0,2},{1,3},{2,0},{3,1},{4,6},{5,7},{6,4},{7,5},{8,10},{9,11},{10,... | collective-permute-start | bytes 294920 | tf_op jit(solution)/shard_map/ppermute | solution.py:31
  126.4 2.2 %collective-permute-start.18 = (f32[64,384]{1,0:T(8,128)}, f32[64,384]{1,0:T(8,128)S(1)}, u32[]{:S(2)}, u32[]{:S(2)}) collective-permute-start(f32[64,384]{1,0:T(8,128)} %get-tuple-element.111), channel_id=1, source_target_pairs={{0,3},{1,0},{2,1},{3,2},{4,7},{5,4},{6,5},{7,6},{8,11},{9,8},{10,9... | collective-permute-start | bytes 294920 | tf_op jit(solution)/shard_map/ppermute | solution.py:31
  132.2 2.0 %sum_last.1 = (f32[32,24,128]{2,1,0:T(8,128)}, f32[16,16,128]{2,1,0:T(8,128)}, f32[8,16,128]{2,1,0:T(8,128)}, f32[8,16,128]{2,1,0:T(8,128)}) custom-call(s32[5]{0:T(128)} %stack.23.place, f32[64,384]{1,0:T(8,128)} %get-tuple-element.108.refs_0_, f32[64,384]{1,0:T(8,128)} %copy-done.19, f32[64,384]{1,0:T(8,128)} %copy-done.20, f32[64,384]{1,0:T(8,128)} %copy-done.21, ...), custom_call_target="tpu_custom_call" | custom-call | tf_op jit(solution)/shard_map/sum_last/pallas_call | solution.py:421
  134.2 5.4 %all-to-all-start.2 = ((f32[32,24,128]{2,1,0:T(8,128)}), f32[32,24,128]{2,1,0:T(8,128)S(1)}, u32[]{:S(2)}, u32[]{:S(2)}) async-start(f32[32,24,128]{2,1,0:T(8,128)} %get-tuple-element.114), calls=%async_computation.2 | async-start | bytes 786432 | tf_op jit(solution)/shard_map/all_to_all | solution.py:492
  141.1 9.0 %all-to-all-done.2.got = f32[32,24,128]{2,1,0:T(8,128)S(1)} async-done(((f32[32,24,128]{2,1,0:T(8,128)}), f32[32,24,128]{2,1,0:T(8,128)S(1)}, u32[]{:S(2)}, u32[]{:S(2)}) %all-to-all-start.2) | async-done | bytes 393248 | tf_op jit(solution)/shard_map/all_to_all | solution.py:492
  152.8 2.0 %collective-permute-start.22 = (f32[32,16,128]{2,1,0:T(8,128)}, f32[32,16,128]{2,1,0:T(8,128)S(1)}, u32[]{:S(2)}, u32[]{:S(2)}) collective-permute-start(f32[32,16,128]{2,1,0:T(8,128)} %select.7.q0), channel_id=1, source_target_pairs={{0,2},{1,3},{2,0},{3,1},{4,6},{5,7},{6,4},{7,5},{8,10},{9,11},{10,... | collective-permute-start | bytes 786440 | tf_op jit(solution)/shard_map/ppermute | solution.py:31
  157.3 6.5 %collective-permute-done.22.q3 = f32[32,16,128]{2,1,0:T(8,128)S(1)} collective-permute-done((f32[32,16,128]{2,1,0:T(8,128)}, f32[32,16,128]{2,1,0:T(8,128)S(1)}, u32[]{:S(2)}, u32[]{:S(2)}) %collective-permute-start.22) | collective-permute-done | bytes 262176 | tf_op jit(solution)/shard_map/ppermute | solution.py:31
  163.7 3.9 %collective-permute-done.21.q2 = f32[32,16,128]{2,1,0:T(8,128)S(1)} collective-permute-done((f32[32,16,128]{2,1,0:T(8,128)}, f32[32,16,128]{2,1,0:T(8,128)S(1)}, u32[]{:S(2)}, u32[]{:S(2)}) %collective-permute-start.21) | collective-permute-done | bytes 262176 | tf_op jit(solution)/shard_map/ppermute | solution.py:49
  169.0 2.7 %assemble.1 = (f32[64,2048]{1,0:T(8,128)}, f32[128,1024]{1,0:T(8,128)}) custom-call(s32[5]{0:T(128)} %stack.23.place, f32[32,16,128]{2,1,0:T(8,128)} %select.7.q0, f32[32,16,128]{2,1,0:T(8,128)} %copy-done.15, f32[32,16,128]{2,1,0:T(8,128)} %copy-done.14, f32[32,16,128]{2,1,0:T(8,128)} %copy-done.13), custom_call_target="tpu_custom_call" | custom-call | tf_op jit(solution)/shard_map/assemble/pallas_call | solution.py:421
  (85 shorter events, 27.9 us)
Async XLA Ops:
  0.6 16.6 %collective-permute-start = (f32[12,1024,128]{2,1,0:T(8,128)}, f32[12,1024,128]{2,1,0:T(8,128)}, u32[]{:S(2)}, u32[]{:S(2)}) collective-permute-start(f32[12,1024,128]{2,1,0:T(8,128)} %own.1), channel_id=1, source_target_pairs={{0,64},{64,0},{1,65},{65,1},{2,66},{66,2},{3,67},{67,3},{4,68},{68... | collective-permute-start | bytes 18874376 | tf_op jit(solution)/shard_map/ppermute | solution.py:440
  9.5 7.7 %collective-permute-start.1 = (f32[128,1536]{1,0:T(8,128)}, f32[128,1536]{1,0:T(8,128)S(1)}, u32[]{:S(2)}, u32[]{:S(2)}) collective-permute-start(f32[128,1536]{1,0:T(8,128)} %get-tuple-element.63), channel_id=1, source_target_pairs={{0,64},{64,0},{1,65},{65,1},{2,66},{66,2},{3,67},{67,3},{4,68},{68... | collective-permute-start | bytes 2359304 | tf_op jit(solution)/shard_map/ppermute | solution.py:442
  10.1 31.9 %all-to-all-start = ((f32[16,16,1536]{2,1,0:T(8,128)}), f32[16,16,1536]{2,1,0:T(8,128)S(1)}, u32[]{:S(2)}, u32[]{:S(2)}) async-start(f32[16,16,1536]{2,1,0:T(8,128)} %get-tuple-element.70), calls=%async_computation | async-start | bytes 3145728 | tf_op jit(solution)/shard_map/all_to_all | solution.py:443
  42.0 3.5 %copy-start.8 = (f32[16,16,1536]{2,1,0:T(8,128)}, f32[16,16,1536]{2,1,0:T(8,128)S(1)}, u32[]{:S(2)}) copy-start(f32[16,16,1536]{2,1,0:T(8,128)S(1)} %all-to-all-done.own) | copy-start | bytes 4718596
  42.0 3.5 %collective-permute-start.5 = (f32[16,16,1536]{2,1,0:T(8,128)S(1)}, f32[16,16,1536]{2,1,0:T(8,128)}, u32[]{:S(2)}, u32[]{:S(2)}) collective-permute-start(f32[16,16,1536]{2,1,0:T(8,128)S(1)} %all-to-all-done.own), channel_id=1, source_target_pairs={{0,64},{64,0},{1,65},{65,1},{2,66},{66,2},{3,67},{67,3},{4,68},{68... | collective-permute-start | bytes 4718600 | tf_op jit(solution)/shard_map/ppermute | solution.py:454
  42.0 12.5 %collective-permute-start.4 = (f32[2,16,16,384]{3,2,1,0:T(8,128)}, f32[2,16,16,384]{3,2,1,0:T(8,128)S(1)}, u32[]{:S(2)}, u32[]{:S(2)}) collective-permute-start(f32[2,16,16,384]{3,2,1,0:T(8,128)} %get-tuple-element.69), channel_id=1, source_target_pairs={{0,1},{1,0},{2,3},{3,2},{4,5},{5,4},{6,7},{7,6},{8,9},{9,8},{10,11... | collective-permute-start | bytes 2359304 | tf_op jit(solution)/shard_map/ppermute | solution.py:49
  43.9 16.4 %collective-permute-start.2 = (f32[2,4,96,384]{3,2,1,0:T(8,128)}, f32[2,4,96,384]{3,2,1,0:T(8,128)S(1)}, u32[]{:S(2)}, u32[]{:S(2)}) collective-permute-start(f32[2,4,96,384]{3,2,1,0:T(8,128)} %get-tuple-element.67), channel_id=1, source_target_pairs={{0,4},{1,5},{2,6},{3,7},{4,0},{5,1},{6,2},{7,3},{8,12},{9,13},{10,... | collective-permute-start | bytes 3538952 | tf_op jit(solution)/shard_map/ppermute | solution.py:49
  43.9 16.4 %collective-permute-start.3 = (f32[2,4,96,384]{3,2,1,0:T(8,128)}, f32[2,4,96,384]{3,2,1,0:T(8,128)S(1)}, u32[]{:S(2)}, u32[]{:S(2)}) collective-permute-start(f32[2,4,96,384]{3,2,1,0:T(8,128)} %get-tuple-element.68), channel_id=1, source_target_pairs={{0,16},{1,17},{2,18},{3,19},{4,20},{5,21},{6,22},{7,23},{8,24},{9,... | collective-permute-start | bytes 3538952 | tf_op jit(solution)/shard_map/ppermute | solution.py:49
  52.0 16.8 %collective-permute-start.6 = (f32[2,4,64,384]{3,2,1,0:T(8,128)}, f32[2,4,64,384]{3,2,1,0:T(8,128)S(1)}, u32[]{:S(2)}, u32[]{:S(2)}) collective-permute-start(f32[2,4,64,384]{3,2,1,0:T(8,128)} %get-tuple-element.75), channel_id=1, source_target_pairs={{0,4},{1,5},{2,6},{3,7},{4,0},{5,1},{6,2},{7,3},{8,12},{9,13},{10,... | collective-permute-start | bytes 2359304 | tf_op jit(solution)/shard_map/ppermute | solution.py:49
  52.5 16.3 %collective-permute-start.7 = (f32[2,4,64,384]{3,2,1,0:T(8,128)}, f32[2,4,64,384]{3,2,1,0:T(8,128)S(1)}, u32[]{:S(2)}, u32[]{:S(2)}) collective-permute-start(f32[2,4,64,384]{3,2,1,0:T(8,128)} %get-tuple-element.76), channel_id=1, source_target_pairs={{0,16},{1,17},{2,18},{3,19},{4,20},{5,21},{6,22},{7,23},{8,24},{9,... | collective-permute-start | bytes 2359304 | tf_op jit(solution)/shard_map/ppermute | solution.py:49
  54.5 5.8 %copy-start.2 = (f32[2,16,16,384]{3,2,1,0:T(8,128)}, f32[2,16,16,384]{3,2,1,0:T(8,128)S(1)}, u32[]{:S(2)}) copy-start(f32[2,16,16,384]{3,2,1,0:T(8,128)S(1)} %collective-permute-done.4.refs_5_) | copy-start | bytes 2359300
  54.5 14.3 %collective-permute-start.8 = (f32[2,16,16,384]{3,2,1,0:T(8,128)}, f32[2,16,16,384]{3,2,1,0:T(8,128)S(1)}, u32[]{:S(2)}, u32[]{:S(2)}) collective-permute-start(f32[2,16,16,384]{3,2,1,0:T(8,128)} %get-tuple-element.77), channel_id=1, source_target_pairs={{0,1},{1,0},{2,3},{3,2},{4,5},{5,4},{6,7},{7,6},{8,9},{9,8},{10,11... | collective-permute-start | bytes 2359304 | tf_op jit(solution)/shard_map/ppermute | solution.py:49
  68.8 1.4 copy-start.5
  72.8 15.5 %collective-permute-start.10 = (f32[4,160,384]{2,1,0:T(8,128)}, f32[4,160,384]{2,1,0:T(8,128)S(1)}, u32[]{:S(2)}, u32[]{:S(2)}) collective-permute-start(f32[4,160,384]{2,1,0:T(8,128)} %get-tuple-element.98), channel_id=1, source_target_pairs={{0,12},{1,13},{2,14},{3,15},{4,8},{5,9},{6,10},{7,11},{8,4},{9,5},... | collective-permute-start | bytes 2949128 | tf_op jit(solution)/shard_map/ppermute | solution.py:49
  73.7 15.5 %collective-permute-start.11 = (f32[4,160,384]{2,1,0:T(8,128)}, f32[4,160,384]{2,1,0:T(8,128)S(1)}, u32[]{:S(2)}, u32[]{:S(2)}) collective-permute-start(f32[4,160,384]{2,1,0:T(8,128)} %get-tuple-element.100), channel_id=1, source_target_pairs={{0,48},{1,49},{2,50},{3,51},{4,52},{5,53},{6,54},{7,55},{8,56},{9,... | collective-permute-start | bytes 2949128 | tf_op jit(solution)/shard_map/ppermute | solution.py:49
  76.5 18.2 %collective-permute-start.9 = (f32[16,32,384]{2,1,0:T(8,128)}, f32[16,32,384]{2,1,0:T(8,128)S(1)}, u32[]{:S(2)}, u32[]{:S(2)}) collective-permute-start(f32[16,32,384]{2,1,0:T(8,128)} %get-tuple-element.84), channel_id=1, source_target_pairs={{0,3},{1,2},{2,1},{3,0},{4,7},{5,6},{6,5},{7,4},{8,11},{9,10},{10,... | collective-permute-start | bytes 2359304 | tf_op jit(solution)/shard_map/ppermute | solution.py:49
  93.8 10.9 %collective-permute-start.12 = (f32[2,160,384]{2,1,0:T(8,128)}, f32[2,160,384]{2,1,0:T(8,128)S(1)}, u32[]{:S(2)}, u32[]{:S(2)}) collective-permute-start(f32[2,160,384]{2,1,0:T(8,128)} %get-tuple-element.103), channel_id=1, source_target_pairs={{0,16},{1,17},{2,18},{3,19},{4,20},{5,21},{6,22},{7,23},{8,24},{9,... | collective-permute-start | bytes 1474568 | tf_op jit(solution)/shard_map/ppermute | solution.py:49
  94.0 10.7 %collective-permute-start.13 = (f32[2,160,384]{2,1,0:T(8,128)}, f32[2,160,384]{2,1,0:T(8,128)S(1)}, u32[]{:S(2)}, u32[]{:S(2)}) collective-permute-start(f32[2,160,384]{2,1,0:T(8,128)} %get-tuple-element.105), channel_id=1, source_target_pairs={{0,4},{1,5},{2,6},{3,7},{4,0},{5,1},{6,2},{7,3},{8,12},{9,13},{10,... | collective-permute-start | bytes 1474568 | tf_op jit(solution)/shard_map/ppermute | solution.py:49
  98.0 30.7 %all-to-all-start.1 = ((f32[16,32,384]{2,1,0:T(8,128)}), f32[16,32,384]{2,1,0:T(8,128)S(1)}, u32[]{:S(2)}, u32[]{:S(2)}) async-start(f32[16,32,384]{2,1,0:T(8,128)} %sum_last_third.1), calls=%async_computation.1 | async-start | bytes 1572864 | tf_op jit(solution)/shard_map/all_to_all | solution.py:473
  108.0 11.1 %collective-permute-start.14 = (f32[160,384]{1,0:T(8,128)}, f32[160,384]{1,0:T(8,128)S(1)}, u32[]{:S(2)}, u32[]{:S(2)}) collective-permute-start(f32[160,384]{1,0:T(8,128)} %get-tuple-element.106), channel_id=1, source_target_pairs={{0,48},{1,49},{2,50},{3,51},{4,52},{5,53},{6,54},{7,55},{8,56},{9,... | collective-permute-start | bytes 737288 | tf_op jit(solution)/shard_map/ppermute | solution.py:49
  111.1 8.1 %collective-permute-start.15 = (f32[160,384]{1,0:T(8,128)}, f32[160,384]{1,0:T(8,128)S(1)}, u32[]{:S(2)}, u32[]{:S(2)}) collective-permute-start(f32[160,384]{1,0:T(8,128)} %get-tuple-element.107), channel_id=1, source_target_pairs={{0,12},{1,13},{2,14},{3,15},{4,8},{5,9},{6,10},{7,11},{8,4},{9,5},... | collective-permute-start | bytes 737288 | tf_op jit(solution)/shard_map/ppermute | solution.py:49
  123.0 7.8 %collective-permute-start.16 = (f32[64,384]{1,0:T(8,128)}, f32[64,384]{1,0:T(8,128)S(1)}, u32[]{:S(2)}, u32[]{:S(2)}) collective-permute-start(f32[64,384]{1,0:T(8,128)} %get-tuple-element.109), channel_id=1, source_target_pairs={{0,1},{1,2},{2,3},{3,0},{4,5},{5,6},{6,7},{7,4},{8,9},{9,10},{10,1... | collective-permute-start | bytes 294920 | tf_op jit(solution)/shard_map/ppermute | solution.py:31
  123.0 8.5 %collective-permute-start.17 = (f32[64,384]{1,0:T(8,128)}, f32[64,384]{1,0:T(8,128)S(1)}, u32[]{:S(2)}, u32[]{:S(2)}) collective-permute-start(f32[64,384]{1,0:T(8,128)} %get-tuple-element.110), channel_id=1, source_target_pairs={{0,2},{1,3},{2,0},{3,1},{4,6},{5,7},{6,4},{7,5},{8,10},{9,11},{10,... | collective-permute-start | bytes 294920 | tf_op jit(solution)/shard_map/ppermute | solution.py:31
  126.4 5.1 %collective-permute-start.18 = (f32[64,384]{1,0:T(8,128)}, f32[64,384]{1,0:T(8,128)S(1)}, u32[]{:S(2)}, u32[]{:S(2)}) collective-permute-start(f32[64,384]{1,0:T(8,128)} %get-tuple-element.111), channel_id=1, source_target_pairs={{0,3},{1,0},{2,1},{3,2},{4,7},{5,4},{6,5},{7,6},{8,11},{9,8},{10,9... | collective-permute-start | bytes 294920 | tf_op jit(solution)/shard_map/ppermute | solution.py:31
  129.3 27.3 %copy-start.18 = (f32[64,384]{1,0:T(8,128)S(1)}, f32[64,384]{1,0:T(8,128)}, u32[]{:S(2)}) copy-start(f32[64,384]{1,0:T(8,128)} %get-tuple-element.120) | copy-start | bytes 294916
  134.2 15.9 %all-to-all-start.2 = ((f32[32,24,128]{2,1,0:T(8,128)}), f32[32,24,128]{2,1,0:T(8,128)S(1)}, u32[]{:S(2)}, u32[]{:S(2)}) async-start(f32[32,24,128]{2,1,0:T(8,128)} %get-tuple-element.114), calls=%async_computation.2 | async-start | bytes 786432 | tf_op jit(solution)/shard_map/all_to_all | solution.py:492
  139.6 1.5 collective-permute-start.19
  141.1 9.0 %copy-start.22 = (f32[8,16,128]{2,1,0:T(8,128)}, f32[8,16,128]{2,1,0:T(8,128)S(1)}, u32[]{:S(2)}) copy-start(f32[8,16,128]{2,1,0:T(8,128)S(1)} %collective-permute-done.19.come) | copy-start | bytes 196612
  152.8 11.0 %collective-permute-start.22 = (f32[32,16,128]{2,1,0:T(8,128)}, f32[32,16,128]{2,1,0:T(8,128)S(1)}, u32[]{:S(2)}, u32[]{:S(2)}) collective-permute-start(f32[32,16,128]{2,1,0:T(8,128)} %select.7.q0), channel_id=1, source_target_pairs={{0,2},{1,3},{2,0},{3,1},{4,6},{5,7},{6,4},{7,5},{8,10},{9,11},{10,... | collective-permute-start | bytes 786440 | tf_op jit(solution)/shard_map/ppermute | solution.py:31
  154.8 12.8 %collective-permute-start.21 = (f32[32,16,128]{2,1,0:T(8,128)}, f32[32,16,128]{2,1,0:T(8,128)S(1)}, u32[]{:S(2)}, u32[]{:S(2)}) collective-permute-start(f32[32,16,128]{2,1,0:T(8,128)} %select.7.q0), channel_id=1, source_target_pairs={{0,3},{1,2},{2,1},{3,0},{4,7},{5,6},{6,5},{7,4},{8,11},{9,10},{10,... | collective-permute-start | bytes 786440 | tf_op jit(solution)/shard_map/ppermute | solution.py:49
  156.6 11.1 %collective-permute-start.20 = (f32[32,16,128]{2,1,0:T(8,128)}, f32[32,16,128]{2,1,0:T(8,128)S(1)}, u32[]{:S(2)}, u32[]{:S(2)}) collective-permute-start(f32[32,16,128]{2,1,0:T(8,128)} %select.7.q0), channel_id=1, source_target_pairs={{0,1},{1,0},{2,3},{3,2},{4,5},{5,4},{6,7},{7,6},{8,9},{9,8},{10,11... | collective-permute-start | bytes 786440 | tf_op jit(solution)/shard_map/ppermute | solution.py:49
  163.7 4.0 %copy-start.13 = (f32[32,16,128]{2,1,0:T(8,128)}, f32[32,16,128]{2,1,0:T(8,128)S(1)}, u32[]{:S(2)}) copy-start(f32[32,16,128]{2,1,0:T(8,128)S(1)} %collective-permute-done.22.q3) | copy-start | bytes 786436
  (18 other events, 15.1 us)
